TPU v7x, 128 devices: a whole 4x4x4 slice. The times are simulated.
128 devices in a mesh: row: 8 (over y, core), col: 16 (over x, z).
Axes of the slice: x: 4, y: 4, z: 4, core: 2. Of those that a mesh axis runs over, the one named last changes fastest.
Arguments:
- features: bfloat16 [65536, 128], P(('col', 'row')), may hold values from -6 to 6
- weight: bfloat16 [128, 128], replicated, may hold values from -0.5 to 0.5
- adjacency: bfloat16 [8, 16, 512, 128, 128], P('row', 'col'), may hold values from -0.046875 to 0.046875
- row_index: int32 [8, 16, 512], P('row', 'col'), may hold values from 0 to 63
- col_index: int32 [8, 16, 512], P('row', 'col'), may hold values from 0 to 31
- block_count: int32 [8, 16], P('row', 'col'), may hold values from 170 to 512, as said below
- grad_out: bfloat16 [65536, 128], P(('row', 'col')), may hold values from -6 to 6
Outputs:
- activated: bfloat16 [65536, 128], P(('row', 'col'))
- input_grad: bfloat16 [65536, 128], P(('col', 'row'))
- weight_grad: float32 [128, 128], replicated
Inputs may be any that keep to these rules, and one draw needn't show every extreme that they name: `block_count`: slots at or beyond a position's count hold arbitrary values and indices and are ignored; some position holds exactly 512 live slots in every draw. `row_index`: several slots may name the same block; their values add.
All inputs are finite; a program needn't handle non-finite values.
Results may differ from a plain program's by a relative error of at most 0.0075.
Values may be sent and summed in bfloat16 or wider, within the bound.
No kernel may reach another device: no remote copies, remote signals or barrier semaphores. Data moves between devices by JAX's collectives and lax.ppermute only.
A program may use at most 192 MiB of HBM per device.

v0:
```python
import jax
import jax.numpy as jnp
from jax import lax
from jax.sharding import PartitionSpec as P


def pick_blocks(source, indices, nsource, side, width):
    selector = (indices[:, None] == jnp.arange(nsource, dtype=jnp.int32)[None, :]).astype(
        jnp.bfloat16
    )
    flat = source.reshape(nsource, side * width)
    picked = jnp.dot(selector, flat, preferred_element_type=jnp.float32).astype(jnp.bfloat16)
    return picked.reshape(indices.shape[0], side, width)


def add_blocks(values, indices, ntarget):
    targets = jnp.arange(ntarget, dtype=jnp.int32)
    selector = (targets[:, None] == indices[None, :]).astype(jnp.float32)
    flat = values.reshape(values.shape[0], values.shape[1] * values.shape[2])
    summed = jnp.dot(
        selector, flat, precision=lax.Precision.HIGHEST, preferred_element_type=jnp.float32
    )
    return summed.reshape(ntarget * values.shape[1], values.shape[2])


def local(features, weight, adjacency, row_index, col_index, block_count, grad_out):
    width = weight.shape[1]
    side = adjacency.shape[3]
    capacity = adjacency.shape[2]
    own_rows = features.shape[0]
    own_blocks = own_rows // side
    row_blocks = own_blocks * lax.axis_size("col")
    col_blocks = own_blocks * lax.axis_size("row")
    nodes_all = own_rows * lax.axis_size("row") * lax.axis_size("col")
    count = block_count[0, 0]
    alive = jnp.arange(capacity, dtype=jnp.int32) < count
    blocks = jnp.where(alive[:, None, None], adjacency[0, 0], jnp.zeros((), jnp.bfloat16))
    brows = row_index[0, 0]
    bcols = col_index[0, 0]
    hidden = jnp.dot(features, weight, preferred_element_type=jnp.float32).astype(jnp.bfloat16)
    gathered = lax.all_gather(hidden, "row", axis=0, tiled=True)
    picked = pick_blocks(gathered, bcols, col_blocks, side, width)
    products = jnp.einsum("kij,kjf->kif", blocks, picked, preferred_element_type=jnp.float32)
    partial_rows = add_blocks(products, brows, row_blocks)
    pre = lax.psum_scatter(partial_rows, "col", scatter_dimension=0, tiled=True)
    squash = jnp.tanh(pre)
    activated = squash.astype(jnp.bfloat16)
    slope = (grad_out.astype(jnp.float32) * (1.0 - squash * squash)).astype(jnp.bfloat16)
    slope_all = lax.all_gather(slope, "col", axis=0, tiled=True)
    chosen = pick_blocks(slope_all, brows, row_blocks, side, width)
    back = jnp.einsum("kij,kif->kjf", blocks, chosen, preferred_element_type=jnp.float32)
    partial_cols = add_blocks(back, bcols, col_blocks)
    hidden_grad = lax.psum_scatter(partial_cols, "row", scatter_dimension=0, tiled=True)
    hidden_grad_b = hidden_grad.astype(jnp.bfloat16)
    input_grad = jnp.dot(hidden_grad_b, weight.T, preferred_element_type=jnp.float32).astype(
        jnp.bfloat16
    )
    weight_term = jnp.einsum(
        "nf,ng->fg", features, hidden_grad_b, preferred_element_type=jnp.float32
    )
    weight_grad = lax.psum(weight_term, ("row", "col")) * nodes_all ** (-0.5)
    return (activated, input_grad, weight_grad)


def solution(mesh):
    placed = (
        P(("col", "row"), None),
        P(),
        P("row", "col", None, None, None),
        P("row", "col", None),
        P("row", "col", None),
        P("row", "col"),
        P(("row", "col"), None),
    )
    return jax.shard_map(
        local,
        mesh=mesh,
        in_specs=placed,
        out_specs=(P(("row", "col"), None), P(("col", "row"), None), P()),
        check_vma=False,
    )
```

profile of v0, /device:TPU:1, one launch (start us, length us, event | category | flops | bytes accessed | tf_op | source)
XLA Modules:
  0.0 511.1 jit_solution(3507408886576685427)
XLA Ops:
  7.2 0.0 copy-start
  7.2 0.0 all-gather.3.cloned.1.call-start
  7.2 0.8 copy-done
  8.1 1.6 convolution_convert_fusion.3
  9.7 0.0 all-gather.3.cloned.1.call-update
  9.7 0.0 reduce-scatter.3.cloned.1.call-start
  10.4 27.0 %all-gather.3.cloned.1.call-done = bf16[4096,128]{1,0:T(8,128)(2,1)} async-done(((bf16[512,128]{1,0:T(8,128)(2,1)}), bf16[4096,128]{1,0:T(8,128)(2,1)}) %all-gather.3.cloned.1.call-update) | async-done | bytes 1048592 | tf_op jit(solution)/shard_map/all_gather | solution.py:41
  37.3 1.5 reshape.38
  38.9 5.5 %fusion.6 = bf16[64,8,128,128]{3,1,2,0:T(8,128)(2,1)S(1)} fusion(bf16[32,16384]{1,0:T(8,128)(2,1)S(1)} %reshape.38, s32[512]{0:T(512)} %bitcast.36), kind=kOutput, calls=%fused_computation.9 | convolution fusion | flops 545275904 | bytes 17827840 | tf_op jit(solution)/shard_map/dot_general | solution.py:12
  44.4 8.4 %copy.13 = bf16[64,8,128,128]{3,2,1,0:T(8,128)(2,1)} copy(bf16[64,8,128,128]{3,1,2,0:T(8,128)(2,1)S(1)} %fusion.6) | data formatting | bytes 33554432
  52.7 0.0 copy-start.2
  52.7 24.4 %fusion.9 = f32[512,128,128]{2,1,0:T(8,128)} fusion(bf16[512,128,128]{2,1,0:T(8,128)(2,1)} %bitcast.35, bf16[1,1,512,128,128]{4,3,2,1,0:T(8,128)(2,1)} %param.9, pred[512]{0:T(512)(128)(4,1)S(1)} %iota_compare_fusion.8), kind=kOutput, calls=%fused_computation.12 | convolution fusion | flops 2155872256 | bytes 67109376 | tf_op jit(solution)/shard_map/kij,kjf->kif/dot_general | solution.py:43
  77.2 0.0 copy-done.2
  77.2 0.0 copy-start.3
  77.2 40.5 %fusion.3 = f32[64,16384]{1,0:T(8,128)} fusion(f32[64,8,128,128]{3,2,1,0:T(8,128)} %bitcast.32, s32[512]{0:T(512)S(1)} %bitcast.38), kind=kOutput, calls=%fused_computation.3 | convolution fusion | flops 6442483712 | bytes 37750784 | tf_op jit(solution)/shard_map/dot_general | solution.py:20
  117.7 4.9 reshape.41
  122.6 0.0 reduce-scatter.3.cloned.1.call-update
  122.6 0.0 all-gather.5.cloned.1.call-start
  122.6 75.7 %reduce-scatter.3.cloned.1.call-done = f32[512,128]{1,0:T(8,128)} async-done(((f32[8192,128]{1,0:T(8,128)}), f32[512,128]{1,0:T(8,128)}) %reduce-scatter.3.cloned.1.call-update) | async-done | bytes 262160 | tf_op jit(solution)/shard_map/reduce_scatter | solution.py:45
  198.3 0.0 copy-done.3
  198.3 1.7 multiply_convert_fusion
  200.0 0.0 all-gather.5.cloned.1.call-update
  200.0 0.0 reduce-scatter.5.cloned.1.call-start
  200.1 46.3 %all-gather.5.cloned.1.call-done = bf16[8192,128]{1,0:T(8,128)(2,1)} async-done(((bf16[512,128]{1,0:T(8,128)(2,1)}), bf16[8192,128]{1,0:T(8,128)(2,1)}) %all-gather.5.cloned.1.call-update) | async-done | bytes 2097168 | tf_op jit(solution)/shard_map/all_gather | solution.py:49
  246.3 2.8 reshape.42
  249.2 4.8 fusion.7
  254.0 8.4 %copy.15 = bf16[64,8,128,128]{3,2,1,0:T(8,128)(2,1)} copy(bf16[64,8,128,128]{3,1,2,0:T(8,128)(2,1)S(1)} %fusion.7) | data formatting | bytes 33554432
  262.3 0.0 copy-start.1
  262.3 25.3 %fusion.8 = f32[512,128,128]{2,1,0:T(8,128)} fusion(bf16[512,128,128]{2,1,0:T(8,128)(2,1)} %bitcast.34, bf16[1,1,512,128,128]{4,3,2,1,0:T(8,128)(2,1)} %param.9, pred[512]{0:T(512)(128)(4,1)S(1)} %iota_compare_fusion.8), kind=kOutput, calls=%fused_computation.11 | convolution fusion | flops 2155872256 | bytes 67109376 | tf_op jit(solution)/shard_map/kij,kif->kjf/dot_general | solution.py:51
  287.7 0.0 copy-done.1
  287.7 0.0 copy-start.4
  287.7 37.3 %fusion = f32[32,16384]{1,0:T(8,128)S(1)} fusion(f32[64,8,128,128]{3,2,1,0:T(8,128)} %bitcast.33, s32[512]{0:T(512)S(1)} %bitcast.37), kind=kOutput, calls=%fused_computation | convolution fusion | flops 3221241856 | bytes 35653632 | tf_op jit(solution)/shard_map/dot_general | solution.py:20
  324.9 1.5 reshape.45
  326.4 0.0 reduce-scatter.5.cloned.1.call-update
  326.5 0.0 all-reduce.2.cloned.1.call-start
  326.5 31.0 %reduce-scatter.5.cloned.1.call-done = f32[512,128]{1,0:T(8,128)} async-done(((f32[4096,128]{1,0:T(8,128)}), f32[512,128]{1,0:T(8,128)}) %reduce-scatter.5.cloned.1.call-update) | async-done | bytes 262160 | tf_op jit(solution)/shard_map/reduce_scatter | solution.py:53
  357.5 1.8 convolution_bitcast_fusion
  359.4 0.0 all-reduce.2.cloned.1.call-update
  359.4 0.0 copy-done.4
  359.4 1.8 convolution_convert_fusion.2
  361.2 141.8 %all-reduce.2.cloned.1.call-done = f32[128,128]{0,1:T(8,128)} async-done(((f32[128,128]{0,1:T(8,128)}), f32[128,128]{0,1:T(8,128)}) %all-reduce.2.cloned.1.call-update) | async-done | bytes 65552 | tf_op jit(solution)/shard_map/psum | solution.py:61
  503.0 0.8 broadcast_multiply_fusion
  503.9 0.7 copy.11
  (1 shorter events, 0.0 us)
Async XLA Ops:
  7.2 0.9 copy-start
  7.2 30.2 %all-gather.3.cloned.1.call-start = ((), (), s32[]{:S(2)}) async-start(), calls=%async_computation.2 | async-start | bytes 1179648 | tf_op jit(solution)/shard_map/all_gather | solution.py:41
  9.7 188.6 %reduce-scatter.3.cloned.1.call-start = ((), (), s32[]{:S(2)}) async-start(), calls=%async_computation.3 | async-start | bytes 4456448 | tf_op jit(solution)/shard_map/reduce_scatter | solution.py:45
  52.7 24.4 %copy-start.2 = (s32[1,1,512]{2,1,0:T(1,128)S(1)}, s32[1,1,512]{2,1,0:T(1,128)}, u32[]{:S(2)}) copy-start(s32[1,1,512]{2,1,0:T(1,128)} %param.10) | copy-start | bytes 6148
  77.2 121.1 %copy-start.3 = (bf16[512,128]{1,0:T(8,128)(2,1)S(1)}, bf16[512,128]{1,0:T(8,128)(2,1)}, u32[]{:S(2)}) copy-start(bf16[512,128]{1,0:T(8,128)(2,1)} %param.13) | copy-start | bytes 393220
  122.6 123.8 %all-gather.5.cloned.1.call-start = ((), (), s32[]{:S(2)}) async-start(), calls=%async_computation.4 | async-start | bytes 2228224 | tf_op jit(solution)/shard_map/all_gather | solution.py:49
  200.0 157.5 %reduce-scatter.5.cloned.1.call-start = ((), (), s32[]{:S(2)}) async-start(), calls=%async_computation.5 | async-start | bytes 2359296 | tf_op jit(solution)/shard_map/reduce_scatter | solution.py:53
  262.3 25.3 %copy-start.1 = (s32[1,1,512]{2,1,0:T(1,128)S(1)}, s32[1,1,512]{2,1,0:T(1,128)}, u32[]{:S(2)}) copy-start(s32[1,1,512]{2,1,0:T(1,128)} %param.11) | copy-start | bytes 6148
  287.7 71.7 %copy-start.4 = (bf16[128,128]{1,0:T(8,128)(2,1)S(1)}, bf16[128,128]{1,0:T(8,128)(2,1)}, u32[]{:S(2)}) copy-start(bf16[128,128]{1,0:T(8,128)(2,1)} %param.8) | copy-start | bytes 98308
  326.5 176.5 %all-reduce.2.cloned.1.call-start = ((), (), s32[]{:S(2)}) async-start(), calls=%async_computation.6 | async-start | bytes 131072 | tf_op jit(solution)/shard_map/psum | solution.py:61
Sparse Core Ops, SparseCore 0:
  10.3 26.9 all-gather.2
  122.7 75.5 reduce-scatter.2
  201.2 45.0 all-gather.4
  326.6 30.9 reduce-scatter.4
  363.4 139.5 all-reduce.1
where the time goes:
time: 512 us; the launch traced here: 511 us
  waiting for transfers between devices  322 us (63%)
  matrix products  143 us (28%)
  local copies, waits for them, and re-layouts  29 us (6%)
  between operations  14.5 us (3%)
    psum x1, waiting for transfers between devices, local(): weight_grad = lax.psum(weight_term, ('row', 'col')) * nodes_all ** (-0.5)  142 us
    dot_general x2, matrix products, add_blocks(): jnp.dot(selector, flat, precision=lax.Precision.HIGHEST, preferred_elemen...  77.8 us
    reduce_scatter x1, waiting for transfers between devices, local(): pre = lax.psum_scatter(partial_rows, 'col', scatter_dimension=0, tiled=True)  75.7 us
    all_gather x1, waiting for transfers between devices, local(): slope_all = lax.all_gather(slope, 'col', axis=0, tiled=True)  46.3 us
    reduce_scatter x1, waiting for transfers between devices, local(): lax.psum_scatter(partial_cols, 'row', scatter_dimension=0, tiled=True)  31 us
    all_gather x1, waiting for transfers between devices, local(): gathered = lax.all_gather(hidden, 'row', axis=0, tiled=True)  27 us
    dot_general x1, matrix products, local(): jnp.einsum('kij,kif->kjf', blocks, chosen, preferred_element_type=jnp.flo...  25.3 us
    dot_general x1, matrix products, local(): jnp.einsum('kij,kjf->kif', blocks, picked, preferred_element_type=jnp.flo...  24.4 us
  transfers between devices with their start and end apart: 5, of which 5 were waited for; matrix products, arithmetic and copies ran while one was open for 0% of the time, Pallas kernels for 0%

commit v1 on v0

v1 whole, which is shorter than its diff:
```python
import functools

import jax
import jax.numpy as jnp
from jax import lax
from jax.experimental import pallas as pl
from jax.experimental.pallas import tpu as pltpu
from jax.sharding import PartitionSpec as P

BLK = 128
NX = 4
NZ = 4
NY = 4
ROW_BLOCKS = 64
COL_BLOCKS = 32
CHUNK = 64
UNROLL = 8
F32 = jnp.float32
BF16 = jnp.bfloat16
VMEM_LIMIT = 48 * 1024 * 1024


def vmem_specs(n):
    return [pl.BlockSpec(memory_space=pltpu.VMEM)] * n


def params():
    return pltpu.CompilerParams(vmem_limit_bytes=VMEM_LIMIT)


def start_chunks(adj_ref, buf, sems, nchunks):
    def copy(i):
        return pltpu.make_async_copy(
            adj_ref.at[pl.ds(i * CHUNK, CHUNK)], buf.at[pl.ds(i * CHUNK, CHUNK)], sems.at[i]
        )

    @pl.loop(0, nchunks)
    def _(i):
        copy(i).start()

    return copy


def forward_kernel(nin, nout, target_ref, source_ref, count_ref, adj_ref, *refs):
    ins, outs = refs[:nin], refs[nin : nin + nout]
    buf, feats, acc, sems = refs[nin + nout :]
    live = count_ref[0]
    nchunks = pl.cdiv(live, CHUNK)
    copy = start_chunks(adj_ref, buf, sems, nchunks)
    per = feats.shape[0] // nin
    for i in range(nin):
        feats[pl.ds(i * per, per)] = ins[i][...].reshape(per, BLK, BLK)
    acc[...] = jnp.zeros_like(acc)

    @pl.loop(0, nchunks)
    def _(i):
        copy(i).wait()
        groups = pl.cdiv(jnp.minimum(live - i * CHUNK, CHUNK), UNROLL)

        @pl.loop(0, groups)
        def _(g):
            base = i * CHUNK + g * UNROLL
            prods = [
                jnp.dot(buf[base + j], feats[source_ref[base + j]], preferred_element_type=F32)
                for j in range(UNROLL)
            ]
            for j in range(UNROLL):
                acc[target_ref[base + j]] += prods[j]

    per = ROW_BLOCKS // nout
    for i in range(nout):
        outs[i][...] = acc[pl.ds(i * per, per)].reshape(per * BLK, BLK).astype(outs[i].dtype)


def forward(adjacency, target, source, count, pieces, nout):
    nin = len(pieces)
    rows = ROW_BLOCKS * BLK // nout
    return pl.pallas_call(
        functools.partial(forward_kernel, nin, nout),
        out_shape=[jax.ShapeDtypeStruct((rows, BLK), BF16)] * nout,
        in_specs=[pl.BlockSpec(memory_space=pltpu.SMEM)] * 3
        + [pl.BlockSpec(memory_space=pl.ANY)]
        + vmem_specs(nin),
        out_specs=vmem_specs(nout),
        scratch_shapes=[
            pltpu.VMEM(adjacency.shape, BF16),
            pltpu.VMEM((COL_BLOCKS, BLK, BLK), BF16),
            pltpu.VMEM((ROW_BLOCKS + 1, BLK, BLK), F32),
            pltpu.SemaphoreType.DMA((adjacency.shape[0] // CHUNK,)),
        ],
        compiler_params=params(),
        cost_estimate=pl.CostEstimate(
            flops=2 * 512 * BLK**3 * 4, bytes_accessed=20 * 2**20, transcendentals=0
        ),
        name="sparse_forward",
    )(target, source, count, adjacency, *pieces)


def backward_kernel(nin, target_ref, source_ref, count_ref, adj_ref, *refs):
    ins, (keep, send) = refs[:nin], refs[nin : nin + 2]
    buf, slopes, acc, sems = refs[nin + 2 :]
    live = count_ref[0]
    nchunks = pl.cdiv(live, CHUNK)
    copy = start_chunks(adj_ref, buf, sems, nchunks)
    per = slopes.shape[0] // nin
    for i in range(nin):
        slopes[pl.ds(i * per, per)] = ins[i][...].reshape(per, BLK, BLK)
    acc[...] = jnp.zeros_like(acc)

    @pl.loop(0, nchunks)
    def _(i):
        copy(i).wait()
        groups = pl.cdiv(jnp.minimum(live - i * CHUNK, CHUNK), UNROLL)

        @pl.loop(0, groups)
        def _(g):
            base = i * CHUNK + g * UNROLL
            prods = [
                jnp.dot(slopes[source_ref[base + j]], buf[base + j], preferred_element_type=F32)
                for j in range(UNROLL)
            ]
            for j in range(UNROLL):
                acc[target_ref[base + j]] += prods[j]

    half = COL_BLOCKS // 2
    for b in range(half):
        keep[pl.ds(b * BLK, BLK)] = acc[b].T.astype(keep.dtype)
        send[pl.ds(b * BLK, BLK)] = acc[half + b].T.astype(send.dtype)


def backward(adjacency, target, source, count, pieces):
    nin = len(pieces)
    rows = COL_BLOCKS * BLK // 2
    return pl.pallas_call(
        functools.partial(backward_kernel, nin),
        out_shape=[
            jax.ShapeDtypeStruct((rows, BLK), F32),
            jax.ShapeDtypeStruct((rows, BLK), F32),
        ],
        in_specs=[pl.BlockSpec(memory_space=pltpu.SMEM)] * 3
        + [pl.BlockSpec(memory_space=pl.ANY)]
        + vmem_specs(nin),
        out_specs=vmem_specs(2),
        scratch_shapes=[
            pltpu.VMEM(adjacency.shape, BF16),
            pltpu.VMEM((ROW_BLOCKS, BLK, BLK), BF16),
            pltpu.VMEM((COL_BLOCKS + 1, BLK, BLK), F32),
            pltpu.SemaphoreType.DMA((adjacency.shape[0] // CHUNK,)),
        ],
        compiler_params=params(),
        cost_estimate=pl.CostEstimate(
            flops=2 * 512 * BLK**3 * 4, bytes_accessed=20 * 2**20, transcendentals=0
        ),
        name="sparse_backward",
    )(target, source, count, adjacency, *pieces)


def add_split_kernel(nin, nout, *refs):
    ins, outs = refs[:nin], refs[nin:]
    rows = outs[0].shape[0]
    for i in range(nout):
        total = ins[0][pl.ds(i * rows, rows)].astype(F32)
        for part in ins[1:]:
            total += part[pl.ds(i * rows, rows)].astype(F32)
        outs[i][...] = total.astype(outs[i].dtype)


def add_split(parts, nout, name):
    rows = parts[0].shape[0] // nout
    return pl.pallas_call(
        functools.partial(add_split_kernel, len(parts), nout),
        out_shape=[jax.ShapeDtypeStruct((rows, BLK), F32)]
        + [jax.ShapeDtypeStruct((rows, BLK), BF16)] * (nout - 1),
        in_specs=vmem_specs(len(parts)),
        out_specs=vmem_specs(nout),
        compiler_params=params(),
        name=name,
    )(*parts)


def activate_kernel(weight_ref, grad_ref, *refs):
    first, second = refs[:4], refs[4:8]
    act_ref, slope_ref, total_ref, st_a, st_b = refs[8:]
    half = act_ref.shape[0] // 2
    for i, parts in enumerate((first, second)):
        total_ref[pl.ds(i * half, half)] = (
            parts[0][...] + parts[1][...].astype(F32) + parts[2][...].astype(F32) + parts[3][...].astype(F32)
        )
    pre = jnp.dot(
        total_ref[...], weight_ref[...].astype(F32), precision=lax.Precision.HIGHEST, preferred_element_type=F32
    )
    squash = jnp.tanh(pre)
    act_ref[...] = squash.astype(BF16)
    slope = (grad_ref[...].astype(F32) * (1.0 - squash * squash)).astype(BF16)
    slope_ref[...] = slope
    for i, out in enumerate((st_a, st_b)):
        for b in range(half // BLK):
            out[pl.ds(b * BLK, BLK)] = slope[i * half + b * BLK : i * half + (b + 1) * BLK].T


def activate(weight, grad_out, first, second):
    rows = grad_out.shape[0]
    return pl.pallas_call(
        activate_kernel,
        out_shape=[
            jax.ShapeDtypeStruct((rows, BLK), BF16),
            jax.ShapeDtypeStruct((rows, BLK), BF16),
            jax.ShapeDtypeStruct((rows, BLK), F32),
            jax.ShapeDtypeStruct((rows // 2, BLK), BF16),
            jax.ShapeDtypeStruct((rows // 2, BLK), BF16),
        ],
        in_specs=vmem_specs(10),
        out_specs=vmem_specs(5),
        compiler_params=params(),
        name="activate",
    )(weight, grad_out, *first, *second)


def finish_kernel(weight_ref, *refs):
    parts, out_ref = refs[:4], refs[4]
    total = parts[0][...]
    for part in parts[1:]:
        total += part[...].astype(F32)
    out_ref[...] = lax.dot_general(
        total.astype(BF16), weight_ref[...], (((1,), (1,)), ((), ())), preferred_element_type=F32
    ).astype(BF16)


def finish(weight, parts):
    return pl.pallas_call(
        finish_kernel,
        out_shape=jax.ShapeDtypeStruct(parts[0].shape, BF16),
        in_specs=vmem_specs(5),
        out_specs=pl.BlockSpec(memory_space=pltpu.VMEM),
        compiler_params=params(),
        name="finish",
    )(weight, *parts)


def shift_x(a, d):
    return lax.ppermute(a, "col", [(i, (i // NZ + d) % NX * NZ + i % NZ) for i in range(NX * NZ)])


def shift_z(a, d):
    return lax.ppermute(a, "col", [(i, i // NZ * NZ + (i % NZ + d) % NZ) for i in range(NX * NZ)])


def shift_y(a, d):
    return lax.ppermute(a, "row", [(i, (i // 2 + d) % NY * 2 + i % 2) for i in range(NY * 2)])


def swap_core(a):
    return lax.ppermute(a, "row", [(i, i ^ 1) for i in range(NY * 2)])


def sum_along(shift, a, n):
    return a + sum(shift(a, d) for d in range(1, n))


def local(features, weight, adjacency, row_index, col_index, block_count, grad_out):
    row, col = lax.axis_index("row"), lax.axis_index("col")
    y, core = row // 2, row % 2
    x, z = col // NZ, col % NZ
    blocks = adjacency[0, 0]
    count = block_count[0]
    alive = jnp.arange(blocks.shape[0], dtype=jnp.int32) < count[0]
    brow, bcol = row_index[0, 0], col_index[0, 0]

    rx, rz, rb = brow // 16, brow // 4 % 4, brow % 4
    cy, cc, cb = bcol // 8, bcol // 4 % 2, bcol % 4
    ex, gz = (rx - x) % NX, (rz - z) % NZ
    to_row = jnp.where(rb < 2, ex * 8 + gz * 2 + rb, 32 + gz * 8 + ex * 2 + rb - 2)
    to_row = jnp.where(alive, to_row, ROW_BLOCKS)
    ex, gz = (x - rx) % NX, (z - rz) % NZ
    from_row = jnp.where(rb < 2, gz * 8 + ex * 2 + rb, 32 + ex * 8 + gz * 2 + rb - 2)
    from_row = jnp.where(alive, from_row, 0)
    other = cc ^ core
    to_col = jnp.where(alive, other * 16 + (cy - y) % NY * 4 + cb, COL_BLOCKS)
    from_col = jnp.where(alive, other * 16 + (y - cy) % NY * 4 + cb, 0)

    mine = [features] + [shift_y(features, d) for d in range(1, NY)]
    theirs = [swap_core(a) for a in mine]

    parts = forward(blocks, to_row, from_col, count, mine + theirs, 8)
    first = [parts[0]] + [shift_x(parts[d], d) for d in range(1, NX)]
    second = [parts[4]] + [shift_z(parts[4 + d], d) for d in range(1, NZ)]
    first = add_split(first, NZ, "add_x")
    second = add_split(second, NX, "add_z")
    first = [first[0]] + [shift_z(first[d], d) for d in range(1, NZ)]
    second = [second[0]] + [shift_x(second[d], d) for d in range(1, NX)]
    activated, slope, total, slope_a, slope_b = activate(weight, grad_out, first, second)

    slope_a = jnp.concatenate([slope_a] + [shift_x(slope_a, d) for d in range(1, NX)])
    slope_b = jnp.concatenate([slope_b] + [shift_z(slope_b, d) for d in range(1, NZ)])
    slopes = [slope_a] + [shift_z(slope_a, d) for d in range(1, NZ)]
    slopes += [slope_b] + [shift_x(slope_b, d) for d in range(1, NX)]

    term = lax.dot_general(
        total, slope.astype(F32), (((0,), (0,)), ((), ())), precision=lax.Precision.HIGHEST, preferred_element_type=F32
    )
    term = term + swap_core(term)
    term = sum_along(shift_y, term, NY)
    term = sum_along(shift_x, term, NX)
    term = sum_along(shift_z, term, NZ)
    nodes_all = features.shape[0] * lax.axis_size("row") * lax.axis_size("col")
    weight_grad = term * nodes_all ** (-0.5)

    keep, send = backward(blocks, to_col, from_row, count, slopes)
    parts = add_split([keep, swap_core(send)], NY, "add_core")
    parts = [parts[0]] + [shift_y(parts[d], d) for d in range(1, NY)]
    input_grad = finish(weight, parts)
    return (activated, input_grad, weight_grad)


def solution(mesh):
    placed = (
        P(("col", "row"), None),
        P(),
        P("row", "col", None, None, None),
        P("row", "col", None),
        P("row", "col", None),
        P("row", "col"),
        P(("row", "col"), None),
    )
    return jax.shard_map(
        local,
        mesh=mesh,
        in_specs=placed,
        out_specs=(P(("row", "col"), None), P(("col", "row"), None), P()),
        check_vma=False,
    )
```

time: 512 us -> 149 us (0.29)
  the two profiles are of different devices: /device:TPU:1 before, /device:TPU:64 now
where the time goes in v1:
time: 149 us; the launch traced here: 148 us
  starting transfers between devices  76.9 us (52%)
  waiting for transfers between devices  41.3 us (28%)
  Pallas kernels  25.9 us (17%)
    ppermute x15, starting transfers between devices, shift_z(): lax.ppermute(a, 'col', [(i, i // NZ * NZ + (i % NZ + d) % NZ) for i in ra...  38.4 us
    ppermute x15, starting transfers between devices, shift_x(): lax.ppermute(a, 'col', [(i, (i // NZ + d) % NX * NZ + i % NZ) for i in ra...  21.9 us
    ppermute x9, starting transfers between devices, shift_y(): lax.ppermute(a, 'row', [(i, (i // 2 + d) % NY * 2 + i % 2) for i in range...  15.9 us
    ppermute x9, waiting for transfers between devices, shift_y(): lax.ppermute(a, 'row', [(i, (i // 2 + d) % NY * 2 + i % 2) for i in range...  15.7 us
    ppermute x15, waiting for transfers between devices, shift_x(): lax.ppermute(a, 'col', [(i, (i // NZ + d) % NX * NZ + i % NZ) for i in ra...  14.2 us
    pallas_call x1, Pallas kernels, backward(): pl.pallas_call(functools.partial(backward_kernel, nin), out_shape=[jax.Sh...  11.9 us
    pallas_call x1, Pallas kernels, forward(): pl.pallas_call(functools.partial(forward_kernel, nin, nout), out_shape=[j...  11.7 us
    ppermute x15, waiting for transfers between devices, shift_z(): lax.ppermute(a, 'col', [(i, i // NZ * NZ + (i % NZ + d) % NZ) for i in ra...  8.99 us
  transfers between devices with their start and end apart: 45, of which 23 were waited for; matrix products, arithmetic and copies ran while one was open for 1% of the time, Pallas kernels for 0%

profile of v1, /device:TPU:64, one launch (start us, length us, event | category | flops | bytes accessed | tf_op | source)
XLA Modules:
  0.0 148.4 jit_solution(10044724287244095888)
XLA Ops:
  0.6 3.1 %collective-permute-start.2 = (bf16[512,128]{1,0:T(8,128)(2,1)}, bf16[512,128]{1,0:T(8,128)(2,1)S(1)}, u32[]{:S(2)}, u32[]{:S(2)}) collective-permute-start(bf16[512,128]{1,0:T(8,128)(2,1)} %refs_0_.1), channel_id=1, source_target_pairs={{0,96},{16,112},{32,0},{48,16},{64,32},{80,48},{96,64},{112,80},{1... | collective-permute-start | bytes 393224 | tf_op jit(solution)/shard_map/ppermute | solution.py:249
  3.7 0.6 collective-permute-start.1
  4.3 1.0 collective-permute-start
  6.0 3.6 %collective-permute-done.2.refs_3_ = bf16[512,128]{1,0:T(8,128)(2,1)S(1)} collective-permute-done((bf16[512,128]{1,0:T(8,128)(2,1)}, bf16[512,128]{1,0:T(8,128)(2,1)S(1)}, u32[]{:S(2)}, u32[]{:S(2)}) %collective-permute-start.2) | collective-permute-done | bytes 131104 | tf_op jit(solution)/shard_map/ppermute | solution.py:249
  9.6 2.2 %collective-permute-done.1.refs_2_ = bf16[512,128]{1,0:T(8,128)(2,1)S(1)} collective-permute-done((bf16[512,128]{1,0:T(8,128)(2,1)}, bf16[512,128]{1,0:T(8,128)(2,1)S(1)}, u32[]{:S(2)}, u32[]{:S(2)}) %collective-permute-start.1) | collective-permute-done | bytes 131104 | tf_op jit(solution)/shard_map/ppermute | solution.py:249
  11.8 1.4 collective-permute-done.refs_1_
  13.2 0.7 fusion.17
  14.0 0.6 collective-permute-done.4.refs_5_
  14.5 0.9 copy-done.2
  15.5 11.7 %sparse_forward.1 = (bf16[1024,128]{1,0:T(8,128)(2,1)S(1)}, bf16[1024,128]{1,0:T(8,128)(2,1)S(1)}, bf16[1024,128]{1,0:T(8,128)(2,1)S(1)}, bf16[1024,128]{1,0:T(8...) custom-call(s32[512]{0:T(512)S(1)} %get-tuple-element.61.target_ref,, ...), custom_call_target="tpu_custom_call" | custom-call | flops 8589934592 | bytes 20971520 | tf_op jit(solution)/shard_map/sparse_forward/pallas_call | solution.py:78
  27.3 4.6 %collective-permute-start.8 = (bf16[1024,128]{1,0:T(8,128)(2,1)S(1)}, bf16[1024,128]{1,0:T(8,128)(2,1)S(1)}, u32[]{:S(2)}, u32[]{:S(2)}) collective-permute-start(bf16[1024,128]{1,0:T(8,128)(2,1)S(1)} %get-tuple-element.32), channel_id=1, source_target_pairs={{0,8},{1,9},{2,10},{3,11},{4,12},{5,13},{6,14},{7,15},{8,0},{9,1},... | collective-permute-start | bytes 786440 | tf_op jit(solution)/shard_map/ppermute | solution.py:241
  31.9 1.4 collective-permute-start.9
  33.4 1.9 %collective-permute-start.13 = (bf16[1024,128]{1,0:T(8,128)(2,1)S(1)}, bf16[1024,128]{1,0:T(8,128)(2,1)S(1)}, u32[]{:S(2)}, u32[]{:S(2)}) collective-permute-start(bf16[1024,128]{1,0:T(8,128)(2,1)S(1)} %get-tuple-element.39), channel_id=1, source_target_pairs={{0,1},{1,2},{2,3},{3,0},{4,5},{5,6},{6,7},{7,4},{8,9},{9,10},{10,1... | collective-permute-start | bytes 786440 | tf_op jit(solution)/shard_map/ppermute | solution.py:245
  35.2 2.3 %collective-permute-start.14 = (bf16[1024,128]{1,0:T(8,128)(2,1)S(1)}, bf16[1024,128]{1,0:T(8,128)(2,1)S(1)}, u32[]{:S(2)}, u32[]{:S(2)}) collective-permute-start(bf16[1024,128]{1,0:T(8,128)(2,1)S(1)} %get-tuple-element.40), channel_id=1, source_target_pairs={{0,2},{1,3},{2,0},{3,1},{4,6},{5,7},{6,4},{7,5},{8,10},{9,11},{10,... | collective-permute-start | bytes 786440 | tf_op jit(solution)/shard_map/ppermute | solution.py:245
  37.5 7.2 %collective-permute-start.15 = (bf16[1024,128]{1,0:T(8,128)(2,1)S(1)}, bf16[1024,128]{1,0:T(8,128)(2,1)S(1)}, u32[]{:S(2)}, u32[]{:S(2)}) collective-permute-start(bf16[1024,128]{1,0:T(8,128)(2,1)S(1)} %get-tuple-element.41), channel_id=1, source_target_pairs={{0,3},{1,0},{2,1},{3,2},{4,7},{5,4},{6,5},{7,6},{8,11},{9,8},{10,9... | collective-permute-start | bytes 786440 | tf_op jit(solution)/shard_map/ppermute | solution.py:245
  44.8 1.7 %collective-permute-start.10 = (bf16[256,128]{1,0:T(8,128)(2,1)S(1)}, bf16[256,128]{1,0:T(8,128)(2,1)S(1)}, u32[]{:S(2)}, u32[]{:S(2)}) collective-permute-start(bf16[256,128]{1,0:T(8,128)(2,1)S(1)} %get-tuple-element.35), channel_id=1, source_target_pairs={{0,1},{1,2},{2,3},{3,0},{4,5},{5,6},{6,7},{7,4},{8,9},{9,10},{10,1... | collective-permute-start | bytes 196616 | tf_op jit(solution)/shard_map/ppermute | solution.py:245
  46.5 2.8 %collective-permute-start.11 = (bf16[256,128]{1,0:T(8,128)(2,1)S(1)}, bf16[256,128]{1,0:T(8,128)(2,1)S(1)}, u32[]{:S(2)}, u32[]{:S(2)}) collective-permute-start(bf16[256,128]{1,0:T(8,128)(2,1)S(1)} %get-tuple-element.36), channel_id=1, source_target_pairs={{0,2},{1,3},{2,0},{3,1},{4,6},{5,7},{6,4},{7,5},{8,10},{9,11},{10,... | collective-permute-start | bytes 196616 | tf_op jit(solution)/shard_map/ppermute | solution.py:245
  49.3 1.3 collective-permute-start.12
  50.6 1.5 collective-permute-done.15.refs_3_
  52.2 0.5 collective-permute-start.16
  52.7 1.8 %collective-permute-start.17 = (bf16[256,128]{1,0:T(8,128)(2,1)S(1)}, bf16[256,128]{1,0:T(8,128)(2,1)S(1)}, u32[]{:S(2)}, u32[]{:S(2)}) collective-permute-start(bf16[256,128]{1,0:T(8,128)(2,1)S(1)} %get-tuple-element.44), channel_id=1, source_target_pairs={{0,8},{1,9},{2,10},{3,11},{4,12},{5,13},{6,14},{7,15},{8,0},{9,1},... | collective-permute-start | bytes 196616 | tf_op jit(solution)/shard_map/ppermute | solution.py:241
  54.5 1.8 %collective-permute-start.18 = (bf16[256,128]{1,0:T(8,128)(2,1)S(1)}, bf16[256,128]{1,0:T(8,128)(2,1)S(1)}, u32[]{:S(2)}, u32[]{:S(2)}) collective-permute-start(bf16[256,128]{1,0:T(8,128)(2,1)S(1)} %get-tuple-element.45), channel_id=1, source_target_pairs={{0,12},{1,13},{2,14},{3,15},{4,0},{5,1},{6,2},{7,3},{8,4},{9,5},{1... | collective-permute-start | bytes 196616 | tf_op jit(solution)/shard_map/ppermute | solution.py:241
  56.3 1.4 collective-permute-done.16.refs_5_
  57.8 1.2 collective-permute-done.17.refs_6_
  59.0 1.4 collective-permute-done.18.refs_7_
  60.4 1.0 activate.1
  61.4 3.0 %collective-permute-start.21 = (bf16[256,128]{1,0:T(8,128)(2,1)S(1)}, bf16[256,128]{1,0:T(8,128)(2,1)S(1)}, u32[]{:S(2)}, u32[]{:S(2)}) collective-permute-start(bf16[256,128]{1,0:T(8,128)(2,1)S(1)} %get-tuple-element.47), channel_id=1, source_target_pairs={{0,12},{1,13},{2,14},{3,15},{4,0},{5,1},{6,2},{7,3},{8,4},{9,5},{1... | collective-permute-start | bytes 196616 | tf_op jit(solution)/shard_map/ppermute | solution.py:241
  64.5 0.8 collective-permute-start.19
  65.3 0.9 collective-permute-start.27
  66.2 2.0 %collective-permute-start.25 = (bf16[256,128]{1,0:T(8,128)(2,1)S(1)}, bf16[256,128]{1,0:T(8,128)(2,1)S(1)}, u32[]{:S(2)}, u32[]{:S(2)}) collective-permute-start(bf16[256,128]{1,0:T(8,128)(2,1)S(1)} %get-tuple-element.48), channel_id=1, source_target_pairs={{0,1},{1,2},{2,3},{3,0},{4,5},{5,6},{6,7},{7,4},{8,9},{9,10},{10,1... | collective-permute-start | bytes 196616 | tf_op jit(solution)/shard_map/ppermute | solution.py:245
  68.2 2.8 %collective-permute-done.25 = bf16[256,128]{1,0:T(8,128)(2,1)S(1)} collective-permute-done((bf16[256,128]{1,0:T(8,128)(2,1)S(1)}, bf16[256,128]{1,0:T(8,128)(2,1)S(1)}, u32[]{:S(2)}, u32[]{:S(2)}) %collective-permute-start.25) | collective-permute-done | bytes 65568 | tf_op jit(solution)/shard_map/ppermute | solution.py:245
  71.0 4.8 %collective-permute-start.26 = (bf16[256,128]{1,0:T(8,128)(2,1)S(1)}, bf16[256,128]{1,0:T(8,128)(2,1)S(1)}, u32[]{:S(2)}, u32[]{:S(2)}) collective-permute-start(bf16[256,128]{1,0:T(8,128)(2,1)S(1)} %get-tuple-element.48), channel_id=1, source_target_pairs={{0,2},{1,3},{2,0},{3,1},{4,6},{5,7},{6,4},{7,5},{8,10},{9,11},{10,... | collective-permute-start | bytes 196616 | tf_op jit(solution)/shard_map/ppermute | solution.py:245
  75.8 2.2 %collective-permute-done.26 = bf16[256,128]{1,0:T(8,128)(2,1)S(1)} collective-permute-done((bf16[256,128]{1,0:T(8,128)(2,1)S(1)}, bf16[256,128]{1,0:T(8,128)(2,1)S(1)}, u32[]{:S(2)}, u32[]{:S(2)}) %collective-permute-start.26) | collective-permute-done | bytes 65568 | tf_op jit(solution)/shard_map/ppermute | solution.py:245
  78.0 3.3 %collective-permute-start.30 = (bf16[1024,128]{1,0:T(8,128)(2,1)S(1)}, bf16[1024,128]{1,0:T(8,128)(2,1)S(1)}, u32[]{:S(2)}, u32[]{:S(2)}) collective-permute-start(bf16[1024,128]{1,0:T(8,128)(2,1)S(1)} %constant_dynamic-update-slice_fusion.4.refs_4_), channel_id=1, source_target_pairs={{0,12},{1,13},{2,14},{3,15},{4,0},{5,1},{6,2},{7,3},{8,4},{9,5},{1... | collective-permute-start | bytes 786440 | tf_op jit(solution)/shard_map/ppermute | solution.py:241
  81.3 1.0 collective-permute-start.29
  82.5 1.4 collective-permute-start.24
  83.9 2.3 %collective-permute-start.23 = (bf16[1024,128]{1,0:T(8,128)(2,1)S(1)}, bf16[1024,128]{1,0:T(8,128)(2,1)S(1)}, u32[]{:S(2)}, u32[]{:S(2)}) collective-permute-start(bf16[1024,128]{1,0:T(8,128)(2,1)S(1)} %constant_dynamic-update-slice_fusion.refs_0_), channel_id=1, source_target_pairs={{0,2},{1,3},{2,0},{3,1},{4,6},{5,7},{6,4},{7,5},{8,10},{9,11},{10,... | collective-permute-start | bytes 786440 | tf_op jit(solution)/shard_map/ppermute | solution.py:245
  86.2 1.9 %collective-permute-done.30.refs_7_ = bf16[1024,128]{1,0:T(8,128)(2,1)S(1)} collective-permute-done((bf16[1024,128]{1,0:T(8,128)(2,1)S(1)}, bf16[1024,128]{1,0:T(8,128)(2,1)S(1)}, u32[]{:S(2)}, u32[]{:S(2)}) %collective-permute-start.30) | collective-permute-done | bytes 262176 | tf_op jit(solution)/shard_map/ppermute | solution.py:241
  88.0 1.2 collective-permute-start.22
  89.3 2.7 %collective-permute-done.28.refs_5_ = bf16[1024,128]{1,0:T(8,128)(2,1)S(1)} collective-permute-done((bf16[1024,128]{1,0:T(8,128)(2,1)S(1)}, bf16[1024,128]{1,0:T(8,128)(2,1)S(1)}, u32[]{:S(2)}, u32[]{:S(2)}) %collective-permute-start.28) | collective-permute-done | bytes 262176 | tf_op jit(solution)/shard_map/ppermute | solution.py:241
  92.0 2.5 %collective-permute-done.22.refs_1_ = bf16[1024,128]{1,0:T(8,128)(2,1)S(1)} collective-permute-done((bf16[1024,128]{1,0:T(8,128)(2,1)S(1)}, bf16[1024,128]{1,0:T(8,128)(2,1)S(1)}, u32[]{:S(2)}, u32[]{:S(2)}) %collective-permute-start.22) | collective-permute-done | bytes 262176 | tf_op jit(solution)/shard_map/ppermute | solution.py:245
  94.5 11.9 %sparse_backward.1 = (f32[2048,128]{1,0:T(8,128)S(1)}, f32[2048,128]{1,0:T(8,128)S(1)}) custom-call(s32[512]{0:T(512)S(1)} %get-tuple-element.59.target_ref, s32[512]{0:T(512)S(1)} %get-tuple-element.62.source_ref, s32[1]{0:T(128)} %bitcast.9.count_ref, bf16[512,128,128]{2,1,0:T(8,128)(2,1)} %bitcast.13, ...), custom_call_target="tpu_custom_call" | custom-call | flops 8589934592 | bytes 20971520 | tf_op jit(solution)/shard_map/sparse_backward/pallas_call | solution.py:134
  107.0 0.6 collective-permute-start.35
  107.5 1.8 %collective-permute-done.35 = f32[128,128]{1,0:T(8,128)S(1)} collective-permute-done((f32[128,128]{1,0:T(8,128)S(1)}, f32[128,128]{1,0:T(8,128)S(1)}, u32[]{:S(2)}, u32[]{:S(2)}) %collective-permute-start.35) | collective-permute-done | bytes 65568 | tf_op jit(solution)/shard_map/ppermute | solution.py:253
  109.3 3.3 %collective-permute-start.38 = (f32[128,128]{1,0:T(8,128)S(1)}, f32[128,128]{1,0:T(8,128)S(1)}, u32[]{:S(2)}, u32[]{:S(2)}) collective-permute-start(f32[128,128]{1,0:T(8,128)S(1)} %add.155), channel_id=1, source_target_pairs={{0,96},{16,112},{32,0},{48,16},{64,32},{80,48},{96,64},{112,80},{1... | collective-permute-start | bytes 196616 | tf_op jit(solution)/shard_map/ppermute | solution.py:249
  112.7 3.0 %collective-permute-start.37 = (f32[128,128]{1,0:T(8,128)S(1)}, f32[128,128]{1,0:T(8,128)S(1)}, u32[]{:S(2)}, u32[]{:S(2)}) collective-permute-start(f32[128,128]{1,0:T(8,128)S(1)} %add.155), channel_id=1, source_target_pairs={{0,64},{16,80},{32,96},{48,112},{64,0},{80,16},{96,32},{112,48},{1... | collective-permute-start | bytes 196616 | tf_op jit(solution)/shard_map/ppermute | solution.py:249
  115.7 1.3 collective-permute-start.36
  117.0 1.8 %collective-permute-done.37 = f32[128,128]{1,0:T(8,128)S(1)} collective-permute-done((f32[128,128]{1,0:T(8,128)S(1)}, f32[128,128]{1,0:T(8,128)S(1)}, u32[]{:S(2)}, u32[]{:S(2)}) %collective-permute-start.37) | collective-permute-done | bytes 65568 | tf_op jit(solution)/shard_map/ppermute | solution.py:249
  118.8 2.4 %collective-permute-done.36 = f32[128,128]{1,0:T(8,128)S(1)} collective-permute-done((f32[128,128]{1,0:T(8,128)S(1)}, f32[128,128]{1,0:T(8,128)S(1)}, u32[]{:S(2)}, u32[]{:S(2)}) %collective-permute-start.36) | collective-permute-done | bytes 65568 | tf_op jit(solution)/shard_map/ppermute | solution.py:249
  121.2 2.0 %collective-permute-start.41 = (f32[128,128]{1,0:T(8,128)S(1)}, f32[128,128]{1,0:T(8,128)S(1)}, u32[]{:S(2)}, u32[]{:S(2)}) collective-permute-start(f32[128,128]{1,0:T(8,128)S(1)} %add_add_fusion.1), channel_id=1, source_target_pairs={{0,12},{1,13},{2,14},{3,15},{4,0},{5,1},{6,2},{7,3},{8,4},{9,5},{1... | collective-permute-start | bytes 196616 | tf_op jit(solution)/shard_map/ppermute | solution.py:241
  123.2 1.3 collective-permute-start.40
  124.5 1.2 collective-permute-done.41
  125.8 3.3 %collective-permute-done.40 = f32[128,128]{1,0:T(8,128)S(1)} collective-permute-done((f32[128,128]{1,0:T(8,128)S(1)}, f32[128,128]{1,0:T(8,128)S(1)}, u32[]{:S(2)}, u32[]{:S(2)}) %collective-permute-start.40) | collective-permute-done | bytes 65568 | tf_op jit(solution)/shard_map/ppermute | solution.py:241
  129.0 1.0 collective-permute-done.39
  130.0 2.5 %collective-permute-start.44 = (f32[128,128]{1,0:T(8,128)S(1)}, f32[128,128]{1,0:T(8,128)S(1)}, u32[]{:S(2)}, u32[]{:S(2)}) collective-permute-start(f32[128,128]{1,0:T(8,128)S(1)} %add_add_fusion), channel_id=1, source_target_pairs={{0,3},{1,0},{2,1},{3,2},{4,7},{5,4},{6,5},{7,6},{8,11},{9,8},{10,9... | collective-permute-start | bytes 196616 | tf_op jit(solution)/shard_map/ppermute | solution.py:245
  132.5 3.7 %collective-permute-start.43 = (f32[128,128]{1,0:T(8,128)S(1)}, f32[128,128]{1,0:T(8,128)S(1)}, u32[]{:S(2)}, u32[]{:S(2)}) collective-permute-start(f32[128,128]{1,0:T(8,128)S(1)} %add_add_fusion), channel_id=1, source_target_pairs={{0,2},{1,3},{2,0},{3,1},{4,6},{5,7},{6,4},{7,5},{8,10},{9,11},{10,... | collective-permute-start | bytes 196616 | tf_op jit(solution)/shard_map/ppermute | solution.py:245
  136.2 2.5 %collective-permute-start.42 = (f32[128,128]{1,0:T(8,128)S(1)}, f32[128,128]{1,0:T(8,128)S(1)}, u32[]{:S(2)}, u32[]{:S(2)}) collective-permute-start(f32[128,128]{1,0:T(8,128)S(1)} %add_add_fusion), channel_id=1, source_target_pairs={{0,1},{1,2},{2,3},{3,0},{4,5},{5,6},{6,7},{7,4},{8,9},{9,10},{10,1... | collective-permute-start | bytes 196616 | tf_op jit(solution)/shard_map/ppermute | solution.py:245
  139.0 0.6 collective-permute-start.32
  139.6 2.6 %collective-permute-start.33 = (bf16[512,128]{1,0:T(8,128)(2,1)S(1)}, bf16[512,128]{1,0:T(8,128)(2,1)S(1)}, u32[]{:S(2)}, u32[]{:S(2)}) collective-permute-start(bf16[512,128]{1,0:T(8,128)(2,1)S(1)} %get-tuple-element.53), channel_id=1, source_target_pairs={{0,64},{16,80},{32,96},{48,112},{64,0},{80,16},{96,32},{112,48},{1... | collective-permute-start | bytes 393224 | tf_op jit(solution)/shard_map/ppermute | solution.py:249
  142.5 0.7 add_multiply_fusion
  143.2 2.1 %collective-permute-done.32.refs_1_ = bf16[512,128]{1,0:T(8,128)(2,1)S(1)} collective-permute-done((bf16[512,128]{1,0:T(8,128)(2,1)S(1)}, bf16[512,128]{1,0:T(8,128)(2,1)S(1)}, u32[]{:S(2)}, u32[]{:S(2)}) %collective-permute-start.32) | collective-permute-done | bytes 131104 | tf_op jit(solution)/shard_map/ppermute | solution.py:249
  145.2 1.4 collective-permute-done.33.refs_2_
  146.6 0.9 collective-permute-done.34.refs_3_
  147.5 0.8 finish.1
  (53 shorter events, 1.8 us)
Async XLA Ops:
  0.6 9.0 %collective-permute-start.2 = (bf16[512,128]{1,0:T(8,128)(2,1)}, bf16[512,128]{1,0:T(8,128)(2,1)S(1)}, u32[]{:S(2)}, u32[]{:S(2)}) collective-permute-start(bf16[512,128]{1,0:T(8,128)(2,1)} %refs_0_.1), channel_id=1, source_target_pairs={{0,96},{16,112},{32,0},{48,16},{64,32},{80,48},{96,64},{112,80},{1... | collective-permute-start | bytes 393224 | tf_op jit(solution)/shard_map/ppermute | solution.py:249
  3.7 8.1 %collective-permute-start.1 = (bf16[512,128]{1,0:T(8,128)(2,1)}, bf16[512,128]{1,0:T(8,128)(2,1)S(1)}, u32[]{:S(2)}, u32[]{:S(2)}) collective-permute-start(bf16[512,128]{1,0:T(8,128)(2,1)} %refs_0_.1), channel_id=1, source_target_pairs={{0,64},{16,80},{32,96},{48,112},{64,0},{80,16},{96,32},{112,48},{1... | collective-permute-start | bytes 393224 | tf_op jit(solution)/shard_map/ppermute | solution.py:249
  4.3 8.9 %collective-permute-start = (bf16[512,128]{1,0:T(8,128)(2,1)}, bf16[512,128]{1,0:T(8,128)(2,1)S(1)}, u32[]{:S(2)}, u32[]{:S(2)}) collective-permute-start(bf16[512,128]{1,0:T(8,128)(2,1)} %refs_0_.1), channel_id=1, source_target_pairs={{0,32},{16,48},{32,64},{48,80},{64,96},{80,112},{96,0},{112,16},{1... | collective-permute-start | bytes 393224 | tf_op jit(solution)/shard_map/ppermute | solution.py:249
  5.3 8.6 %collective-permute-start.3 = (bf16[512,128]{1,0:T(8,128)(2,1)}, bf16[512,128]{1,0:T(8,128)(2,1)S(1)}, u32[]{:S(2)}, u32[]{:S(2)}) collective-permute-start(bf16[512,128]{1,0:T(8,128)(2,1)} %refs_0_.1), channel_id=1, source_target_pairs={{0,16},{16,0},{32,48},{48,32},{64,80},{80,64},{96,112},{112,96},{1... | collective-permute-start | bytes 393224 | tf_op jit(solution)/shard_map/ppermute | solution.py:253
  9.6 4.4 %collective-permute-start.6 = (bf16[512,128]{1,0:T(8,128)(2,1)S(1)}, bf16[512,128]{1,0:T(8,128)(2,1)S(1)}, u32[]{:S(2)}, u32[]{:S(2)}) collective-permute-start(bf16[512,128]{1,0:T(8,128)(2,1)S(1)} %collective-permute-done.2.refs_3_), channel_id=1, source_target_pairs={{0,16},{16,0},{32,48},{48,32},{64,80},{80,64},{96,112},{112,96},{1... | collective-permute-start | bytes 393224 | tf_op jit(solution)/shard_map/ppermute | solution.py:253
  11.8 2.2 %collective-permute-start.5 = (bf16[512,128]{1,0:T(8,128)(2,1)S(1)}, bf16[512,128]{1,0:T(8,128)(2,1)S(1)}, u32[]{:S(2)}, u32[]{:S(2)}) collective-permute-start(bf16[512,128]{1,0:T(8,128)(2,1)S(1)} %collective-permute-done.1.refs_2_), channel_id=1, source_target_pairs={{0,16},{16,0},{32,48},{48,32},{64,80},{80,64},{96,112},{112,96},{1... | collective-permute-start | bytes 393224 | tf_op jit(solution)/shard_map/ppermute | solution.py:253
  13.2 1.3 collective-permute-start.4
  14.5 0.9 copy-start.2
  15.4 44.9 %copy-start = (bf16[512,128]{1,0:T(8,128)(2,1)S(1)}, bf16[512,128]{1,0:T(8,128)(2,1)}, u32[]{:S(2)}) copy-start(bf16[512,128]{1,0:T(8,128)(2,1)} %grad_ref.1) | copy-start | bytes 393220
  15.5 44.9 %copy-start.1 = (bf16[128,128]{1,0:T(8,128)(2,1)S(1)}, bf16[128,128]{1,0:T(8,128)(2,1)}, u32[]{:S(2)}) copy-start(bf16[128,128]{1,0:T(8,128)(2,1)} %weight_ref.3) | copy-start | bytes 98308
  27.1 10.3 %collective-permute-start.7 = (bf16[1024,128]{1,0:T(8,128)(2,1)S(1)}, bf16[1024,128]{1,0:T(8,128)(2,1)S(1)}, u32[]{:S(2)}, u32[]{:S(2)}) collective-permute-start(bf16[1024,128]{1,0:T(8,128)(2,1)S(1)} %get-tuple-element.31), channel_id=1, source_target_pairs={{0,4},{1,5},{2,6},{3,7},{4,8},{5,9},{6,10},{7,11},{8,12},{9,13},{1... | collective-permute-start | bytes 786440 | tf_op jit(solution)/shard_map/ppermute | solution.py:241
  27.3 17.4 %collective-permute-start.8 = (bf16[1024,128]{1,0:T(8,128)(2,1)S(1)}, bf16[1024,128]{1,0:T(8,128)(2,1)S(1)}, u32[]{:S(2)}, u32[]{:S(2)}) collective-permute-start(bf16[1024,128]{1,0:T(8,128)(2,1)S(1)} %get-tuple-element.32), channel_id=1, source_target_pairs={{0,8},{1,9},{2,10},{3,11},{4,12},{5,13},{6,14},{7,15},{8,0},{9,1},... | collective-permute-start | bytes 786440 | tf_op jit(solution)/shard_map/ppermute | solution.py:241
  31.9 12.7 %collective-permute-start.9 = (bf16[1024,128]{1,0:T(8,128)(2,1)S(1)}, bf16[1024,128]{1,0:T(8,128)(2,1)S(1)}, u32[]{:S(2)}, u32[]{:S(2)}) collective-permute-start(bf16[1024,128]{1,0:T(8,128)(2,1)S(1)} %get-tuple-element.33), channel_id=1, source_target_pairs={{0,12},{1,13},{2,14},{3,15},{4,0},{5,1},{6,2},{7,3},{8,4},{9,5},{1... | collective-permute-start | bytes 786440 | tf_op jit(solution)/shard_map/ppermute | solution.py:241
  33.4 15.9 %collective-permute-start.13 = (bf16[1024,128]{1,0:T(8,128)(2,1)S(1)}, bf16[1024,128]{1,0:T(8,128)(2,1)S(1)}, u32[]{:S(2)}, u32[]{:S(2)}) collective-permute-start(bf16[1024,128]{1,0:T(8,128)(2,1)S(1)} %get-tuple-element.39), channel_id=1, source_target_pairs={{0,1},{1,2},{2,3},{3,0},{4,5},{5,6},{6,7},{7,4},{8,9},{9,10},{10,1... | collective-permute-start | bytes 786440 | tf_op jit(solution)/shard_map/ppermute | solution.py:245
  35.2 15.4 %collective-permute-start.14 = (bf16[1024,128]{1,0:T(8,128)(2,1)S(1)}, bf16[1024,128]{1,0:T(8,128)(2,1)S(1)}, u32[]{:S(2)}, u32[]{:S(2)}) collective-permute-start(bf16[1024,128]{1,0:T(8,128)(2,1)S(1)} %get-tuple-element.40), channel_id=1, source_target_pairs={{0,2},{1,3},{2,0},{3,1},{4,6},{5,7},{6,4},{7,5},{8,10},{9,11},{10,... | collective-permute-start | bytes 786440 | tf_op jit(solution)/shard_map/ppermute | solution.py:245
  37.5 14.6 %collective-permute-start.15 = (bf16[1024,128]{1,0:T(8,128)(2,1)S(1)}, bf16[1024,128]{1,0:T(8,128)(2,1)S(1)}, u32[]{:S(2)}, u32[]{:S(2)}) collective-permute-start(bf16[1024,128]{1,0:T(8,128)(2,1)S(1)} %get-tuple-element.41), channel_id=1, source_target_pairs={{0,3},{1,0},{2,1},{3,2},{4,7},{5,4},{6,5},{7,6},{8,11},{9,8},{10,9... | collective-permute-start | bytes 786440 | tf_op jit(solution)/shard_map/ppermute | solution.py:245
  44.8 9.7 %collective-permute-start.10 = (bf16[256,128]{1,0:T(8,128)(2,1)S(1)}, bf16[256,128]{1,0:T(8,128)(2,1)S(1)}, u32[]{:S(2)}, u32[]{:S(2)}) collective-permute-start(bf16[256,128]{1,0:T(8,128)(2,1)S(1)} %get-tuple-element.35), channel_id=1, source_target_pairs={{0,1},{1,2},{2,3},{3,0},{4,5},{5,6},{6,7},{7,4},{8,9},{9,10},{10,1... | collective-permute-start | bytes 196616 | tf_op jit(solution)/shard_map/ppermute | solution.py:245
  46.5 9.8 %collective-permute-start.11 = (bf16[256,128]{1,0:T(8,128)(2,1)S(1)}, bf16[256,128]{1,0:T(8,128)(2,1)S(1)}, u32[]{:S(2)}, u32[]{:S(2)}) collective-permute-start(bf16[256,128]{1,0:T(8,128)(2,1)S(1)} %get-tuple-element.36), channel_id=1, source_target_pairs={{0,2},{1,3},{2,0},{3,1},{4,6},{5,7},{6,4},{7,5},{8,10},{9,11},{10,... | collective-permute-start | bytes 196616 | tf_op jit(solution)/shard_map/ppermute | solution.py:245
  49.3 7.0 %collective-permute-start.12 = (bf16[256,128]{1,0:T(8,128)(2,1)S(1)}, bf16[256,128]{1,0:T(8,128)(2,1)S(1)}, u32[]{:S(2)}, u32[]{:S(2)}) collective-permute-start(bf16[256,128]{1,0:T(8,128)(2,1)S(1)} %get-tuple-element.37), channel_id=1, source_target_pairs={{0,3},{1,0},{2,1},{3,2},{4,7},{5,4},{6,5},{7,6},{8,11},{9,8},{10,9... | collective-permute-start | bytes 196616 | tf_op jit(solution)/shard_map/ppermute | solution.py:245
  52.2 5.5 %collective-permute-start.16 = (bf16[256,128]{1,0:T(8,128)(2,1)S(1)}, bf16[256,128]{1,0:T(8,128)(2,1)S(1)}, u32[]{:S(2)}, u32[]{:S(2)}) collective-permute-start(bf16[256,128]{1,0:T(8,128)(2,1)S(1)} %get-tuple-element.43), channel_id=1, source_target_pairs={{0,4},{1,5},{2,6},{3,7},{4,8},{5,9},{6,10},{7,11},{8,12},{9,13},{1... | collective-permute-start | bytes 196616 | tf_op jit(solution)/shard_map/ppermute | solution.py:241
  52.7 6.3 %collective-permute-start.17 = (bf16[256,128]{1,0:T(8,128)(2,1)S(1)}, bf16[256,128]{1,0:T(8,128)(2,1)S(1)}, u32[]{:S(2)}, u32[]{:S(2)}) collective-permute-start(bf16[256,128]{1,0:T(8,128)(2,1)S(1)} %get-tuple-element.44), channel_id=1, source_target_pairs={{0,8},{1,9},{2,10},{3,11},{4,12},{5,13},{6,14},{7,15},{8,0},{9,1},... | collective-permute-start | bytes 196616 | tf_op jit(solution)/shard_map/ppermute | solution.py:241
  54.5 5.8 %collective-permute-start.18 = (bf16[256,128]{1,0:T(8,128)(2,1)S(1)}, bf16[256,128]{1,0:T(8,128)(2,1)S(1)}, u32[]{:S(2)}, u32[]{:S(2)}) collective-permute-start(bf16[256,128]{1,0:T(8,128)(2,1)S(1)} %get-tuple-element.45), channel_id=1, source_target_pairs={{0,12},{1,13},{2,14},{3,15},{4,0},{5,1},{6,2},{7,3},{8,4},{9,5},{1... | collective-permute-start | bytes 196616 | tf_op jit(solution)/shard_map/ppermute | solution.py:241
  61.4 21.0 %collective-permute-start.21 = (bf16[256,128]{1,0:T(8,128)(2,1)S(1)}, bf16[256,128]{1,0:T(8,128)(2,1)S(1)}, u32[]{:S(2)}, u32[]{:S(2)}) collective-permute-start(bf16[256,128]{1,0:T(8,128)(2,1)S(1)} %get-tuple-element.47), channel_id=1, source_target_pairs={{0,12},{1,13},{2,14},{3,15},{4,0},{5,1},{6,2},{7,3},{8,4},{9,5},{1... | collective-permute-start | bytes 196616 | tf_op jit(solution)/shard_map/ppermute | solution.py:241
  64.4 18.0 %collective-permute-start.20 = (bf16[256,128]{1,0:T(8,128)(2,1)S(1)}, bf16[256,128]{1,0:T(8,128)(2,1)S(1)}, u32[]{:S(2)}, u32[]{:S(2)}) collective-permute-start(bf16[256,128]{1,0:T(8,128)(2,1)S(1)} %get-tuple-element.47), channel_id=1, source_target_pairs={{0,8},{1,9},{2,10},{3,11},{4,12},{5,13},{6,14},{7,15},{8,0},{9,1},... | collective-permute-start | bytes 196616 | tf_op jit(solution)/shard_map/ppermute | solution.py:241
  64.5 17.9 %collective-permute-start.19 = (bf16[256,128]{1,0:T(8,128)(2,1)S(1)}, bf16[256,128]{1,0:T(8,128)(2,1)S(1)}, u32[]{:S(2)}, u32[]{:S(2)}) collective-permute-start(bf16[256,128]{1,0:T(8,128)(2,1)S(1)} %get-tuple-element.47), channel_id=1, source_target_pairs={{0,4},{1,5},{2,6},{3,7},{4,8},{5,9},{6,10},{7,11},{8,12},{9,13},{1... | collective-permute-start | bytes 196616 | tf_op jit(solution)/shard_map/ppermute | solution.py:241
  65.3 12.7 %collective-permute-start.27 = (bf16[256,128]{1,0:T(8,128)(2,1)S(1)}, bf16[256,128]{1,0:T(8,128)(2,1)S(1)}, u32[]{:S(2)}, u32[]{:S(2)}) collective-permute-start(bf16[256,128]{1,0:T(8,128)(2,1)S(1)} %get-tuple-element.48), channel_id=1, source_target_pairs={{0,3},{1,0},{2,1},{3,2},{4,7},{5,4},{6,5},{7,6},{8,11},{9,8},{10,9... | collective-permute-start | bytes 196616 | tf_op jit(solution)/shard_map/ppermute | solution.py:245
  66.2 4.8 %collective-permute-start.25 = (bf16[256,128]{1,0:T(8,128)(2,1)S(1)}, bf16[256,128]{1,0:T(8,128)(2,1)S(1)}, u32[]{:S(2)}, u32[]{:S(2)}) collective-permute-start(bf16[256,128]{1,0:T(8,128)(2,1)S(1)} %get-tuple-element.48), channel_id=1, source_target_pairs={{0,1},{1,2},{2,3},{3,0},{4,5},{5,6},{6,7},{7,4},{8,9},{9,10},{10,1... | collective-permute-start | bytes 196616 | tf_op jit(solution)/shard_map/ppermute | solution.py:245
  71.0 7.0 %collective-permute-start.26 = (bf16[256,128]{1,0:T(8,128)(2,1)S(1)}, bf16[256,128]{1,0:T(8,128)(2,1)S(1)}, u32[]{:S(2)}, u32[]{:S(2)}) collective-permute-start(bf16[256,128]{1,0:T(8,128)(2,1)S(1)} %get-tuple-element.48), channel_id=1, source_target_pairs={{0,2},{1,3},{2,0},{3,1},{4,6},{5,7},{6,4},{7,5},{8,10},{9,11},{10,... | collective-permute-start | bytes 196616 | tf_op jit(solution)/shard_map/ppermute | solution.py:245
  78.0 10.0 %collective-permute-start.30 = (bf16[1024,128]{1,0:T(8,128)(2,1)S(1)}, bf16[1024,128]{1,0:T(8,128)(2,1)S(1)}, u32[]{:S(2)}, u32[]{:S(2)}) collective-permute-start(bf16[1024,128]{1,0:T(8,128)(2,1)S(1)} %constant_dynamic-update-slice_fusion.4.refs_4_), channel_id=1, source_target_pairs={{0,12},{1,13},{2,14},{3,15},{4,0},{5,1},{6,2},{7,3},{8,4},{9,5},{1... | collective-permute-start | bytes 786440 | tf_op jit(solution)/shard_map/ppermute | solution.py:241
  81.3 8.0 %collective-permute-start.29 = (bf16[1024,128]{1,0:T(8,128)(2,1)S(1)}, bf16[1024,128]{1,0:T(8,128)(2,1)S(1)}, u32[]{:S(2)}, u32[]{:S(2)}) collective-permute-start(bf16[1024,128]{1,0:T(8,128)(2,1)S(1)} %constant_dynamic-update-slice_fusion.4.refs_4_), channel_id=1, source_target_pairs={{0,8},{1,9},{2,10},{3,11},{4,12},{5,13},{6,14},{7,15},{8,0},{9,1},... | collective-permute-start | bytes 786440 | tf_op jit(solution)/shard_map/ppermute | solution.py:241
  82.4 9.7 %collective-permute-start.28 = (bf16[1024,128]{1,0:T(8,128)(2,1)S(1)}, bf16[1024,128]{1,0:T(8,128)(2,1)S(1)}, u32[]{:S(2)}, u32[]{:S(2)}) collective-permute-start(bf16[1024,128]{1,0:T(8,128)(2,1)S(1)} %constant_dynamic-update-slice_fusion.4.refs_4_), channel_id=1, source_target_pairs={{0,4},{1,5},{2,6},{3,7},{4,8},{5,9},{6,10},{7,11},{8,12},{9,13},{1... | collective-permute-start | bytes 786440 | tf_op jit(solution)/shard_map/ppermute | solution.py:241
  82.5 9.6 %collective-permute-start.24 = (bf16[1024,128]{1,0:T(8,128)(2,1)S(1)}, bf16[1024,128]{1,0:T(8,128)(2,1)S(1)}, u32[]{:S(2)}, u32[]{:S(2)}) collective-permute-start(bf16[1024,128]{1,0:T(8,128)(2,1)S(1)} %constant_dynamic-update-slice_fusion.refs_0_), channel_id=1, source_target_pairs={{0,3},{1,0},{2,1},{3,2},{4,7},{5,4},{6,5},{7,6},{8,11},{9,8},{10,9... | collective-permute-start | bytes 786440 | tf_op jit(solution)/shard_map/ppermute | solution.py:245
  83.9 8.2 %collective-permute-start.23 = (bf16[1024,128]{1,0:T(8,128)(2,1)S(1)}, bf16[1024,128]{1,0:T(8,128)(2,1)S(1)}, u32[]{:S(2)}, u32[]{:S(2)}) collective-permute-start(bf16[1024,128]{1,0:T(8,128)(2,1)S(1)} %constant_dynamic-update-slice_fusion.refs_0_), channel_id=1, source_target_pairs={{0,2},{1,3},{2,0},{3,1},{4,6},{5,7},{6,4},{7,5},{8,10},{9,11},{10,... | collective-permute-start | bytes 786440 | tf_op jit(solution)/shard_map/ppermute | solution.py:245
  88.0 6.5 %collective-permute-start.22 = (bf16[1024,128]{1,0:T(8,128)(2,1)S(1)}, bf16[1024,128]{1,0:T(8,128)(2,1)S(1)}, u32[]{:S(2)}, u32[]{:S(2)}) collective-permute-start(bf16[1024,128]{1,0:T(8,128)(2,1)S(1)} %constant_dynamic-update-slice_fusion.refs_0_), channel_id=1, source_target_pairs={{0,1},{1,2},{2,3},{3,0},{4,5},{5,6},{6,7},{7,4},{8,9},{9,10},{10,1... | collective-permute-start | bytes 786440 | tf_op jit(solution)/shard_map/ppermute | solution.py:245
  106.5 32.3 %collective-permute-start.31 = (f32[2048,128]{1,0:T(8,128)S(1)}, f32[2048,128]{1,0:T(8,128)S(1)}, u32[]{:S(2)}, u32[]{:S(2)}) collective-permute-start(f32[2048,128]{1,0:T(8,128)S(1)} %get-tuple-element.50), channel_id=1, source_target_pairs={{0,16},{16,0},{32,48},{48,32},{64,80},{80,64},{96,112},{112,96},{1... | collective-permute-start | bytes 3145736 | tf_op jit(solution)/shard_map/ppermute | solution.py:253
  107.0 2.4 %collective-permute-start.35 = (f32[128,128]{1,0:T(8,128)S(1)}, f32[128,128]{1,0:T(8,128)S(1)}, u32[]{:S(2)}, u32[]{:S(2)}) collective-permute-start(f32[128,128]{1,0:T(8,128)S(1)} %fusion.20), channel_id=1, source_target_pairs={{0,16},{16,0},{32,48},{48,32},{64,80},{80,64},{96,112},{112,96},{1... | collective-permute-start | bytes 196616 | tf_op jit(solution)/shard_map/ppermute | solution.py:253
  109.3 7.7 %collective-permute-start.38 = (f32[128,128]{1,0:T(8,128)S(1)}, f32[128,128]{1,0:T(8,128)S(1)}, u32[]{:S(2)}, u32[]{:S(2)}) collective-permute-start(f32[128,128]{1,0:T(8,128)S(1)} %add.155), channel_id=1, source_target_pairs={{0,96},{16,112},{32,0},{48,16},{64,32},{80,48},{96,64},{112,80},{1... | collective-permute-start | bytes 196616 | tf_op jit(solution)/shard_map/ppermute | solution.py:249
  112.7 6.1 %collective-permute-start.37 = (f32[128,128]{1,0:T(8,128)S(1)}, f32[128,128]{1,0:T(8,128)S(1)}, u32[]{:S(2)}, u32[]{:S(2)}) collective-permute-start(f32[128,128]{1,0:T(8,128)S(1)} %add.155), channel_id=1, source_target_pairs={{0,64},{16,80},{32,96},{48,112},{64,0},{80,16},{96,32},{112,48},{1... | collective-permute-start | bytes 196616 | tf_op jit(solution)/shard_map/ppermute | solution.py:249
  115.7 5.5 %collective-permute-start.36 = (f32[128,128]{1,0:T(8,128)S(1)}, f32[128,128]{1,0:T(8,128)S(1)}, u32[]{:S(2)}, u32[]{:S(2)}) collective-permute-start(f32[128,128]{1,0:T(8,128)S(1)} %add.155), channel_id=1, source_target_pairs={{0,32},{16,48},{32,64},{48,80},{64,96},{80,112},{96,0},{112,16},{1... | collective-permute-start | bytes 196616 | tf_op jit(solution)/shard_map/ppermute | solution.py:249
  121.2 4.6 %collective-permute-start.41 = (f32[128,128]{1,0:T(8,128)S(1)}, f32[128,128]{1,0:T(8,128)S(1)}, u32[]{:S(2)}, u32[]{:S(2)}) collective-permute-start(f32[128,128]{1,0:T(8,128)S(1)} %add_add_fusion.1), channel_id=1, source_target_pairs={{0,12},{1,13},{2,14},{3,15},{4,0},{5,1},{6,2},{7,3},{8,4},{9,5},{1... | collective-permute-start | bytes 196616 | tf_op jit(solution)/shard_map/ppermute | solution.py:241
  123.2 5.8 %collective-permute-start.40 = (f32[128,128]{1,0:T(8,128)S(1)}, f32[128,128]{1,0:T(8,128)S(1)}, u32[]{:S(2)}, u32[]{:S(2)}) collective-permute-start(f32[128,128]{1,0:T(8,128)S(1)} %add_add_fusion.1), channel_id=1, source_target_pairs={{0,8},{1,9},{2,10},{3,11},{4,12},{5,13},{6,14},{7,15},{8,0},{9,1},... | collective-permute-start | bytes 196616 | tf_op jit(solution)/shard_map/ppermute | solution.py:241
  124.5 5.5 %collective-permute-start.39 = (f32[128,128]{1,0:T(8,128)S(1)}, f32[128,128]{1,0:T(8,128)S(1)}, u32[]{:S(2)}, u32[]{:S(2)}) collective-permute-start(f32[128,128]{1,0:T(8,128)S(1)} %add_add_fusion.1), channel_id=1, source_target_pairs={{0,4},{1,5},{2,6},{3,7},{4,8},{5,9},{6,10},{7,11},{8,12},{9,13},{1... | collective-permute-start | bytes 196616 | tf_op jit(solution)/shard_map/ppermute | solution.py:241
  130.0 12.2 %collective-permute-start.44 = (f32[128,128]{1,0:T(8,128)S(1)}, f32[128,128]{1,0:T(8,128)S(1)}, u32[]{:S(2)}, u32[]{:S(2)}) collective-permute-start(f32[128,128]{1,0:T(8,128)S(1)} %add_add_fusion), channel_id=1, source_target_pairs={{0,3},{1,0},{2,1},{3,2},{4,7},{5,4},{6,5},{7,6},{8,11},{9,8},{10,9... | collective-permute-start | bytes 196616 | tf_op jit(solution)/shard_map/ppermute | solution.py:245
  132.5 10.0 %collective-permute-start.43 = (f32[128,128]{1,0:T(8,128)S(1)}, f32[128,128]{1,0:T(8,128)S(1)}, u32[]{:S(2)}, u32[]{:S(2)}) collective-permute-start(f32[128,128]{1,0:T(8,128)S(1)} %add_add_fusion), channel_id=1, source_target_pairs={{0,2},{1,3},{2,0},{3,1},{4,6},{5,7},{6,4},{7,5},{8,10},{9,11},{10,... | collective-permute-start | bytes 196616 | tf_op jit(solution)/shard_map/ppermute | solution.py:245
  136.2 6.3 %collective-permute-start.42 = (f32[128,128]{1,0:T(8,128)S(1)}, f32[128,128]{1,0:T(8,128)S(1)}, u32[]{:S(2)}, u32[]{:S(2)}) collective-permute-start(f32[128,128]{1,0:T(8,128)S(1)} %add_add_fusion), channel_id=1, source_target_pairs={{0,1},{1,2},{2,3},{3,0},{4,5},{5,6},{6,7},{7,4},{8,9},{9,10},{10,1... | collective-permute-start | bytes 196616 | tf_op jit(solution)/shard_map/ppermute | solution.py:245
  139.0 6.3 %collective-permute-start.32 = (bf16[512,128]{1,0:T(8,128)(2,1)S(1)}, bf16[512,128]{1,0:T(8,128)(2,1)S(1)}, u32[]{:S(2)}, u32[]{:S(2)}) collective-permute-start(bf16[512,128]{1,0:T(8,128)(2,1)S(1)} %get-tuple-element.52), channel_id=1, source_target_pairs={{0,32},{16,48},{32,64},{48,80},{64,96},{80,112},{96,0},{112,16},{1... | collective-permute-start | bytes 393224 | tf_op jit(solution)/shard_map/ppermute | solution.py:249
  139.6 7.0 %collective-permute-start.33 = (bf16[512,128]{1,0:T(8,128)(2,1)S(1)}, bf16[512,128]{1,0:T(8,128)(2,1)S(1)}, u32[]{:S(2)}, u32[]{:S(2)}) collective-permute-start(bf16[512,128]{1,0:T(8,128)(2,1)S(1)} %get-tuple-element.53), channel_id=1, source_target_pairs={{0,64},{16,80},{32,96},{48,112},{64,0},{80,16},{96,32},{112,48},{1... | collective-permute-start | bytes 393224 | tf_op jit(solution)/shard_map/ppermute | solution.py:249
  142.2 5.3 %collective-permute-start.34 = (bf16[512,128]{1,0:T(8,128)(2,1)S(1)}, bf16[512,128]{1,0:T(8,128)(2,1)S(1)}, u32[]{:S(2)}, u32[]{:S(2)}) collective-permute-start(bf16[512,128]{1,0:T(8,128)(2,1)S(1)} %get-tuple-element.54), channel_id=1, source_target_pairs={{0,96},{16,112},{32,0},{48,16},{64,32},{80,48},{96,64},{112,80},{1... | collective-permute-start | bytes 393224 | tf_op jit(solution)/shard_map/ppermute | solution.py:249

commit v2 on v0

v2 whole, which is shorter than its diff:
```python
import functools

import jax
import jax.numpy as jnp
from jax import lax
from jax.experimental import pallas as pl
from jax.experimental.pallas import tpu as pltpu
from jax.sharding import PartitionSpec as P

BLK = 128
NX = 4
NZ = 4
NY = 4
ROW_BLOCKS = 64
COL_BLOCKS = 32
HALF = 32
OWN = 4
UNROLL = 64
F32 = jnp.float32
BF16 = jnp.bfloat16
VMEM_LIMIT = 24 * 1024 * 1024


def vmem_specs(n):
    return [pl.BlockSpec(memory_space=pltpu.VMEM)] * n


def params():
    return pltpu.CompilerParams(vmem_limit_bytes=VMEM_LIMIT)


def accumulate(live, codes_ref, acc, product):
    @pl.loop(0, pl.cdiv(live, UNROLL))
    def _(g):
        codes = [codes_ref[g * UNROLL + j] for j in range(UNROLL)]
        prods = [product(c & 511, c >> 16) for c in codes]
        for j in range(UNROLL):
            acc[(codes[j] >> 9) & 127] += prods[j]


def sparse_cost():
    return pl.CostEstimate(flops=512 * BLK**3 * 4, bytes_accessed=10 * 2**20, transcendentals=0)


def load_kernel(adj_ref, out_ref, sem):
    copy = pltpu.make_async_copy(adj_ref, out_ref, sem)
    copy.start()
    copy.wait()


def load(adjacency):
    return pl.pallas_call(
        load_kernel,
        out_shape=jax.ShapeDtypeStruct(adjacency.shape, adjacency.dtype),
        in_specs=[pl.BlockSpec(memory_space=pl.ANY)],
        out_specs=pl.BlockSpec(memory_space=pltpu.VMEM),
        scratch_shapes=[pltpu.SemaphoreType.DMA],
        compiler_params=params(),
        cost_estimate=pl.CostEstimate(flops=0, bytes_accessed=2 * adjacency.size * 2, transcendentals=0),
        name="load_blocks",
    )(adjacency)


def forward_kernel(nin, codes_ref, count_ref, adj_ref, *refs):
    ins, outs = refs[:nin], refs[nin:-2]
    feats, acc = refs[-2:]
    per = feats.shape[0] // nin
    for i in range(nin):
        feats[pl.ds(i * per, per)] = ins[i][...].reshape(per, BLK, BLK)
    acc[...] = jnp.zeros_like(acc)

    def product(slot, source):
        return jnp.dot(adj_ref[slot], feats[source], preferred_element_type=F32)

    accumulate(count_ref[0], codes_ref, acc, product)
    at = 0
    for out in outs:
        blocks = out.shape[0] // BLK
        out[...] = acc[pl.ds(at, blocks)].reshape(out.shape).astype(out.dtype)
        at += blocks


def forward(adjacency, codes, count, pieces, outs, name):
    return pl.pallas_call(
        functools.partial(forward_kernel, len(pieces)),
        out_shape=[jax.ShapeDtypeStruct((units * OWN * BLK, BLK), dtype) for units, dtype in outs],
        in_specs=[pl.BlockSpec(memory_space=pltpu.SMEM)] * 2 + vmem_specs(1 + len(pieces)),
        out_specs=vmem_specs(len(outs)),
        scratch_shapes=[
            pltpu.VMEM((COL_BLOCKS, BLK, BLK), BF16),
            pltpu.VMEM((HALF + 1, BLK, BLK), F32),
        ],
        compiler_params=params(),
        cost_estimate=sparse_cost(),
        name=name,
    )(codes, count, adjacency, *pieces)


def gather_slopes(slopes, ins):
    at = 0
    for part in ins:
        blocks = part.shape[0] // BLK - 1
        slopes[pl.ds(at, blocks)] = part[pl.ds(0, blocks * BLK)].reshape(blocks, BLK, BLK)
        at += blocks


def last_block(part):
    return part[pl.ds(part.shape[0] - BLK, BLK)].astype(F32)


def backward_even_kernel(nin, codes_ref, count_ref, adj_ref, *refs):
    ins, (acc, wsum) = refs[:nin], refs[nin : nin + 2]
    slopes = refs[-1]
    gather_slopes(slopes, ins)
    acc[...] = jnp.zeros_like(acc)

    def product(slot, source):
        return jnp.dot(slopes[source], adj_ref[slot], preferred_element_type=F32)

    accumulate(count_ref[0], codes_ref, acc, product)
    wsum[...] = sum(last_block(part) for part in ins)


def backward_even(adjacency, codes, count, pieces):
    return pl.pallas_call(
        functools.partial(backward_even_kernel, len(pieces)),
        out_shape=[
            jax.ShapeDtypeStruct((COL_BLOCKS + 1, BLK, BLK), F32),
            jax.ShapeDtypeStruct((BLK, BLK), F32),
        ],
        in_specs=[pl.BlockSpec(memory_space=pltpu.SMEM)] * 2 + vmem_specs(1 + len(pieces)),
        out_specs=vmem_specs(2),
        scratch_shapes=[pltpu.VMEM((HALF, BLK, BLK), BF16)],
        compiler_params=params(),
        cost_estimate=sparse_cost(),
        name="backward_even",
    )(codes, count, adjacency, *pieces)


def backward_odd_kernel(nin, codes_ref, count_ref, adj_ref, part_ref, wpart_ref, *refs):
    ins, (keep, send, wsum) = refs[:nin], refs[nin : nin + 3]
    slopes, acc = refs[nin + 3 :]
    gather_slopes(slopes, ins)
    acc[...] = part_ref[...]

    def product(slot, source):
        return jnp.dot(slopes[source], adj_ref[slot], preferred_element_type=F32)

    accumulate(count_ref[0], codes_ref, acc, product)
    half = COL_BLOCKS // 2
    for b in range(half):
        keep[pl.ds(b * BLK, BLK)] = acc[b].T.astype(keep.dtype)
        send[pl.ds(b * BLK, BLK)] = acc[half + b].T.astype(send.dtype)
    total = wpart_ref[...] + sum(last_block(part) for part in ins)
    wsum[...] = total
    send[pl.ds(half * BLK, BLK)] = total.astype(send.dtype)


def backward_odd(adjacency, codes, count, part, wpart, pieces):
    rows = COL_BLOCKS * BLK // 2
    return pl.pallas_call(
        functools.partial(backward_odd_kernel, len(pieces)),
        out_shape=[
            jax.ShapeDtypeStruct((rows, BLK), F32),
            jax.ShapeDtypeStruct((rows + BLK, BLK), F32),
            jax.ShapeDtypeStruct((BLK, BLK), F32),
        ],
        in_specs=[pl.BlockSpec(memory_space=pltpu.SMEM)] * 2 + vmem_specs(3 + len(pieces)),
        out_specs=vmem_specs(3),
        scratch_shapes=[
            pltpu.VMEM((HALF, BLK, BLK), BF16),
            pltpu.VMEM((COL_BLOCKS + 1, BLK, BLK), F32),
        ],
        compiler_params=params(),
        cost_estimate=sparse_cost(),
        name="backward_odd",
    )(codes, count, adjacency, part, wpart, *pieces)


def add_split_kernel(nin, *refs):
    ins, outs = refs[:nin], refs[nin:]
    at = 0
    for out in outs:
        rows = out.shape[0]
        total = ins[0][pl.ds(at, rows)].astype(F32)
        for part in ins[1:]:
            total += part[pl.ds(at, rows)].astype(F32)
        out[...] = total.astype(out.dtype)
        at += rows


def add_split(parts, dtypes, name):
    rows = parts[0].shape[0] // len(dtypes)
    return pl.pallas_call(
        functools.partial(add_split_kernel, len(parts)),
        out_shape=[jax.ShapeDtypeStruct((rows, BLK), dtype) for dtype in dtypes],
        in_specs=vmem_specs(len(parts)),
        out_specs=vmem_specs(len(dtypes)),
        compiler_params=params(),
        name=name,
    )(*parts)


def activate_kernel(weight_ref, grad_ref, *refs):
    parts, (act_ref, pay_ref) = refs[:-2], refs[-2:]
    rows = act_ref.shape[0]
    total = parts[0][...]
    for part in parts[1:]:
        total += part[...].astype(F32)
    weight = weight_ref[...].astype(F32)
    pre = jnp.dot(total, weight, precision=lax.Precision.HIGHEST, preferred_element_type=F32)
    squash = jnp.tanh(pre)
    act_ref[...] = squash.astype(BF16)
    slope = (grad_ref[...].astype(F32) * (1.0 - squash * squash)).astype(BF16)
    high = total.astype(BF16)
    low = (total - high.astype(F32)).astype(BF16)
    wterm = jnp.zeros((BLK, BLK), F32)
    for b in range(0, rows, BLK):
        turned = slope[b : b + BLK].T
        pay_ref[pl.ds(b, BLK)] = turned
        wterm += jnp.dot(turned, high[b : b + BLK], preferred_element_type=F32)
        wterm += jnp.dot(turned, low[b : b + BLK], preferred_element_type=F32)
    pay_ref[pl.ds(rows, BLK)] = wterm.astype(BF16)


def activate(weight, grad_out, parts):
    rows = grad_out.shape[0]
    return pl.pallas_call(
        activate_kernel,
        out_shape=[
            jax.ShapeDtypeStruct((rows, BLK), BF16),
            jax.ShapeDtypeStruct((rows + BLK, BLK), BF16),
        ],
        in_specs=vmem_specs(2 + len(parts)),
        out_specs=vmem_specs(2),
        compiler_params=params(),
        name="activate",
    )(weight, grad_out, *parts)


def merge_kernel(*refs):
    parts, out = refs[:-1], refs[-1]
    rows = parts[0].shape[0] - BLK
    total = jnp.zeros((BLK, BLK), F32)
    for i, part in enumerate(parts):
        out[pl.ds(i * rows, rows)] = part[pl.ds(0, rows)]
        total += last_block(part)
    out[pl.ds(len(parts) * rows, BLK)] = total.astype(BF16)


def merge(parts, name):
    rows = len(parts) * (parts[0].shape[0] - BLK) + BLK
    return pl.pallas_call(
        merge_kernel,
        out_shape=jax.ShapeDtypeStruct((rows, BLK), BF16),
        in_specs=vmem_specs(len(parts)),
        out_specs=pl.BlockSpec(memory_space=pltpu.VMEM),
        compiler_params=params(),
        name=name,
    )(*parts)


def add_core_kernel(nout, keep, wkeep, got, *outs):
    rows = keep.shape[0] // nout
    wsum = wkeep[...] + got[pl.ds(rows * nout, BLK)].astype(F32)
    outs[nout][...] = wsum
    for i in range(nout):
        total = keep[pl.ds(i * rows, rows)] + got[pl.ds(i * rows, rows)].astype(F32)
        outs[i][pl.ds(0, rows)] = total.astype(outs[i].dtype)
        if i:
            outs[i][pl.ds(rows, BLK)] = wsum.astype(outs[i].dtype)


def add_core(keep, wkeep, got):
    rows = keep.shape[0] // NY
    return pl.pallas_call(
        functools.partial(add_core_kernel, NY),
        out_shape=[jax.ShapeDtypeStruct((rows, BLK), F32)]
        + [jax.ShapeDtypeStruct((rows + BLK, BLK), BF16)] * (NY - 1)
        + [jax.ShapeDtypeStruct((BLK, BLK), F32)],
        in_specs=vmem_specs(3),
        out_specs=vmem_specs(NY + 1),
        compiler_params=params(),
        name="add_core",
    )(keep, wkeep, got)


def finish_kernel(scale, weight_ref, own, wown, *refs):
    parts, (out_ref, wout_ref) = refs[:-2], refs[-2:]
    rows = own.shape[0]
    total, wsum = own[...], wown[...]
    for part in parts:
        total += part[pl.ds(0, rows)].astype(F32)
        wsum += part[pl.ds(rows, BLK)].astype(F32)
    out_ref[...] = lax.dot_general(
        total.astype(BF16), weight_ref[...], (((1,), (1,)), ((), ())), preferred_element_type=F32
    ).astype(BF16)
    wout_ref[...] = wsum.T * scale


def finish(scale, weight, own, wown, parts):
    return pl.pallas_call(
        functools.partial(finish_kernel, scale),
        out_shape=[
            jax.ShapeDtypeStruct(own.shape, BF16),
            jax.ShapeDtypeStruct((BLK, BLK), F32),
        ],
        in_specs=vmem_specs(3 + len(parts)),
        out_specs=vmem_specs(2),
        compiler_params=params(),
        name="finish",
    )(weight, own, wown, *parts)


def shift_x(a, d):
    return lax.ppermute(a, "col", [(i, (i // NZ + d) % NX * NZ + i % NZ) for i in range(NX * NZ)])


def shift_z(a, d):
    return lax.ppermute(a, "col", [(i, i // NZ * NZ + (i % NZ + d) % NZ) for i in range(NX * NZ)])


def shift_y(a, d):
    return lax.ppermute(a, "row", [(i, (i // 2 + d) % NY * 2 + i % 2) for i in range(NY * 2)])


def swap_core(a):
    return lax.ppermute(a, "row", [(i, i ^ 1) for i in range(NY * 2)])


def order_slots(slots, odd, even, forward_code, backward_code, idle_forward, idle_backward):
    before = slots[:, None] >= slots[None, :]
    rank_odd = jnp.sum(before & odd[None, :], axis=1, dtype=jnp.int32) - 1
    rank_even = jnp.sum(before & even[None, :], axis=1, dtype=jnp.int32) - 1
    lists = []
    for chosen, rank in ((odd, rank_odd), (even, rank_even)):
        here = (slots[:, None] == rank[None, :]) & chosen[None, :]
        count = jnp.sum(chosen, dtype=jnp.int32)
        lists.append(count[None])
        for code, idle in ((forward_code, idle_forward), (backward_code, idle_backward)):
            picked = jnp.sum(jnp.where(here, code[None, :], 0), axis=1, dtype=jnp.int32)
            lists.append(jnp.where(slots < count, picked, idle))
    return lists


def local(features, weight, adjacency, row_index, col_index, block_count, grad_out):
    row, col = lax.axis_index("row"), lax.axis_index("col")
    y, core = row // 2, row % 2
    x, z = col // NZ, col % NZ
    capacity = adjacency.shape[2]
    slots = jnp.arange(capacity, dtype=jnp.int32)
    alive = slots < block_count[0, 0]
    brow, bcol = row_index[0, 0], col_index[0, 0]

    mine = [features] + [shift_y(features, d) for d in range(1, NY)]
    theirs = [swap_core(a) for a in mine]
    blocks = load(adjacency[0, 0])

    rx, rz, rb = brow // 16, brow // 4 % 4, brow % 4
    cy, cc, cb = bcol // 8, bcol // 4 % 2, bcol % 4
    odd = alive & ((rx - x) % 2 == 1)
    even = alive & ((rx - x) % 2 == 0)
    to_row = (rx - x) % NX // 2 * 16 + (rz - z) % NZ * OWN + rb
    from_row = (x - rx) % NX // 2 * 16 + (z - rz) % NZ * OWN + rb
    to_col = (cc ^ core) * 16 + (cy - y) % NY * OWN + cb
    from_col = (cc ^ core) * 16 + (y - cy) % NY * OWN + cb
    n_odd, odd_forward, odd_backward, n_even, even_forward, even_backward = order_slots(
        slots,
        odd,
        even,
        slots + 512 * to_row + 65536 * from_col,
        slots + 512 * to_col + 65536 * from_row,
        512 * HALF,
        512 * COL_BLOCKS,
    )

    x1, x3 = forward(blocks, odd_forward, n_odd, mine + theirs, [(4, BF16)] * 2, "forward_odd")
    column, across, z1, z2, z3 = forward(
        blocks, even_forward, n_even, mine + theirs, [(4, F32), (1, F32)] + [(1, BF16)] * 3, "forward_even"
    )
    x1, x3 = shift_x(x1, 1), shift_x(x3, 3)
    z1, z2, z3 = shift_z(z1, 1), shift_z(z2, 2), shift_z(z3, 3)
    across = add_split([across, z1, z2, z3], [BF16], "add_z")[0]
    own, z1, z2, z3 = add_split([column, x1, x3], [F32, BF16, BF16, BF16], "add_x")
    parts = [own, shift_z(z1, 1), shift_z(z2, 2), shift_z(z3, 3), shift_x(across, 2)]
    activated, pay = activate(weight, grad_out, parts)

    beside = [shift_z(pay, d) for d in range(1, NZ)]
    across = shift_x(pay, 2)
    column = merge([pay] + beside, "merge_z")
    odds = [shift_x(column, 1), shift_x(column, 3)]
    evens = [column, across] + [shift_z(across, d) for d in range(1, NZ)]

    part, wpart = backward_even(blocks, even_backward, n_even, evens)
    keep, send, wkeep = backward_odd(blocks, odd_backward, n_odd, part, wpart, odds)
    parts = add_core(keep, wkeep, swap_core(send))
    got = [shift_y(parts[d], d) for d in range(1, NY)]
    nodes_all = features.shape[0] * lax.axis_size("row") * lax.axis_size("col")
    input_grad, weight_grad = finish(nodes_all ** (-0.5), weight, parts[0], parts[NY], got)
    return (activated, input_grad, weight_grad)


def solution(mesh):
    placed = (
        P(("col", "row"), None),
        P(),
        P("row", "col", None, None, None),
        P("row", "col", None),
        P("row", "col", None),
        P("row", "col"),
        P(("row", "col"), None),
    )
    return jax.shard_map(
        local,
        mesh=mesh,
        in_specs=placed,
        out_specs=(P(("row", "col"), None), P(("col", "row"), None), P()),
        check_vma=False,
    )
```

time: 512 us -> 108 us (0.21)
  waiting for transfers between devices: 322 us -> 30.7 us
  matrix products: 143 us -> 0 us
  starting transfers between devices: 0.2 us -> 41.7 us
  local copies, waits for them, and re-layouts: 29 us -> 0.02 us
  Pallas kernels: 0 us -> 28.6 us
  between operations: 14.5 us -> 1.49 us
    dot_general x9 -> x0, matrix products: 143 us -> none  [the longest x2 77.8 us: add_blocks(): jnp.dot(selector, flat, precision=lax.Precision.HIGHEST, preferred_elemen...]
    psum x1 -> x0, waiting for transfers between devices: 142 us -> none  [local(): weight_grad = lax.psum(weight_term, ('row', 'col')) * nodes_all ** (-0.5)]
    reduce_scatter x2 -> x0, waiting for transfers between devices: 107 us -> none  [the longest x1 75.7 us: local(): pre = lax.psum_scatter(partial_rows, 'col', scatter_dimension=0, tiled=True)]
    all_gather x2 -> x0, waiting for transfers between devices: 73.2 us -> none  [the longest x1 46.3 us: local(): slope_all = lax.all_gather(slope, 'col', axis=0, tiled=True)]
    ppermute x0 -> x29, starting transfers between devices: none -> 41.7 us  [the longest x12 16.2 us: shift_z(): lax.ppermute(a, 'col', [(i, i // NZ * NZ + (i % NZ + d) % NZ) for i in ra...]
    ppermute x0 -> x29, waiting for transfers between devices: none -> 30.7 us  [the longest x12 21 us: shift_z(): lax.ppermute(a, 'col', [(i, i // NZ * NZ + (i % NZ + d) % NZ) for i in ra...]
    pallas_call x0 -> x11, Pallas kernels: none -> 28.6 us  [the longest x2 9.86 us: forward(): pl.pallas_call(functools.partial(forward_kernel, len(pieces)), out_shape=...]
    unnamed x13 -> x6, local copies, waits for them, and re-layouts: 18.3 us -> 0.02 us
  transfers between devices with their start and end apart: 5 -> 29, of which waited for: 5 -> 13; matrix products, arithmetic and copies ran while one was open for 0% -> 5% of each run, Pallas kernels for 0% -> 15%
where the time goes in v2:
time: 108 us
  starting transfers between devices  41.7 us (39%)
  waiting for transfers between devices  30.7 us (28%)
  Pallas kernels  28.6 us (26%)
  other arithmetic  5.65 us (5%)
  between operations  1.49 us (1%)
    ppermute x12, waiting for transfers between devices, shift_z(): lax.ppermute(a, 'col', [(i, i // NZ * NZ + (i % NZ + d) % NZ) for i in ra...  21 us
    ppermute x12, starting transfers between devices, shift_z(): lax.ppermute(a, 'col', [(i, i // NZ * NZ + (i % NZ + d) % NZ) for i in ra...  16.2 us
    ppermute x6, starting transfers between devices, shift_y(): lax.ppermute(a, 'row', [(i, (i // 2 + d) % NY * 2 + i % 2) for i in range...  10.7 us
    pallas_call x2, Pallas kernels, forward(): pl.pallas_call(functools.partial(forward_kernel, len(pieces)), out_shape=...  9.86 us
    ppermute x6, starting transfers between devices, shift_x(): lax.ppermute(a, 'col', [(i, (i // NZ + d) % NX * NZ + i % NZ) for i in ra...  8.99 us
    ppermute x6, waiting for transfers between devices, shift_y(): lax.ppermute(a, 'row', [(i, (i // 2 + d) % NY * 2 + i % 2) for i in range...  7.3 us
    ppermute x5, starting transfers between devices, swap_core(): return lax.ppermute(a, 'row', [(i, i ^ 1) for i in range(NY * 2)])  5.85 us
    pallas_call x1, Pallas kernels, load(): pl.pallas_call(load_kernel, out_shape=jax.ShapeDtypeStruct(adjacency.shap...  5.82 us
  transfers between devices with their start and end apart: 29, of which 13 were waited for; matrix products, arithmetic and copies ran while one was open for 5% of the time, Pallas kernels for 15%

profile of v2, /device:TPU:1, one launch (start us, length us, event | category | flops | bytes accessed | tf_op | source)
XLA Modules:
  0.0 108.1 jit_solution(17223025123968819235)
XLA Ops:
  0.6 1.5 %collective-permute-start.3 = (bf16[512,128]{1,0:T(8,128)(2,1)}, bf16[512,128]{1,0:T(8,128)(2,1)S(1)}, u32[]{:S(2)}, u32[]{:S(2)}) collective-permute-start(bf16[512,128]{1,0:T(8,128)(2,1)} %refs_0_.3), channel_id=1, source_target_pairs={{0,16},{16,0},{32,48},{48,32},{64,80},{80,64},{96,112},{112,96},{1... | collective-permute-start | bytes 393224 | tf_op jit(solution)/shard_map/ppermute | solution.py:328
  2.1 2.8 %collective-permute-start.2 = (bf16[512,128]{1,0:T(8,128)(2,1)}, bf16[512,128]{1,0:T(8,128)(2,1)S(1)}, u32[]{:S(2)}, u32[]{:S(2)}) collective-permute-start(bf16[512,128]{1,0:T(8,128)(2,1)} %refs_0_.3), channel_id=1, source_target_pairs={{0,96},{16,112},{32,0},{48,16},{64,32},{80,48},{96,64},{112,80},{1... | collective-permute-start | bytes 393224 | tf_op jit(solution)/shard_map/ppermute | solution.py:324
  5.0 0.3 collective-permute-start.1
  5.3 0.7 collective-permute-start
  6.7 1.4 %fusion.11 = (s32[512]{0:T(512)S(1)}, s32[512]{0:T(512)S(1)}, s32[]{:T(128)}, pred[512]{0:T(512)(128)(4,1)S(1)}, s32[512]{0:T(512)S(1)}) fusion(s32[]{:T(128)S(6)} %select_n.226, s32[]{:T(128)S(6)} %select_n.220, s32[]{:T(128)S(6)} %select_n.214, s32[512]{0:T(512)} %bitcast.9, s32[512]{0:T(512)} %bitcast.10, s32[]{:T(128)S(6)} %select_n.225, s32[]{:T(128)} %bitcast.7), kind=kLoop, calls=%fused_computation.70 | loop fusion | flops 112127 | bytes 10776 | tf_op jit(solution)/shard_map/add | solution.py:371
  8.0 0.6 convert_reduce_fusion.3
  8.7 0.1 convert_reduce_fusion.1
  8.8 0.1 convert_reduce_fusion
  9.0 0.0 copy-start
  9.0 5.8 %load_blocks.1.adj_ref = bf16[512,128,128]{2,1,0:T(8,128)(2,1)S(1)} custom-call(bf16[512,128,128]{2,1,0:T(8,128)(2,1)} %bitcast.8), custom_call_target="tpu_custom_call" | custom-call | bytes 33554432 | tf_op jit(solution)/shard_map/load_blocks/pallas_call | solution.py:52
  14.8 0.9 select_reduce_fusion.1
  15.8 0.0 collective-permute-done.2.refs_3_
  15.8 1.0 collective-permute-start.6
  16.8 0.0 collective-permute-done.1.refs_2_
  16.8 0.1 collective-permute-start.5
  16.9 0.0 collective-permute-done.refs_1_
  16.9 0.4 collective-permute-start.4
  17.3 1.2 %fusion.40 = (s32[512]{0:T(512)S(1)}, s32[512]{0:T(512)S(1)}) fusion(s32[512]{0:T(512)S(1)} %get-tuple-element.56, s32[]{:T(128)} %get-tuple-element.66, s32[512]{0:T(512)S(1)} %get-tuple-element.57, s32[]{:T(128)} %get-tuple-element.62), kind=kLoop, calls=%fused_computation.102 | loop fusion | flops 2048 | bytes 8200 | tf_op jit(solution)/shard_map/jit(_where)/select_n | solution.py:342
  18.5 5.0 %forward_odd.1 = (bf16[2048,128]{1,0:T(8,128)(2,1)S(1)}, bf16[2048,128]{1,0:T(8,128)(2,1)S(1)}) custom-call(s32[512]{0:T(512)S(1)} %get-tuple-element.69.codes_ref, s32[1]{0:T(128)} %bitcast.5.count_ref, bf16[512,128,128]{2,1,0:T(8,128)(2,1)S(1)} %load_blocks.1.adj_ref, bf16[512,128]{1,0:T(8,128)(2,1)S(1)} %copy-done, ...), custom_call_target="tpu_custom_call" | custom-call | flops 4294967296 | bytes 10485760 | tf_op jit(solution)/shard_map/forward_odd/pallas_call | solution.py:84
  23.5 0.4 collective-permute-start.7
  23.9 2.3 %collective-permute-start.8 = (bf16[2048,128]{1,0:T(8,128)(2,1)S(1)}, bf16[2048,128]{1,0:T(8,128)(2,1)S(1)}, u32[]{:S(2)}, u32[]{:S(2)}) collective-permute-start(bf16[2048,128]{1,0:T(8,128)(2,1)S(1)} %get-tuple-element.30), channel_id=1, source_target_pairs={{0,12},{1,13},{2,14},{3,15},{4,0},{5,1},{6,2},{7,3},{8,4},{9,5},{1... | collective-permute-start | bytes 1572872 | tf_op jit(solution)/shard_map/ppermute | solution.py:316
  26.3 4.9 %forward_even.1 = (f32[2048,128]{1,0:T(8,128)S(1)}, f32[512,128]{1,0:T(8,128)S(1)}, bf16[512,128]{1,0:T(8,128)(2,1)S(1)}, bf16[512,128]{1,0:T(8,128)(2,1)S(1)}, bf16[512,128]{1,0:T(8,128)(2,1)S(1)}) custom-call(s32[512]{0:T(512)S(1)} %get-tuple-element.70.codes_ref, s32[1]{0:T(128)} %bitcast.3.count_ref, bf16[512,128,128]{2,1,0:T(8,128)(2,1)S(1)} %load_blocks.1.adj_ref, ...), custom_call_target="tpu_custom_call" | custom-call | flops 4294967296 | bytes 10485760 | tf_op jit(solution)/shard_map/forward_even/pallas_call | solution.py:84
  31.2 0.0 copy-start.1
  31.2 0.0 copy-start.2
  31.2 0.8 collective-permute-start.12
  32.0 2.4 %collective-permute-start.13 = (bf16[512,128]{1,0:T(8,128)(2,1)S(1)}, bf16[512,128]{1,0:T(8,128)(2,1)S(1)}, u32[]{:S(2)}, u32[]{:S(2)}) collective-permute-start(bf16[512,128]{1,0:T(8,128)(2,1)S(1)} %get-tuple-element.37), channel_id=1, source_target_pairs={{0,2},{1,3},{2,0},{3,1},{4,6},{5,7},{6,4},{7,5},{8,10},{9,11},{10,... | collective-permute-start | bytes 393224 | tf_op jit(solution)/shard_map/ppermute | solution.py:320
  34.5 0.7 collective-permute-start.14
  35.2 1.4 %collective-permute-done.12.refs_1_ = bf16[512,128]{1,0:T(8,128)(2,1)S(1)} collective-permute-done((bf16[512,128]{1,0:T(8,128)(2,1)S(1)}, bf16[512,128]{1,0:T(8,128)(2,1)S(1)}, u32[]{:S(2)}, u32[]{:S(2)}) %collective-permute-start.12) | collective-permute-done | bytes 131104 | tf_op jit(solution)/shard_map/ppermute | solution.py:320
  36.6 1.7 %collective-permute-done.13.refs_2_ = bf16[512,128]{1,0:T(8,128)(2,1)S(1)} collective-permute-done((bf16[512,128]{1,0:T(8,128)(2,1)S(1)}, bf16[512,128]{1,0:T(8,128)(2,1)S(1)}, u32[]{:S(2)}, u32[]{:S(2)}) %collective-permute-start.13) | collective-permute-done | bytes 131104 | tf_op jit(solution)/shard_map/ppermute | solution.py:320
  38.3 0.8 collective-permute-done.14.refs_3_
  39.1 0.1 add_z.1
  39.2 2.0 %collective-permute-start.15 = (bf16[512,128]{1,0:T(8,128)(2,1)S(1)}, bf16[512,128]{1,0:T(8,128)(2,1)S(1)}, u32[]{:S(2)}, u32[]{:S(2)}) collective-permute-start(bf16[512,128]{1,0:T(8,128)(2,1)S(1)} %add_z.1), channel_id=1, source_target_pairs={{0,8},{1,9},{2,10},{3,11},{4,12},{5,13},{6,14},{7,15},{8,0},{9,1},... | collective-permute-start | bytes 393224 | tf_op jit(solution)/shard_map/ppermute | solution.py:316
  41.2 0.2 add_x.1
  41.4 2.7 %collective-permute-start.9 = (bf16[512,128]{1,0:T(8,128)(2,1)S(1)}, bf16[512,128]{1,0:T(8,128)(2,1)S(1)}, u32[]{:S(2)}, u32[]{:S(2)}) collective-permute-start(bf16[512,128]{1,0:T(8,128)(2,1)S(1)} %get-tuple-element.32), channel_id=1, source_target_pairs={{0,1},{1,2},{2,3},{3,0},{4,5},{5,6},{6,7},{7,4},{8,9},{9,10},{10,1... | collective-permute-start | bytes 393224 | tf_op jit(solution)/shard_map/ppermute | solution.py:320
  44.0 2.1 %collective-permute-start.10 = (bf16[512,128]{1,0:T(8,128)(2,1)S(1)}, bf16[512,128]{1,0:T(8,128)(2,1)S(1)}, u32[]{:S(2)}, u32[]{:S(2)}) collective-permute-start(bf16[512,128]{1,0:T(8,128)(2,1)S(1)} %get-tuple-element.33), channel_id=1, source_target_pairs={{0,2},{1,3},{2,0},{3,1},{4,6},{5,7},{6,4},{7,5},{8,10},{9,11},{10,... | collective-permute-start | bytes 393224 | tf_op jit(solution)/shard_map/ppermute | solution.py:320
  46.2 1.7 %collective-permute-start.11 = (bf16[512,128]{1,0:T(8,128)(2,1)S(1)}, bf16[512,128]{1,0:T(8,128)(2,1)S(1)}, u32[]{:S(2)}, u32[]{:S(2)}) collective-permute-start(bf16[512,128]{1,0:T(8,128)(2,1)S(1)} %get-tuple-element.34), channel_id=1, source_target_pairs={{0,3},{1,0},{2,1},{3,2},{4,7},{5,4},{6,5},{7,6},{8,11},{9,8},{10,9... | collective-permute-start | bytes 393224 | tf_op jit(solution)/shard_map/ppermute | solution.py:320
  47.9 2.5 %collective-permute-done.10.refs_2_ = bf16[512,128]{1,0:T(8,128)(2,1)S(1)} collective-permute-done((bf16[512,128]{1,0:T(8,128)(2,1)S(1)}, bf16[512,128]{1,0:T(8,128)(2,1)S(1)}, u32[]{:S(2)}, u32[]{:S(2)}) %collective-permute-start.10) | collective-permute-done | bytes 131104 | tf_op jit(solution)/shard_map/ppermute | solution.py:320
  50.4 1.2 %collective-permute-done.11.refs_3_ = bf16[512,128]{1,0:T(8,128)(2,1)S(1)} collective-permute-done((bf16[512,128]{1,0:T(8,128)(2,1)S(1)}, bf16[512,128]{1,0:T(8,128)(2,1)S(1)}, u32[]{:S(2)}, u32[]{:S(2)}) %collective-permute-start.11) | collective-permute-done | bytes 131104 | tf_op jit(solution)/shard_map/ppermute | solution.py:320
  51.6 1.1 %activate.1 = (bf16[512,128]{1,0:T(8,128)(2,1)}, bf16[640,128]{1,0:T(8,128)(2,1)S(1)}) custom-call(bf16[128,128]{1,0:T(8,128)(2,1)S(1)} %copy-done.2, bf16[512,128]{1,0:T(8,128)(2,1)S(1)} %copy-done.1, f32[512,128]{1,0:T(8,128)S(1)} %get-tuple-element.31.refs_0_, bf16[512,128]{1,0:T(8,128)(2,1)S(1)} %collective-permute-done.9.refs_1_, ...), custom_call_target="tpu_custom_call" | custom-call | tf_op jit(solution)/shard_map/activate/pallas_call | solution.py:228
  52.7 3.6 %collective-permute-start.18 = (bf16[640,128]{1,0:T(8,128)(2,1)S(1)}, bf16[640,128]{1,0:T(8,128)(2,1)S(1)}, u32[]{:S(2)}, u32[]{:S(2)}) collective-permute-start(bf16[640,128]{1,0:T(8,128)(2,1)S(1)} %get-tuple-element.40.refs_0_), channel_id=1, source_target_pairs={{0,3},{1,0},{2,1},{3,2},{4,7},{5,4},{6,5},{7,6},{8,11},{9,8},{10,9... | collective-permute-start | bytes 491528 | tf_op jit(solution)/shard_map/ppermute | solution.py:320
  56.2 0.6 collective-permute-start.16
  56.8 0.6 fusion.39.codes_ref
  57.4 5.3 %collective-permute-done.18.refs_3_ = bf16[640,128]{1,0:T(8,128)(2,1)S(1)} collective-permute-done((bf16[640,128]{1,0:T(8,128)(2,1)S(1)}, bf16[640,128]{1,0:T(8,128)(2,1)S(1)}, u32[]{:S(2)}, u32[]{:S(2)}) %collective-permute-start.18) | collective-permute-done | bytes 163872 | tf_op jit(solution)/shard_map/ppermute | solution.py:320
  62.7 1.3 %collective-permute-done.16.refs_1_ = bf16[640,128]{1,0:T(8,128)(2,1)S(1)} collective-permute-done((bf16[640,128]{1,0:T(8,128)(2,1)S(1)}, bf16[640,128]{1,0:T(8,128)(2,1)S(1)}, u32[]{:S(2)}, u32[]{:S(2)}) %collective-permute-start.16) | collective-permute-done | bytes 163872 | tf_op jit(solution)/shard_map/ppermute | solution.py:320
  64.0 0.1 merge_z.1.refs_0_
  64.1 3.2 %collective-permute-start.24 = (bf16[2176,128]{1,0:T(8,128)(2,1)S(1)}, bf16[2176,128]{1,0:T(8,128)(2,1)S(1)}, u32[]{:S(2)}, u32[]{:S(2)}) collective-permute-start(bf16[2176,128]{1,0:T(8,128)(2,1)S(1)} %merge_z.1.refs_0_), channel_id=1, source_target_pairs={{0,12},{1,13},{2,14},{3,15},{4,0},{5,1},{6,2},{7,3},{8,4},{9,5},{1... | collective-permute-start | bytes 1671176 | tf_op jit(solution)/shard_map/ppermute | solution.py:316
  67.3 1.0 collective-permute-start.23
  68.4 0.5 collective-permute-start.21
  68.8 1.0 collective-permute-start.20
  69.8 0.6 fusion.43.codes_ref
  70.4 2.4 %collective-permute-done.22.refs_4_ = bf16[640,128]{1,0:T(8,128)(2,1)S(1)} collective-permute-done((bf16[640,128]{1,0:T(8,128)(2,1)S(1)}, bf16[640,128]{1,0:T(8,128)(2,1)S(1)}, u32[]{:S(2)}, u32[]{:S(2)}) %collective-permute-start.22) | collective-permute-done | bytes 163872 | tf_op jit(solution)/shard_map/ppermute | solution.py:320
  72.8 1.3 %collective-permute-done.21.refs_3_ = bf16[640,128]{1,0:T(8,128)(2,1)S(1)} collective-permute-done((bf16[640,128]{1,0:T(8,128)(2,1)S(1)}, bf16[640,128]{1,0:T(8,128)(2,1)S(1)}, u32[]{:S(2)}, u32[]{:S(2)}) %collective-permute-start.21) | collective-permute-done | bytes 163872 | tf_op jit(solution)/shard_map/ppermute | solution.py:320
  74.1 3.1 %collective-permute-done.20.refs_2_ = bf16[640,128]{1,0:T(8,128)(2,1)S(1)} collective-permute-done((bf16[640,128]{1,0:T(8,128)(2,1)S(1)}, bf16[640,128]{1,0:T(8,128)(2,1)S(1)}, u32[]{:S(2)}, u32[]{:S(2)}) %collective-permute-start.20) | collective-permute-done | bytes 163872 | tf_op jit(solution)/shard_map/ppermute | solution.py:320
  77.2 4.9 %backward_even.1 = (f32[33,128,128]{2,1,0:T(8,128)S(1)}, f32[128,128]{1,0:T(8,128)S(1)}) custom-call(s32[512]{0:T(512)S(1)} %fusion.43.codes_ref, s32[1]{0:T(128)} %bitcast.3.count_ref, bf16[512,128,128]{2,1,0:T(8,128)(2,1)S(1)} %load_blocks.1.adj_ref, bf16[2176,128]{1,0:T(8,128)(2,1)S(1)} %merge_z.1.refs_0_, ...), custom_call_target="tpu_custom_call" | custom-call | flops 4294967296 | bytes 10485760 | tf_op jit(solution)/shard_map/backward_even/pallas_call | solution.py:125
  82.1 5.6 %backward_odd.1 = (f32[2048,128]{1,0:T(8,128)S(1)}, f32[2176,128]{1,0:T(8,128)S(1)}, f32[128,128]{1,0:T(8,128)S(1)}) custom-call(s32[512]{0:T(512)S(1)} %fusion.39.codes_ref, s32[1]{0:T(128)} %bitcast.5.count_ref, bf16[512,128,128]{2,1,0:T(8,128)(2,1)S(1)} %load_blocks.1.adj_ref, f32[33,128,128]{2,1,0:T(8,128)S(1)} %get-tuple-element.41.part_ref, ...), custom_call_target="tpu_custom_call" | custom-call | flops 4294967296 | bytes 10485760 | tf_op jit(solution)/shard_map/backward_odd/pallas_call | solution.py:161
  87.7 2.9 %collective-permute-start.25 = (f32[2176,128]{1,0:T(8,128)S(1)}, f32[2176,128]{1,0:T(8,128)S(1)}, u32[]{:S(2)}, u32[]{:S(2)}) collective-permute-start(f32[2176,128]{1,0:T(8,128)S(1)} %get-tuple-element.45), channel_id=1, source_target_pairs={{0,16},{16,0},{32,48},{48,32},{64,80},{80,64},{96,112},{112,96},{1... | collective-permute-start | bytes 3342344 | tf_op jit(solution)/shard_map/ppermute | solution.py:328
  90.6 2.4 %collective-permute-done.25.got = f32[2176,128]{1,0:T(8,128)S(1)} collective-permute-done((f32[2176,128]{1,0:T(8,128)S(1)}, f32[2176,128]{1,0:T(8,128)S(1)}, u32[]{:S(2)}, u32[]{:S(2)}) %collective-permute-start.25) | collective-permute-done | bytes 1114144 | tf_op jit(solution)/shard_map/ppermute | solution.py:328
  92.9 0.2 add_core.1
  93.1 4.3 %collective-permute-start.26 = (bf16[640,128]{1,0:T(8,128)(2,1)S(1)}, bf16[640,128]{1,0:T(8,128)(2,1)S(1)}, u32[]{:S(2)}, u32[]{:S(2)}) collective-permute-start(bf16[640,128]{1,0:T(8,128)(2,1)S(1)} %get-tuple-element.48), channel_id=1, source_target_pairs={{0,32},{16,48},{32,64},{48,80},{64,96},{80,112},{96,0},{112,16},{1... | collective-permute-start | bytes 491528 | tf_op jit(solution)/shard_map/ppermute | solution.py:324
  97.4 2.3 %collective-permute-start.27 = (bf16[640,128]{1,0:T(8,128)(2,1)S(1)}, bf16[640,128]{1,0:T(8,128)(2,1)S(1)}, u32[]{:S(2)}, u32[]{:S(2)}) collective-permute-start(bf16[640,128]{1,0:T(8,128)(2,1)S(1)} %get-tuple-element.49), channel_id=1, source_target_pairs={{0,64},{16,80},{32,96},{48,112},{64,0},{80,16},{96,32},{112,48},{1... | collective-permute-start | bytes 491528 | tf_op jit(solution)/shard_map/ppermute | solution.py:324
  99.8 0.2 collective-permute-start.28
  99.9 2.9 %collective-permute-done.26.refs_0_ = bf16[640,128]{1,0:T(8,128)(2,1)S(1)} collective-permute-done((bf16[640,128]{1,0:T(8,128)(2,1)S(1)}, bf16[640,128]{1,0:T(8,128)(2,1)S(1)}, u32[]{:S(2)}, u32[]{:S(2)}) %collective-permute-start.26) | collective-permute-done | bytes 163872 | tf_op jit(solution)/shard_map/ppermute | solution.py:324
  102.9 4.4 %collective-permute-done.27.refs_1_ = bf16[640,128]{1,0:T(8,128)(2,1)S(1)} collective-permute-done((bf16[640,128]{1,0:T(8,128)(2,1)S(1)}, bf16[640,128]{1,0:T(8,128)(2,1)S(1)}, u32[]{:S(2)}, u32[]{:S(2)}) %collective-permute-start.27) | collective-permute-done | bytes 163872 | tf_op jit(solution)/shard_map/ppermute | solution.py:324
  107.2 0.9 finish.1
  (21 shorter events, 0.1 us)
Async XLA Ops:
  0.6 17.9 %collective-permute-start.3 = (bf16[512,128]{1,0:T(8,128)(2,1)}, bf16[512,128]{1,0:T(8,128)(2,1)S(1)}, u32[]{:S(2)}, u32[]{:S(2)}) collective-permute-start(bf16[512,128]{1,0:T(8,128)(2,1)} %refs_0_.3), channel_id=1, source_target_pairs={{0,16},{16,0},{32,48},{48,32},{64,80},{80,64},{96,112},{112,96},{1... | collective-permute-start | bytes 393224 | tf_op jit(solution)/shard_map/ppermute | solution.py:328
  2.1 13.6 %collective-permute-start.2 = (bf16[512,128]{1,0:T(8,128)(2,1)}, bf16[512,128]{1,0:T(8,128)(2,1)S(1)}, u32[]{:S(2)}, u32[]{:S(2)}) collective-permute-start(bf16[512,128]{1,0:T(8,128)(2,1)} %refs_0_.3), channel_id=1, source_target_pairs={{0,96},{16,112},{32,0},{48,16},{64,32},{80,48},{96,64},{112,80},{1... | collective-permute-start | bytes 393224 | tf_op jit(solution)/shard_map/ppermute | solution.py:324
  5.0 11.8 %collective-permute-start.1 = (bf16[512,128]{1,0:T(8,128)(2,1)}, bf16[512,128]{1,0:T(8,128)(2,1)S(1)}, u32[]{:S(2)}, u32[]{:S(2)}) collective-permute-start(bf16[512,128]{1,0:T(8,128)(2,1)} %refs_0_.3), channel_id=1, source_target_pairs={{0,64},{16,80},{32,96},{48,112},{64,0},{80,16},{96,32},{112,48},{1... | collective-permute-start | bytes 393224 | tf_op jit(solution)/shard_map/ppermute | solution.py:324
  5.3 11.5 %collective-permute-start = (bf16[512,128]{1,0:T(8,128)(2,1)}, bf16[512,128]{1,0:T(8,128)(2,1)S(1)}, u32[]{:S(2)}, u32[]{:S(2)}) collective-permute-start(bf16[512,128]{1,0:T(8,128)(2,1)} %refs_0_.3), channel_id=1, source_target_pairs={{0,32},{16,48},{32,64},{48,80},{64,96},{80,112},{96,0},{112,16},{1... | collective-permute-start | bytes 393224 | tf_op jit(solution)/shard_map/ppermute | solution.py:324
  9.0 9.5 %copy-start = (bf16[512,128]{1,0:T(8,128)(2,1)S(1)}, bf16[512,128]{1,0:T(8,128)(2,1)}, u32[]{:S(2)}) copy-start(bf16[512,128]{1,0:T(8,128)(2,1)} %refs_0_.3) | copy-start | bytes 393220
  15.8 2.7 %collective-permute-start.6 = (bf16[512,128]{1,0:T(8,128)(2,1)S(1)}, bf16[512,128]{1,0:T(8,128)(2,1)S(1)}, u32[]{:S(2)}, u32[]{:S(2)}) collective-permute-start(bf16[512,128]{1,0:T(8,128)(2,1)S(1)} %collective-permute-done.2.refs_3_), channel_id=1, source_target_pairs={{0,16},{16,0},{32,48},{48,32},{64,80},{80,64},{96,112},{112,96},{1... | collective-permute-start | bytes 393224 | tf_op jit(solution)/shard_map/ppermute | solution.py:328
  16.8 1.8 %collective-permute-start.5 = (bf16[512,128]{1,0:T(8,128)(2,1)S(1)}, bf16[512,128]{1,0:T(8,128)(2,1)S(1)}, u32[]{:S(2)}, u32[]{:S(2)}) collective-permute-start(bf16[512,128]{1,0:T(8,128)(2,1)S(1)} %collective-permute-done.1.refs_2_), channel_id=1, source_target_pairs={{0,16},{16,0},{32,48},{48,32},{64,80},{80,64},{96,112},{112,96},{1... | collective-permute-start | bytes 393224 | tf_op jit(solution)/shard_map/ppermute | solution.py:328
  16.9 1.7 %collective-permute-start.4 = (bf16[512,128]{1,0:T(8,128)(2,1)S(1)}, bf16[512,128]{1,0:T(8,128)(2,1)S(1)}, u32[]{:S(2)}, u32[]{:S(2)}) collective-permute-start(bf16[512,128]{1,0:T(8,128)(2,1)S(1)} %collective-permute-done.refs_1_), channel_id=1, source_target_pairs={{0,16},{16,0},{32,48},{48,32},{64,80},{80,64},{96,112},{112,96},{1... | collective-permute-start | bytes 393224 | tf_op jit(solution)/shard_map/ppermute | solution.py:328
  23.5 17.7 %collective-permute-start.7 = (bf16[2048,128]{1,0:T(8,128)(2,1)S(1)}, bf16[2048,128]{1,0:T(8,128)(2,1)S(1)}, u32[]{:S(2)}, u32[]{:S(2)}) collective-permute-start(bf16[2048,128]{1,0:T(8,128)(2,1)S(1)} %get-tuple-element.29), channel_id=1, source_target_pairs={{0,4},{1,5},{2,6},{3,7},{4,8},{5,9},{6,10},{7,11},{8,12},{9,13},{1... | collective-permute-start | bytes 1572872 | tf_op jit(solution)/shard_map/ppermute | solution.py:316
  23.9 17.3 %collective-permute-start.8 = (bf16[2048,128]{1,0:T(8,128)(2,1)S(1)}, bf16[2048,128]{1,0:T(8,128)(2,1)S(1)}, u32[]{:S(2)}, u32[]{:S(2)}) collective-permute-start(bf16[2048,128]{1,0:T(8,128)(2,1)S(1)} %get-tuple-element.30), channel_id=1, source_target_pairs={{0,12},{1,13},{2,14},{3,15},{4,0},{5,1},{6,2},{7,3},{8,4},{9,5},{1... | collective-permute-start | bytes 1572872 | tf_op jit(solution)/shard_map/ppermute | solution.py:316
  31.2 20.4 %copy-start.1 = (bf16[512,128]{1,0:T(8,128)(2,1)S(1)}, bf16[512,128]{1,0:T(8,128)(2,1)}, u32[]{:S(2)}) copy-start(bf16[512,128]{1,0:T(8,128)(2,1)} %grad_ref.1) | copy-start | bytes 393220
  31.2 20.4 %copy-start.2 = (bf16[128,128]{1,0:T(8,128)(2,1)S(1)}, bf16[128,128]{1,0:T(8,128)(2,1)}, u32[]{:S(2)}) copy-start(bf16[128,128]{1,0:T(8,128)(2,1)} %weight_ref.3) | copy-start | bytes 98308
  31.2 5.4 %collective-permute-start.12 = (bf16[512,128]{1,0:T(8,128)(2,1)S(1)}, bf16[512,128]{1,0:T(8,128)(2,1)S(1)}, u32[]{:S(2)}, u32[]{:S(2)}) collective-permute-start(bf16[512,128]{1,0:T(8,128)(2,1)S(1)} %get-tuple-element.36), channel_id=1, source_target_pairs={{0,1},{1,2},{2,3},{3,0},{4,5},{5,6},{6,7},{7,4},{8,9},{9,10},{10,1... | collective-permute-start | bytes 393224 | tf_op jit(solution)/shard_map/ppermute | solution.py:320
  32.0 6.3 %collective-permute-start.13 = (bf16[512,128]{1,0:T(8,128)(2,1)S(1)}, bf16[512,128]{1,0:T(8,128)(2,1)S(1)}, u32[]{:S(2)}, u32[]{:S(2)}) collective-permute-start(bf16[512,128]{1,0:T(8,128)(2,1)S(1)} %get-tuple-element.37), channel_id=1, source_target_pairs={{0,2},{1,3},{2,0},{3,1},{4,6},{5,7},{6,4},{7,5},{8,10},{9,11},{10,... | collective-permute-start | bytes 393224 | tf_op jit(solution)/shard_map/ppermute | solution.py:320
  34.5 4.7 %collective-permute-start.14 = (bf16[512,128]{1,0:T(8,128)(2,1)S(1)}, bf16[512,128]{1,0:T(8,128)(2,1)S(1)}, u32[]{:S(2)}, u32[]{:S(2)}) collective-permute-start(bf16[512,128]{1,0:T(8,128)(2,1)S(1)} %get-tuple-element.38), channel_id=1, source_target_pairs={{0,3},{1,0},{2,1},{3,2},{4,7},{5,4},{6,5},{7,6},{8,11},{9,8},{10,9... | collective-permute-start | bytes 393224 | tf_op jit(solution)/shard_map/ppermute | solution.py:320
  39.2 8.7 %collective-permute-start.15 = (bf16[512,128]{1,0:T(8,128)(2,1)S(1)}, bf16[512,128]{1,0:T(8,128)(2,1)S(1)}, u32[]{:S(2)}, u32[]{:S(2)}) collective-permute-start(bf16[512,128]{1,0:T(8,128)(2,1)S(1)} %add_z.1), channel_id=1, source_target_pairs={{0,8},{1,9},{2,10},{3,11},{4,12},{5,13},{6,14},{7,15},{8,0},{9,1},... | collective-permute-start | bytes 393224 | tf_op jit(solution)/shard_map/ppermute | solution.py:316
  41.4 6.6 %collective-permute-start.9 = (bf16[512,128]{1,0:T(8,128)(2,1)S(1)}, bf16[512,128]{1,0:T(8,128)(2,1)S(1)}, u32[]{:S(2)}, u32[]{:S(2)}) collective-permute-start(bf16[512,128]{1,0:T(8,128)(2,1)S(1)} %get-tuple-element.32), channel_id=1, source_target_pairs={{0,1},{1,2},{2,3},{3,0},{4,5},{5,6},{6,7},{7,4},{8,9},{9,10},{10,1... | collective-permute-start | bytes 393224 | tf_op jit(solution)/shard_map/ppermute | solution.py:320
  44.0 6.4 %collective-permute-start.10 = (bf16[512,128]{1,0:T(8,128)(2,1)S(1)}, bf16[512,128]{1,0:T(8,128)(2,1)S(1)}, u32[]{:S(2)}, u32[]{:S(2)}) collective-permute-start(bf16[512,128]{1,0:T(8,128)(2,1)S(1)} %get-tuple-element.33), channel_id=1, source_target_pairs={{0,2},{1,3},{2,0},{3,1},{4,6},{5,7},{6,4},{7,5},{8,10},{9,11},{10,... | collective-permute-start | bytes 393224 | tf_op jit(solution)/shard_map/ppermute | solution.py:320
  46.2 5.4 %collective-permute-start.11 = (bf16[512,128]{1,0:T(8,128)(2,1)S(1)}, bf16[512,128]{1,0:T(8,128)(2,1)S(1)}, u32[]{:S(2)}, u32[]{:S(2)}) collective-permute-start(bf16[512,128]{1,0:T(8,128)(2,1)S(1)} %get-tuple-element.34), channel_id=1, source_target_pairs={{0,3},{1,0},{2,1},{3,2},{4,7},{5,4},{6,5},{7,6},{8,11},{9,8},{10,9... | collective-permute-start | bytes 393224 | tf_op jit(solution)/shard_map/ppermute | solution.py:320
  52.7 15.7 %collective-permute-start.19 = (bf16[640,128]{1,0:T(8,128)(2,1)S(1)}, bf16[640,128]{1,0:T(8,128)(2,1)S(1)}, u32[]{:S(2)}, u32[]{:S(2)}) collective-permute-start(bf16[640,128]{1,0:T(8,128)(2,1)S(1)} %get-tuple-element.40.refs_0_), channel_id=1, source_target_pairs={{0,8},{1,9},{2,10},{3,11},{4,12},{5,13},{6,14},{7,15},{8,0},{9,1},... | collective-permute-start | bytes 491528 | tf_op jit(solution)/shard_map/ppermute | solution.py:316
  52.7 10.0 %collective-permute-start.18 = (bf16[640,128]{1,0:T(8,128)(2,1)S(1)}, bf16[640,128]{1,0:T(8,128)(2,1)S(1)}, u32[]{:S(2)}, u32[]{:S(2)}) collective-permute-start(bf16[640,128]{1,0:T(8,128)(2,1)S(1)} %get-tuple-element.40.refs_0_), channel_id=1, source_target_pairs={{0,3},{1,0},{2,1},{3,2},{4,7},{5,4},{6,5},{7,6},{8,11},{9,8},{10,9... | collective-permute-start | bytes 491528 | tf_op jit(solution)/shard_map/ppermute | solution.py:320
  56.2 6.5 %collective-permute-start.17 = (bf16[640,128]{1,0:T(8,128)(2,1)S(1)}, bf16[640,128]{1,0:T(8,128)(2,1)S(1)}, u32[]{:S(2)}, u32[]{:S(2)}) collective-permute-start(bf16[640,128]{1,0:T(8,128)(2,1)S(1)} %get-tuple-element.40.refs_0_), channel_id=1, source_target_pairs={{0,2},{1,3},{2,0},{3,1},{4,6},{5,7},{6,4},{7,5},{8,10},{9,11},{10,... | collective-permute-start | bytes 491528 | tf_op jit(solution)/shard_map/ppermute | solution.py:320
  56.2 7.8 %collective-permute-start.16 = (bf16[640,128]{1,0:T(8,128)(2,1)S(1)}, bf16[640,128]{1,0:T(8,128)(2,1)S(1)}, u32[]{:S(2)}, u32[]{:S(2)}) collective-permute-start(bf16[640,128]{1,0:T(8,128)(2,1)S(1)} %get-tuple-element.40.refs_0_), channel_id=1, source_target_pairs={{0,1},{1,2},{2,3},{3,0},{4,5},{5,6},{6,7},{7,4},{8,9},{9,10},{10,1... | collective-permute-start | bytes 491528 | tf_op jit(solution)/shard_map/ppermute | solution.py:320
  64.1 18.0 %collective-permute-start.24 = (bf16[2176,128]{1,0:T(8,128)(2,1)S(1)}, bf16[2176,128]{1,0:T(8,128)(2,1)S(1)}, u32[]{:S(2)}, u32[]{:S(2)}) collective-permute-start(bf16[2176,128]{1,0:T(8,128)(2,1)S(1)} %merge_z.1.refs_0_), channel_id=1, source_target_pairs={{0,12},{1,13},{2,14},{3,15},{4,0},{5,1},{6,2},{7,3},{8,4},{9,5},{1... | collective-permute-start | bytes 1671176 | tf_op jit(solution)/shard_map/ppermute | solution.py:316
  67.3 14.8 %collective-permute-start.23 = (bf16[2176,128]{1,0:T(8,128)(2,1)S(1)}, bf16[2176,128]{1,0:T(8,128)(2,1)S(1)}, u32[]{:S(2)}, u32[]{:S(2)}) collective-permute-start(bf16[2176,128]{1,0:T(8,128)(2,1)S(1)} %merge_z.1.refs_0_), channel_id=1, source_target_pairs={{0,4},{1,5},{2,6},{3,7},{4,8},{5,9},{6,10},{7,11},{8,12},{9,13},{1... | collective-permute-start | bytes 1671176 | tf_op jit(solution)/shard_map/ppermute | solution.py:316
  68.4 4.5 %collective-permute-start.22 = (bf16[640,128]{1,0:T(8,128)(2,1)S(1)}, bf16[640,128]{1,0:T(8,128)(2,1)S(1)}, u32[]{:S(2)}, u32[]{:S(2)}) collective-permute-start(bf16[640,128]{1,0:T(8,128)(2,1)S(1)} %collective-permute-done.19.refs_1_), channel_id=1, source_target_pairs={{0,3},{1,0},{2,1},{3,2},{4,7},{5,4},{6,5},{7,6},{8,11},{9,8},{10,9... | collective-permute-start | bytes 491528 | tf_op jit(solution)/shard_map/ppermute | solution.py:320
  68.4 5.8 %collective-permute-start.21 = (bf16[640,128]{1,0:T(8,128)(2,1)S(1)}, bf16[640,128]{1,0:T(8,128)(2,1)S(1)}, u32[]{:S(2)}, u32[]{:S(2)}) collective-permute-start(bf16[640,128]{1,0:T(8,128)(2,1)S(1)} %collective-permute-done.19.refs_1_), channel_id=1, source_target_pairs={{0,2},{1,3},{2,0},{3,1},{4,6},{5,7},{6,4},{7,5},{8,10},{9,11},{10,... | collective-permute-start | bytes 491528 | tf_op jit(solution)/shard_map/ppermute | solution.py:320
  68.8 8.4 %collective-permute-start.20 = (bf16[640,128]{1,0:T(8,128)(2,1)S(1)}, bf16[640,128]{1,0:T(8,128)(2,1)S(1)}, u32[]{:S(2)}, u32[]{:S(2)}) collective-permute-start(bf16[640,128]{1,0:T(8,128)(2,1)S(1)} %collective-permute-done.19.refs_1_), channel_id=1, source_target_pairs={{0,1},{1,2},{2,3},{3,0},{4,5},{5,6},{6,7},{7,4},{8,9},{9,10},{10,1... | collective-permute-start | bytes 491528 | tf_op jit(solution)/shard_map/ppermute | solution.py:320
  87.7 5.2 %collective-permute-start.25 = (f32[2176,128]{1,0:T(8,128)S(1)}, f32[2176,128]{1,0:T(8,128)S(1)}, u32[]{:S(2)}, u32[]{:S(2)}) collective-permute-start(f32[2176,128]{1,0:T(8,128)S(1)} %get-tuple-element.45), channel_id=1, source_target_pairs={{0,16},{16,0},{32,48},{48,32},{64,80},{80,64},{96,112},{112,96},{1... | collective-permute-start | bytes 3342344 | tf_op jit(solution)/shard_map/ppermute | solution.py:328
  93.1 9.7 %collective-permute-start.26 = (bf16[640,128]{1,0:T(8,128)(2,1)S(1)}, bf16[640,128]{1,0:T(8,128)(2,1)S(1)}, u32[]{:S(2)}, u32[]{:S(2)}) collective-permute-start(bf16[640,128]{1,0:T(8,128)(2,1)S(1)} %get-tuple-element.48), channel_id=1, source_target_pairs={{0,32},{16,48},{32,64},{48,80},{64,96},{80,112},{96,0},{112,16},{1... | collective-permute-start | bytes 491528 | tf_op jit(solution)/shard_map/ppermute | solution.py:324
  97.4 9.8 %collective-permute-start.27 = (bf16[640,128]{1,0:T(8,128)(2,1)S(1)}, bf16[640,128]{1,0:T(8,128)(2,1)S(1)}, u32[]{:S(2)}, u32[]{:S(2)}) collective-permute-start(bf16[640,128]{1,0:T(8,128)(2,1)S(1)} %get-tuple-element.49), channel_id=1, source_target_pairs={{0,64},{16,80},{32,96},{48,112},{64,0},{80,16},{96,32},{112,48},{1... | collective-permute-start | bytes 491528 | tf_op jit(solution)/shard_map/ppermute | solution.py:324
  99.8 7.5 %collective-permute-start.28 = (bf16[640,128]{1,0:T(8,128)(2,1)S(1)}, bf16[640,128]{1,0:T(8,128)(2,1)S(1)}, u32[]{:S(2)}, u32[]{:S(2)}) collective-permute-start(bf16[640,128]{1,0:T(8,128)(2,1)S(1)} %get-tuple-element.50), channel_id=1, source_target_pairs={{0,96},{16,112},{32,0},{48,16},{64,32},{80,48},{96,64},{112,80},{1... | collective-permute-start | bytes 491528 | tf_op jit(solution)/shard_map/ppermute | solution.py:324

commit v3 on v2

v3 whole, which is shorter than its diff:
```python
import functools

import jax
import jax.numpy as jnp
from jax import lax
from jax.experimental import pallas as pl
from jax.experimental.pallas import tpu as pltpu
from jax.sharding import PartitionSpec as P

BLK = 128
NX = 4
NZ = 4
NY = 4
ROW_BLOCKS = 64
COL_BLOCKS = 32
HALF = 32
OWN = 4
F32 = jnp.float32
BF16 = jnp.bfloat16
VMEM_LIMIT = 24 * 1024 * 1024


def vmem_specs(n):
    return [pl.BlockSpec(memory_space=pltpu.VMEM)] * n


def params():
    return pltpu.CompilerParams(vmem_limit_bytes=VMEM_LIMIT)


ODD_F, TWO_F, ZERO_F, ZERO_B, TWO_B, OTHER_B, OWN_B = range(7)
LISTS = 8


def prepare_kernel(count_ref, brow_hbm, bcol_hbm, adj_ref, blocks_ref, codes_ref, brow_ref, bcol_ref, sems):
    first = pltpu.make_async_copy(brow_hbm, brow_ref, sems.at[0])
    second = pltpu.make_async_copy(bcol_hbm, bcol_ref, sems.at[1])
    copy = pltpu.make_async_copy(adj_ref, blocks_ref, sems.at[2])
    first.start()
    second.start()
    copy.start()
    first.wait()
    second.wait()
    row, col = lax.axis_index("row"), lax.axis_index("col")
    y, core = row >> 1, row & 1
    x, z = col >> 2, col & 3
    brow, bcol = brow_ref[...], bcol_ref[...]
    capacity = brow.shape[1]
    slot = lax.broadcasted_iota(jnp.int32, (1, capacity), 1)
    alive = slot < count_ref[0, 0]
    rx, rz, rb = (brow >> 4) & 3, (brow >> 2) & 3, brow & 3
    cy, cc, cb = (bcol >> 3) & 3, (bcol >> 2) & 1, bcol & 3
    ahead, behind = (rx - x) & 3, (x - rx) & 3
    other = cc ^ core
    odd = ahead & 1
    to_row = odd * (ahead >> 1) * 16 + ((rz - z) & 3) * OWN + rb
    from_row = odd * (behind >> 1) * 16 + ((z - rz) & 3) * OWN + rb
    to_col = (1 - odd) * other * 16 + ((cy - y) & 3) * OWN + cb
    from_col = other * 16 + ((y - cy) & 3) * OWN + cb
    kind = jnp.where(odd == 1, 2 + (1 - other), ahead >> 1)
    kind = jnp.where(alive, kind, 4)
    row_codes = [
        (slot + 512 * to_row + 65536 * from_col).astype(F32),
        (slot + 512 * to_col + 65536 * from_row).astype(F32),
        kind.astype(F32),
    ]
    counts = [jnp.sum((kind == k).astype(F32), axis=1, keepdims=True) for k in range(4)]
    member = [(kind == k).astype(F32) for k in range(4)]
    lists = [jnp.zeros((1, capacity), F32) for _ in range(7)]
    step = 64
    lane = lax.broadcasted_iota(jnp.int32, (step, capacity), 1)
    place = lane.astype(F32)
    for c in range(0, capacity, step):
        sub = lax.broadcasted_iota(jnp.int32, (step, capacity), 0) + c
        fcode, bcode, ckind = (
            jnp.sum(jnp.where(lane == sub, v, 0.0), axis=1, keepdims=True) for v in row_codes
        )
        ranks = [
            jnp.sum(jnp.where(lane <= sub, m, 0.0), axis=1, keepdims=True) - 1.0 for m in member
        ]
        ranks = [jnp.where(ckind == float(k), r, -1.0) for k, r in enumerate(ranks)]
        both = jnp.where(ckind == 2.0, ranks[2], jnp.where(ckind == 3.0, ranks[3] + counts[2], -1.0))
        for q, rank, code in (
            (ODD_F, both, fcode),
            (TWO_F, ranks[1], fcode),
            (ZERO_F, ranks[0], fcode),
            (ZERO_B, ranks[0], bcode),
            (TWO_B, ranks[1], bcode),
            (OTHER_B, ranks[2], bcode),
            (OWN_B, ranks[3], bcode),
        ):
            lists[q] += jnp.sum(jnp.where(place == rank, code, 0.0), axis=0, keepdims=True)
    where = slot.astype(F32)
    codes_ref[...] = jnp.zeros_like(codes_ref)
    for q, count, idle in (
        (ODD_F, counts[2] + counts[3], HALF),
        (TWO_F, counts[1], HALF // 2),
        (ZERO_F, counts[0], HALF // 2),
        (ZERO_B, counts[0], COL_BLOCKS),
        (TWO_B, counts[1], COL_BLOCKS),
        (OTHER_B, counts[2], COL_BLOCKS // 2),
        (OWN_B, counts[3], COL_BLOCKS // 2),
    ):
        codes_ref[q : q + 1, 0:capacity] = jnp.where(where < count, lists[q], 512.0 * idle).astype(jnp.int32)
        codes_ref[q : q + 1, capacity : capacity + BLK] = jnp.broadcast_to(count, (1, BLK)).astype(jnp.int32)
    copy.wait()


def prepare(adjacency, row_index, col_index, block_count):
    capacity = adjacency.shape[0]
    return pl.pallas_call(
        prepare_kernel,
        out_shape=[
            jax.ShapeDtypeStruct(adjacency.shape, adjacency.dtype),
            jax.ShapeDtypeStruct((LISTS, capacity + BLK), jnp.int32),
        ],
        in_specs=[pl.BlockSpec(memory_space=pltpu.SMEM)] + [pl.BlockSpec(memory_space=pltpu.HBM)] * 3,
        out_specs=vmem_specs(2),
        scratch_shapes=[pltpu.VMEM((1, capacity), jnp.int32)] * 2 + [pltpu.SemaphoreType.DMA((3,))],
        compiler_params=params(),
        cost_estimate=pl.CostEstimate(flops=0, bytes_accessed=2 * adjacency.size * 2, transcendentals=0),
        name="prepare",
    )(block_count, row_index, col_index, adjacency)


def accumulate(which, unroll, codes_ref, acc, product):
    live = codes_ref[which, codes_ref.shape[1] - BLK]

    @pl.loop(0, (live + unroll - 1) // unroll)
    def _(g):
        codes = [codes_ref[which, g * unroll + j] for j in range(unroll)]
        prods = [product(c & 511, c >> 16) for c in codes]
        for j in range(unroll):
            acc[(codes[j] >> 9) & 127] += prods[j]


def sparse_cost(share):
    return pl.CostEstimate(
        flops=int(512 * BLK**3 * 8 * share), bytes_accessed=int(20 * 2**20 * share), transcendentals=0
    )


def sparse_call(kernel, codes, adjacency, operands, outs, scratch, share, name):
    return pl.pallas_call(
        kernel,
        out_shape=[jax.ShapeDtypeStruct(shape, dtype) for shape, dtype in outs],
        in_specs=[pl.BlockSpec(memory_space=pltpu.SMEM)] + vmem_specs(1 + len(operands)),
        out_specs=vmem_specs(len(outs)),
        scratch_shapes=[pltpu.VMEM((blocks, BLK, BLK), dtype) for blocks, dtype in scratch],
        compiler_params=params(),
        cost_estimate=sparse_cost(share),
        name=name,
    )(codes, adjacency, *operands)


def write_rows(acc, outs):
    at = 0
    for out in outs:
        blocks = out.shape[0] // BLK
        out[...] = acc[pl.ds(at, blocks)].reshape(out.shape).astype(out.dtype)
        at += blocks


def forward_odd_kernel(nin, codes_ref, adj_ref, *refs):
    ins, (feats, *outs), acc = refs[:nin], refs[nin:-1], refs[-1]
    per = feats.shape[0] // nin
    for i in range(nin):
        feats[pl.ds(i * per, per)] = ins[i][...].reshape(per, BLK, BLK)
    acc[...] = jnp.zeros_like(acc)

    def product(slot, source):
        return jnp.dot(adj_ref[slot], feats[source], preferred_element_type=F32)

    accumulate(ODD_F, 64, codes_ref, acc, product)
    write_rows(acc, outs)


def forward_even_kernel(which, codes_ref, adj_ref, feats, *refs):
    outs, acc = refs[:-1], refs[-1]
    acc[...] = jnp.zeros_like(acc)

    def product(slot, source):
        return jnp.dot(adj_ref[slot], feats[source], preferred_element_type=F32)

    accumulate(which, 32, codes_ref, acc, product)
    write_rows(acc, outs)


def gather_slopes(slopes, ins):
    at = 0
    for part in ins:
        blocks = part.shape[0] // BLK - 1
        slopes[pl.ds(at, blocks)] = part[pl.ds(0, blocks * BLK)].reshape(blocks, BLK, BLK)
        at += blocks


def last_block(part):
    return part[pl.ds(part.shape[0] - BLK, BLK)].astype(F32)


def backward_zero_kernel(codes_ref, adj_ref, column, acc, slopes):
    gather_slopes(slopes, [column])
    acc[...] = jnp.zeros_like(acc)

    def product(slot, source):
        return jnp.dot(slopes[source], adj_ref[slot], preferred_element_type=F32)

    accumulate(ZERO_B, 32, codes_ref, acc, product)


def backward_two_kernel(nin, codes_ref, adj_ref, before, column, *refs):
    ins, (acc, wsum), slopes = refs[:nin], refs[nin : nin + 2], refs[-1]
    gather_slopes(slopes, ins)
    acc[...] = before[...]

    def product(slot, source):
        return jnp.dot(slopes[source], adj_ref[slot], preferred_element_type=F32)

    accumulate(TWO_B, 32, codes_ref, acc, product)
    wsum[...] = last_block(column) + sum(last_block(part) for part in ins)


def backward_other_kernel(codes_ref, adj_ref, before, wpart, first, second, send, wsum, slopes, acc):
    half = COL_BLOCKS // 2
    gather_slopes(slopes, [first, second])
    acc[...] = before[pl.ds(half, half + 1)]

    def product(slot, source):
        return jnp.dot(slopes[source], adj_ref[slot], preferred_element_type=F32)

    accumulate(OTHER_B, 32, codes_ref, acc, product)
    for b in range(half):
        send[pl.ds(b * BLK, BLK)] = acc[b].T
    total = wpart[...] + last_block(first) + last_block(second)
    wsum[...] = total
    send[pl.ds(half * BLK, BLK)] = total


def backward_own_kernel(codes_ref, adj_ref, before, first, second, keep, slopes, acc):
    half = COL_BLOCKS // 2
    gather_slopes(slopes, [first, second])
    acc[...] = before[pl.ds(0, half + 1)]

    def product(slot, source):
        return jnp.dot(slopes[source], adj_ref[slot], preferred_element_type=F32)

    accumulate(OWN_B, 32, codes_ref, acc, product)
    for b in range(half):
        keep[pl.ds(b * BLK, BLK)] = acc[b].T


def add_split_kernel(nin, *refs):
    ins, outs = refs[:nin], refs[nin:]
    at = 0
    for out in outs:
        rows = out.shape[0]
        total = ins[0][pl.ds(at, rows)].astype(F32)
        for part in ins[1:]:
            total += part[pl.ds(at, rows)].astype(F32)
        out[...] = total.astype(out.dtype)
        at += rows


def add_split(parts, dtypes, name):
    rows = parts[0].shape[0] // len(dtypes)
    return pl.pallas_call(
        functools.partial(add_split_kernel, len(parts)),
        out_shape=[jax.ShapeDtypeStruct((rows, BLK), dtype) for dtype in dtypes],
        in_specs=vmem_specs(len(parts)),
        out_specs=vmem_specs(len(dtypes)),
        compiler_params=params(),
        name=name,
    )(*parts)


def activate_kernel(weight_ref, grad_ref, *refs):
    parts, (act_ref, pay_ref) = refs[:-2], refs[-2:]
    rows = act_ref.shape[0]
    total = parts[0][...]
    for part in parts[1:]:
        total += part[...].astype(F32)
    weight = weight_ref[...].astype(F32)
    pre = jnp.dot(total, weight, precision=lax.Precision.HIGHEST, preferred_element_type=F32)
    squash = jnp.tanh(pre)
    act_ref[...] = squash.astype(BF16)
    slope = (grad_ref[...].astype(F32) * (1.0 - squash * squash)).astype(BF16)
    high = total.astype(BF16)
    low = (total - high.astype(F32)).astype(BF16)
    wterm = jnp.zeros((BLK, BLK), F32)
    for b in range(0, rows, BLK):
        turned = slope[b : b + BLK].T
        pay_ref[pl.ds(b, BLK)] = turned
        wterm += jnp.dot(turned, high[b : b + BLK], preferred_element_type=F32)
        wterm += jnp.dot(turned, low[b : b + BLK], preferred_element_type=F32)
    pay_ref[pl.ds(rows, BLK)] = wterm.astype(BF16)


def activate(weight, grad_out, parts):
    rows = grad_out.shape[0]
    return pl.pallas_call(
        activate_kernel,
        out_shape=[
            jax.ShapeDtypeStruct((rows, BLK), BF16),
            jax.ShapeDtypeStruct((rows + BLK, BLK), BF16),
        ],
        in_specs=vmem_specs(2 + len(parts)),
        out_specs=vmem_specs(2),
        compiler_params=params(),
        name="activate",
    )(weight, grad_out, *parts)


def merge_kernel(*refs):
    parts, out = refs[:-1], refs[-1]
    rows = parts[0].shape[0] - BLK
    total = jnp.zeros((BLK, BLK), F32)
    for i, part in enumerate(parts):
        out[pl.ds(i * rows, rows)] = part[pl.ds(0, rows)]
        total += last_block(part)
    out[pl.ds(len(parts) * rows, BLK)] = total.astype(BF16)


def merge(parts, name):
    rows = len(parts) * (parts[0].shape[0] - BLK) + BLK
    return pl.pallas_call(
        merge_kernel,
        out_shape=jax.ShapeDtypeStruct((rows, BLK), BF16),
        in_specs=vmem_specs(len(parts)),
        out_specs=pl.BlockSpec(memory_space=pltpu.VMEM),
        compiler_params=params(),
        name=name,
    )(*parts)


def add_core_kernel(nout, keep, wkeep, got, *outs):
    rows = keep.shape[0] // nout
    wsum = wkeep[...] + got[pl.ds(rows * nout, BLK)].astype(F32)
    outs[nout][...] = wsum
    for i in range(nout):
        total = keep[pl.ds(i * rows, rows)] + got[pl.ds(i * rows, rows)].astype(F32)
        outs[i][pl.ds(0, rows)] = total.astype(outs[i].dtype)
        if i:
            outs[i][pl.ds(rows, BLK)] = wsum.astype(outs[i].dtype)


def add_core(keep, wkeep, got):
    rows = keep.shape[0] // NY
    return pl.pallas_call(
        functools.partial(add_core_kernel, NY),
        out_shape=[jax.ShapeDtypeStruct((rows, BLK), F32)]
        + [jax.ShapeDtypeStruct((rows + BLK, BLK), BF16)] * (NY - 1)
        + [jax.ShapeDtypeStruct((BLK, BLK), F32)],
        in_specs=vmem_specs(3),
        out_specs=vmem_specs(NY + 1),
        compiler_params=params(),
        name="add_core",
    )(keep, wkeep, got)


def finish_kernel(scale, weight_ref, own, wown, *refs):
    parts, (out_ref, wout_ref) = refs[:-2], refs[-2:]
    rows = own.shape[0]
    total, wsum = own[...], wown[...]
    for part in parts:
        total += part[pl.ds(0, rows)].astype(F32)
        wsum += part[pl.ds(rows, BLK)].astype(F32)
    out_ref[...] = lax.dot_general(
        total.astype(BF16), weight_ref[...], (((1,), (1,)), ((), ())), preferred_element_type=F32
    ).astype(BF16)
    wout_ref[...] = wsum.T * scale


def finish(scale, weight, own, wown, parts):
    return pl.pallas_call(
        functools.partial(finish_kernel, scale),
        out_shape=[
            jax.ShapeDtypeStruct(own.shape, BF16),
            jax.ShapeDtypeStruct((BLK, BLK), F32),
        ],
        in_specs=vmem_specs(3 + len(parts)),
        out_specs=vmem_specs(2),
        compiler_params=params(),
        name="finish",
    )(weight, own, wown, *parts)


def shift_x(a, d):
    return lax.ppermute(a, "col", [(i, (i // NZ + d) % NX * NZ + i % NZ) for i in range(NX * NZ)])


def shift_z(a, d):
    return lax.ppermute(a, "col", [(i, i // NZ * NZ + (i % NZ + d) % NZ) for i in range(NX * NZ)])


def shift_y(a, d):
    return lax.ppermute(a, "row", [(i, (i // 2 + d) % NY * 2 + i % 2) for i in range(NY * 2)])


def swap_core(a):
    return lax.ppermute(a, "row", [(i, i ^ 1) for i in range(NY * 2)])


def local(features, weight, adjacency, row_index, col_index, block_count, grad_out):
    own_rows = features.shape[0]

    beside = [shift_y(features, d) for d in range(1, NY)]
    blocks, codes = prepare(adjacency[0, 0], row_index[0], col_index[0], block_count)
    beside, blocks, codes = lax.optimization_barrier((beside, blocks, codes))
    mine = [features] + beside
    theirs = [swap_core(a) for a in mine]

    feats, x1, x3 = sparse_call(
        functools.partial(forward_odd_kernel, 2 * NY),
        codes,
        blocks,
        mine + theirs,
        [((COL_BLOCKS, BLK, BLK), BF16)] + [((NZ * own_rows, BLK), BF16)] * 2,
        [(HALF + 1, F32)],
        0.5,
        "forward_odd",
    )
    x1, x3 = shift_x(x1, 1), shift_x(x3, 3)
    across, z1, z2, z3 = sparse_call(
        functools.partial(forward_even_kernel, TWO_F),
        codes,
        blocks,
        [feats],
        [((own_rows, BLK), F32)] + [((own_rows, BLK), BF16)] * 3,
        [(HALF // 2 + 1, F32)],
        0.25,
        "forward_two",
    )
    z1, z2, z3 = shift_z(z1, 1), shift_z(z2, 2), shift_z(z3, 3)
    column = sparse_call(
        functools.partial(forward_even_kernel, ZERO_F),
        codes,
        blocks,
        [feats],
        [((NZ * own_rows, BLK), F32)],
        [(HALF // 2 + 1, F32)],
        0.25,
        "forward_zero",
    )[0]
    from_z = [z1, z2, z3]
    own, z1, z2, z3 = add_split([column, x1, x3], [F32, BF16, BF16, BF16], "add_x")
    across, own = lax.optimization_barrier((across, own))
    across = add_split([across] + from_z, [BF16], "add_z")[0]
    parts = [own, shift_z(z1, 1), shift_z(z2, 2), shift_z(z3, 3), shift_x(across, 2)]
    activated, pay = activate(weight, grad_out, parts)

    beside = [shift_z(pay, d) for d in range(1, NZ)]
    across = shift_x(pay, 2)
    column = merge([pay] + beside, "merge_z")
    first, second = shift_x(column, 1), shift_x(column, 3)
    across = [across] + [shift_z(across, d) for d in range(1, NZ)]

    half_rows = COL_BLOCKS // 2 * BLK
    part = sparse_call(
        backward_zero_kernel,
        codes,
        blocks,
        [column],
        [((COL_BLOCKS + 1, BLK, BLK), F32)],
        [(HALF // 2, BF16)],
        0.25,
        "backward_zero",
    )[0]
    part, wpart = sparse_call(
        functools.partial(backward_two_kernel, NZ),
        codes,
        blocks,
        [part, column] + across,
        [((COL_BLOCKS + 1, BLK, BLK), F32), ((BLK, BLK), F32)],
        [(HALF // 2, BF16)],
        0.25,
        "backward_two",
    )
    odd_scratch = [(HALF, BF16), (COL_BLOCKS // 2 + 1, F32)]
    send, wkeep = sparse_call(
        backward_other_kernel,
        codes,
        blocks,
        [part, wpart, first, second],
        [((half_rows + BLK, BLK), F32), ((BLK, BLK), F32)],
        odd_scratch,
        0.25,
        "backward_other",
    )
    got = swap_core(send)
    keep = sparse_call(
        backward_own_kernel,
        codes,
        blocks,
        [part, first, second],
        [((half_rows, BLK), F32)],
        odd_scratch,
        0.25,
        "backward_own",
    )[0]
    parts = add_core(keep, wkeep, got)
    got = [shift_y(parts[d], d) for d in range(1, NY)]
    nodes_all = own_rows * lax.axis_size("row") * lax.axis_size("col")
    input_grad, weight_grad = finish(nodes_all ** (-0.5), weight, parts[0], parts[NY], got)
    return (activated, input_grad, weight_grad)


def solution(mesh):
    placed = (
        P(("col", "row"), None),
        P(),
        P("row", "col", None, None, None),
        P("row", "col", None),
        P("row", "col", None),
        P("row", "col"),
        P(("row", "col"), None),
    )
    return jax.shard_map(
        local,
        mesh=mesh,
        in_specs=placed,
        out_specs=(P(("row", "col"), None), P(("col", "row"), None), P()),
        check_vma=False,
    )
```

time: 108 us -> 97.2 us (0.900); the launches traced: 108 us -> 95.8 us
  waiting for transfers between devices: 30.7 us -> 22.6 us
  other arithmetic: 5.65 us -> 0 us
  Pallas kernels: 28.6 us -> 30.6 us
  starting transfers between devices: 41.7 us -> 39.8 us
  local copies, waits for them, and re-layouts: 0.02 us -> 1.37 us
    ppermute x12, waiting for transfers between devices: 21 us -> 12.3 us  [shift_z(): lax.ppermute(a, 'col', [(i, i // NZ * NZ + (i % NZ + d) % NZ) for i in ra...]
    ppermute x12, starting transfers between devices: 16.2 us -> 18.9 us  [shift_z(): lax.ppermute(a, 'col', [(i, i // NZ * NZ + (i % NZ + d) % NZ) for i in ra...]
    select_n x3 -> x0, other arithmetic: 2.41 us -> none  [order_slots(): lists.append(jnp.where(slots < count, picked, idle))]
    ppermute x6, starting transfers between devices: 8.99 us -> 6.73 us  [shift_x(): lax.ppermute(a, 'col', [(i, (i // NZ + d) % NX * NZ + i % NZ) for i in ra...]
    pallas_call x5 -> x8, Pallas kernels: 26.1 us -> 28.2 us  [the longest x7 22.4 us: sparse_call(): pl.pallas_call(kernel, out_shape=[jax.ShapeDtypeStruct(shape, dtype) for...]
    reduce_sum x4 -> x0, other arithmetic: 1.86 us -> none  [the longest x1 0.93 us: order_slots(): picked = jnp.sum(jnp.where(here, code[None, :], 0), axis=1, dtype=jnp.int32)]
    ppermute x6, waiting for transfers between devices: 0.02 us -> 1.83 us  [shift_x(): lax.ppermute(a, 'col', [(i, (i // NZ + d) % NX * NZ + i % NZ) for i in ra...]
    ppermute x5, starting transfers between devices: 5.85 us -> 4.05 us  [swap_core(): return lax.ppermute(a, 'row', [(i, i ^ 1) for i in range(NY * 2)])]
  transfers between devices with their start and end apart: 29 -> 29, of which waited for: 13 -> 13; matrix products, arithmetic and copies ran while one was open for 5% -> 0% of each run, Pallas kernels for 15% -> 21%
where the time goes in v3:
time: 97.2 us; the launch traced here: 95.8 us
  starting transfers between devices  39.8 us (41%)
  Pallas kernels  30.6 us (31%)
  waiting for transfers between devices  22.6 us (23%)
  between operations  1.48 us (2%)
  local copies, waits for them, and re-layouts  1.37 us (1%)
    pallas_call x7, Pallas kernels, sparse_call(): pl.pallas_call(kernel, out_shape=[jax.ShapeDtypeStruct(shape, dtype) for...  22.4 us
    ppermute x12, starting transfers between devices, shift_z(): lax.ppermute(a, 'col', [(i, i // NZ * NZ + (i % NZ + d) % NZ) for i in ra...  18.9 us
    ppermute x12, waiting for transfers between devices, shift_z(): lax.ppermute(a, 'col', [(i, i // NZ * NZ + (i % NZ + d) % NZ) for i in ra...  12.3 us
    ppermute x6, starting transfers between devices, shift_y(): lax.ppermute(a, 'row', [(i, (i // 2 + d) % NY * 2 + i % 2) for i in range...  10.2 us
    ppermute x6, waiting for transfers between devices, shift_y(): lax.ppermute(a, 'row', [(i, (i // 2 + d) % NY * 2 + i % 2) for i in range...  7.21 us
    ppermute x6, starting transfers between devices, shift_x(): lax.ppermute(a, 'col', [(i, (i // NZ + d) % NX * NZ + i % NZ) for i in ra...  6.73 us
    pallas_call x1, Pallas kernels, prepare(): pl.pallas_call(prepare_kernel, out_shape=[jax.ShapeDtypeStruct(adjacency....  5.83 us
    ppermute x5, starting transfers between devices, swap_core(): return lax.ppermute(a, 'row', [(i, i ^ 1) for i in range(NY * 2)])  4.05 us
  transfers between devices with their start and end apart: 29, of which 13 were waited for; matrix products, arithmetic and copies ran while one was open for 0% of the time, Pallas kernels for 21%

profile of v3, /device:TPU:1, one launch (start us, length us, event | category | flops | bytes accessed | tf_op | source)
XLA Modules:
  0.0 95.8 jit_solution(5405788636258975445)
XLA Ops:
  0.6 2.2 %collective-permute-start = (bf16[512,128]{1,0:T(8,128)(2,1)}, bf16[512,128]{1,0:T(8,128)(2,1)S(1)}, u32[]{:S(2)}, u32[]{:S(2)}) collective-permute-start(bf16[512,128]{1,0:T(8,128)(2,1)} %refs_0_.1), channel_id=1, source_target_pairs={{0,32},{16,48},{32,64},{48,80},{64,96},{80,112},{96,0},{112,16},{1... | collective-permute-start | bytes 393224 | tf_op jit(solution)/shard_map/ppermute | solution.py:396
  2.8 2.6 %collective-permute-start.1 = (bf16[512,128]{1,0:T(8,128)(2,1)}, bf16[512,128]{1,0:T(8,128)(2,1)S(1)}, u32[]{:S(2)}, u32[]{:S(2)}) collective-permute-start(bf16[512,128]{1,0:T(8,128)(2,1)} %refs_0_.1), channel_id=1, source_target_pairs={{0,64},{16,80},{32,96},{48,112},{64,0},{80,16},{96,32},{112,48},{1... | collective-permute-start | bytes 393224 | tf_op jit(solution)/shard_map/ppermute | solution.py:396
  5.4 1.1 %collective-permute-start.2 = (bf16[512,128]{1,0:T(8,128)(2,1)}, bf16[512,128]{1,0:T(8,128)(2,1)S(1)}, u32[]{:S(2)}, u32[]{:S(2)}) collective-permute-start(bf16[512,128]{1,0:T(8,128)(2,1)} %refs_0_.1), channel_id=1, source_target_pairs={{0,96},{16,112},{32,0},{48,16},{64,32},{80,48},{96,64},{112,80},{1... | collective-permute-start | bytes 393224 | tf_op jit(solution)/shard_map/ppermute | solution.py:396
  6.5 1.5 %collective-permute-start.3 = (bf16[512,128]{1,0:T(8,128)(2,1)}, bf16[512,128]{1,0:T(8,128)(2,1)S(1)}, u32[]{:S(2)}, u32[]{:S(2)}) collective-permute-start(bf16[512,128]{1,0:T(8,128)(2,1)} %refs_0_.1), channel_id=1, source_target_pairs={{0,16},{16,0},{32,48},{48,32},{64,80},{80,64},{96,112},{112,96},{1... | collective-permute-start | bytes 393224 | tf_op jit(solution)/shard_map/ppermute | solution.py:400
  8.7 0.7 copy-done.3
  9.4 0.7 copy-done.4
  10.1 5.8 %prepare.1 = (bf16[512,128,128]{2,1,0:T(8,128)(2,1)S(1)}, s32[8,640]{1,0:T(8,128)S(1)}) custom-call(s32[1,1]{1,0:T(1,128)S(6)} %copy.10.count_ref, s32[1,512]{1,0:T(1,128)S(1)} %bitcast.3, s32[1,512]{1,0:T(1,128)S(1)} %bitcast.4, bf16[512,128,128]{2,1,0:T(8,128)(2,1)} %bitcast.5), custom_call_target="tpu_custom_call" | custom-call | bytes 33554432 | tf_op jit(solution)/shard_map/prepare/pallas_call | solution.py:111
  15.9 0.0 collective-permute-done.1.refs_2_
  15.9 0.0 collective-permute-done.2.refs_3_
  15.9 0.1 collective-permute-start.4
  16.0 0.5 collective-permute-start.5
  16.5 0.1 collective-permute-start.6
  16.6 0.7 collective-permute-done.4.refs_5_
  17.4 0.2 collective-permute-done.5.refs_6_
  17.5 0.3 collective-permute-done.6.refs_7_
  17.9 4.6 %forward_odd.1 = (bf16[32,128,128]{2,1,0:T(8,128)(2,1)S(1)}, bf16[2048,128]{1,0:T(8,128)(2,1)S(1)}, bf16[2048,128]{1,0:T(8,128)(2,1)S(1)}) custom-call(s32[8,640]{1,0:T(8,128)S(1)} %get-tuple-element.38.codes_ref, bf16[512,128,128]{2,1,0:T(8,128)(2,1)S(1)} %get-tuple-element.39.adj_ref, bf16[512,128]{1,0:T(8,128)(2,1)S(1)} %copy-done, ...), custom_call_target="tpu_custom_call" | custom-call | flops 4294967296 | bytes 10485760 | tf_op jit(solution)/shard_map/forward_odd/pallas_call | solution.py:144
  22.5 0.1 collective-permute-start.7
  22.6 2.7 %collective-permute-start.8 = (bf16[2048,128]{1,0:T(8,128)(2,1)S(1)}, bf16[2048,128]{1,0:T(8,128)(2,1)S(1)}, u32[]{:S(2)}, u32[]{:S(2)}) collective-permute-start(bf16[2048,128]{1,0:T(8,128)(2,1)S(1)} %get-tuple-element.46), channel_id=1, source_target_pairs={{0,12},{1,13},{2,14},{3,15},{4,0},{5,1},{6,2},{7,3},{8,4},{9,5},{1... | collective-permute-start | bytes 1572872 | tf_op jit(solution)/shard_map/ppermute | solution.py:388
  25.2 2.5 %forward_two.1 = (f32[512,128]{1,0:T(8,128)S(1)}, bf16[512,128]{1,0:T(8,128)(2,1)S(1)}, bf16[512,128]{1,0:T(8,128)(2,1)S(1)}, bf16[512,128]{1,0:T(8,128)(2,1)S(1)}) custom-call(s32[8,640]{1,0:T(8,128)S(1)} %get-tuple-element.38.codes_ref, bf16[512,128,128]{2,1,0:T(8,128)(2,1)S(1)} %get-tuple-element.39.adj_ref, bf16[32,128,128]{2,1,0:T(8,128)(2,1)S(1)} %get-tuple-element.43.feats), custom_call_target="tpu_custom_call" | custom-call | flops 2147483648 | bytes 5242880 | tf_op jit(solution)/shard_map/forward_two/pallas_call | solution.py:144
  27.7 2.7 %collective-permute-start.12 = (bf16[512,128]{1,0:T(8,128)(2,1)S(1)}, bf16[512,128]{1,0:T(8,128)(2,1)S(1)}, u32[]{:S(2)}, u32[]{:S(2)}) collective-permute-start(bf16[512,128]{1,0:T(8,128)(2,1)S(1)} %get-tuple-element.53), channel_id=1, source_target_pairs={{0,1},{1,2},{2,3},{3,0},{4,5},{5,6},{6,7},{7,4},{8,9},{9,10},{10,1... | collective-permute-start | bytes 393224 | tf_op jit(solution)/shard_map/ppermute | solution.py:392
  30.4 1.4 %collective-permute-start.13 = (bf16[512,128]{1,0:T(8,128)(2,1)S(1)}, bf16[512,128]{1,0:T(8,128)(2,1)S(1)}, u32[]{:S(2)}, u32[]{:S(2)}) collective-permute-start(bf16[512,128]{1,0:T(8,128)(2,1)S(1)} %get-tuple-element.54), channel_id=1, source_target_pairs={{0,2},{1,3},{2,0},{3,1},{4,6},{5,7},{6,4},{7,5},{8,10},{9,11},{10,... | collective-permute-start | bytes 393224 | tf_op jit(solution)/shard_map/ppermute | solution.py:392
  31.9 1.6 %collective-permute-start.14 = (bf16[512,128]{1,0:T(8,128)(2,1)S(1)}, bf16[512,128]{1,0:T(8,128)(2,1)S(1)}, u32[]{:S(2)}, u32[]{:S(2)}) collective-permute-start(bf16[512,128]{1,0:T(8,128)(2,1)S(1)} %get-tuple-element.55), channel_id=1, source_target_pairs={{0,3},{1,0},{2,1},{3,2},{4,7},{5,4},{6,5},{7,6},{8,11},{9,8},{10,9... | collective-permute-start | bytes 393224 | tf_op jit(solution)/shard_map/ppermute | solution.py:392
  33.5 3.0 %forward_zero.1.refs_0_ = f32[2048,128]{1,0:T(8,128)S(1)} custom-call(s32[8,640]{1,0:T(8,128)S(1)} %get-tuple-element.38.codes_ref, bf16[512,128,128]{2,1,0:T(8,128)(2,1)S(1)} %get-tuple-element.39.adj_ref, bf16[32,128,128]{2,1,0:T(8,128)(2,1)S(1)} %get-tuple-element.43.feats), custom_call_target="tpu_custom_call" | custom-call | flops 2147483648 | bytes 5242880 | tf_op jit(solution)/shard_map/forward_zero/pallas_call | solution.py:144
  36.5 0.0 copy-start.1
  36.5 0.0 copy-start.2
  36.5 1.1 %collective-permute-done.7.refs_1_ = bf16[2048,128]{1,0:T(8,128)(2,1)S(1)} collective-permute-done((bf16[2048,128]{1,0:T(8,128)(2,1)S(1)}, bf16[2048,128]{1,0:T(8,128)(2,1)S(1)}, u32[]{:S(2)}, u32[]{:S(2)}) %collective-permute-start.7) | collective-permute-done | bytes 524320 | tf_op jit(solution)/shard_map/ppermute | solution.py:388
  37.5 0.2 add_x.1
  37.7 1.5 %collective-permute-start.9 = (bf16[512,128]{1,0:T(8,128)(2,1)S(1)}, bf16[512,128]{1,0:T(8,128)(2,1)S(1)}, u32[]{:S(2)}, u32[]{:S(2)}) collective-permute-start(bf16[512,128]{1,0:T(8,128)(2,1)S(1)} %get-tuple-element.49), channel_id=1, source_target_pairs={{0,1},{1,2},{2,3},{3,0},{4,5},{5,6},{6,7},{7,4},{8,9},{9,10},{10,1... | collective-permute-start | bytes 393224 | tf_op jit(solution)/shard_map/ppermute | solution.py:392
  39.2 3.6 %collective-permute-start.10 = (bf16[512,128]{1,0:T(8,128)(2,1)S(1)}, bf16[512,128]{1,0:T(8,128)(2,1)S(1)}, u32[]{:S(2)}, u32[]{:S(2)}) collective-permute-start(bf16[512,128]{1,0:T(8,128)(2,1)S(1)} %get-tuple-element.50), channel_id=1, source_target_pairs={{0,2},{1,3},{2,0},{3,1},{4,6},{5,7},{6,4},{7,5},{8,10},{9,11},{10,... | collective-permute-start | bytes 393224 | tf_op jit(solution)/shard_map/ppermute | solution.py:392
  42.9 0.6 collective-permute-start.11
  43.5 0.1 add_z.1
  43.5 0.9 collective-permute-start.15
  44.5 0.7 collective-permute-done.9.refs_1_
  45.2 3.7 %collective-permute-done.10.refs_2_ = bf16[512,128]{1,0:T(8,128)(2,1)S(1)} collective-permute-done((bf16[512,128]{1,0:T(8,128)(2,1)S(1)}, bf16[512,128]{1,0:T(8,128)(2,1)S(1)}, u32[]{:S(2)}, u32[]{:S(2)}) %collective-permute-start.10) | collective-permute-done | bytes 131104 | tf_op jit(solution)/shard_map/ppermute | solution.py:392
  48.8 0.0 collective-permute-done.11.refs_3_
  48.8 0.4 collective-permute-done.15.refs_4_
  49.2 1.1 %activate.1 = (bf16[512,128]{1,0:T(8,128)(2,1)}, bf16[640,128]{1,0:T(8,128)(2,1)S(1)}) custom-call(bf16[128,128]{1,0:T(8,128)(2,1)S(1)} %copy-done.2, bf16[512,128]{1,0:T(8,128)(2,1)S(1)} %copy-done.1, f32[512,128]{1,0:T(8,128)S(1)} %get-tuple-element.48.refs_0_, bf16[512,128]{1,0:T(8,128)(2,1)S(1)} %collective-permute-done.9.refs_1_, ...), custom_call_target="tpu_custom_call" | custom-call | tf_op jit(solution)/shard_map/activate/pallas_call | solution.py:300
  50.3 1.1 %collective-permute-start.16 = (bf16[640,128]{1,0:T(8,128)(2,1)S(1)}, bf16[640,128]{1,0:T(8,128)(2,1)S(1)}, u32[]{:S(2)}, u32[]{:S(2)}) collective-permute-start(bf16[640,128]{1,0:T(8,128)(2,1)S(1)} %get-tuple-element.57.refs_0_), channel_id=1, source_target_pairs={{0,1},{1,2},{2,3},{3,0},{4,5},{5,6},{6,7},{7,4},{8,9},{9,10},{10,1... | collective-permute-start | bytes 491528 | tf_op jit(solution)/shard_map/ppermute | solution.py:392
  51.5 1.9 %collective-permute-start.17 = (bf16[640,128]{1,0:T(8,128)(2,1)S(1)}, bf16[640,128]{1,0:T(8,128)(2,1)S(1)}, u32[]{:S(2)}, u32[]{:S(2)}) collective-permute-start(bf16[640,128]{1,0:T(8,128)(2,1)S(1)} %get-tuple-element.57.refs_0_), channel_id=1, source_target_pairs={{0,2},{1,3},{2,0},{3,1},{4,6},{5,7},{6,4},{7,5},{8,10},{9,11},{10,... | collective-permute-start | bytes 491528 | tf_op jit(solution)/shard_map/ppermute | solution.py:392
  53.3 0.5 collective-permute-start.18
  53.9 0.3 collective-permute-start.19
  54.2 1.6 %collective-permute-done.16.refs_1_ = bf16[640,128]{1,0:T(8,128)(2,1)S(1)} collective-permute-done((bf16[640,128]{1,0:T(8,128)(2,1)S(1)}, bf16[640,128]{1,0:T(8,128)(2,1)S(1)}, u32[]{:S(2)}, u32[]{:S(2)}) %collective-permute-start.16) | collective-permute-done | bytes 163872 | tf_op jit(solution)/shard_map/ppermute | solution.py:392
  55.7 4.4 %collective-permute-done.17.refs_2_ = bf16[640,128]{1,0:T(8,128)(2,1)S(1)} collective-permute-done((bf16[640,128]{1,0:T(8,128)(2,1)S(1)}, bf16[640,128]{1,0:T(8,128)(2,1)S(1)}, u32[]{:S(2)}, u32[]{:S(2)}) %collective-permute-start.17) | collective-permute-done | bytes 163872 | tf_op jit(solution)/shard_map/ppermute | solution.py:392
  60.1 0.0 collective-permute-done.18.refs_3_
  60.1 0.1 merge_z.1.column
  60.2 2.1 %collective-permute-start.23 = (bf16[2176,128]{1,0:T(8,128)(2,1)S(1)}, bf16[2176,128]{1,0:T(8,128)(2,1)S(1)}, u32[]{:S(2)}, u32[]{:S(2)}) collective-permute-start(bf16[2176,128]{1,0:T(8,128)(2,1)S(1)} %merge_z.1.column), channel_id=1, source_target_pairs={{0,4},{1,5},{2,6},{3,7},{4,8},{5,9},{6,10},{7,11},{8,12},{9,13},{1... | collective-permute-start | bytes 1671176 | tf_op jit(solution)/shard_map/ppermute | solution.py:388
  62.3 0.6 collective-permute-start.24
  62.9 0.0 collective-permute-done.19.refs_0_
  62.9 1.1 %collective-permute-start.20 = (bf16[640,128]{1,0:T(8,128)(2,1)S(1)}, bf16[640,128]{1,0:T(8,128)(2,1)S(1)}, u32[]{:S(2)}, u32[]{:S(2)}) collective-permute-start(bf16[640,128]{1,0:T(8,128)(2,1)S(1)} %collective-permute-done.19.refs_0_), channel_id=1, source_target_pairs={{0,1},{1,2},{2,3},{3,0},{4,5},{5,6},{6,7},{7,4},{8,9},{9,10},{10,1... | collective-permute-start | bytes 491528 | tf_op jit(solution)/shard_map/ppermute | solution.py:392
  64.0 2.8 %collective-permute-start.21 = (bf16[640,128]{1,0:T(8,128)(2,1)S(1)}, bf16[640,128]{1,0:T(8,128)(2,1)S(1)}, u32[]{:S(2)}, u32[]{:S(2)}) collective-permute-start(bf16[640,128]{1,0:T(8,128)(2,1)S(1)} %collective-permute-done.19.refs_0_), channel_id=1, source_target_pairs={{0,2},{1,3},{2,0},{3,1},{4,6},{5,7},{6,4},{7,5},{8,10},{9,11},{10,... | collective-permute-start | bytes 491528 | tf_op jit(solution)/shard_map/ppermute | solution.py:392
  66.8 3.0 %backward_zero.1.before = f32[33,128,128]{2,1,0:T(8,128)S(1)} custom-call(s32[8,640]{1,0:T(8,128)S(1)} %get-tuple-element.38.codes_ref, bf16[512,128,128]{2,1,0:T(8,128)(2,1)S(1)} %get-tuple-element.39.adj_ref, bf16[2176,128]{1,0:T(8,128)(2,1)S(1)} %merge_z.1.column), custom_call_target="tpu_custom_call" | custom-call | flops 2147483648 | bytes 5242880 | tf_op jit(solution)/shard_map/backward_zero/pallas_call | solution.py:144
  69.9 0.0 collective-permute-done.20.refs_1_
  69.9 2.0 %collective-permute-done.21.refs_2_ = bf16[640,128]{1,0:T(8,128)(2,1)S(1)} collective-permute-done((bf16[640,128]{1,0:T(8,128)(2,1)S(1)}, bf16[640,128]{1,0:T(8,128)(2,1)S(1)}, u32[]{:S(2)}, u32[]{:S(2)}) %collective-permute-start.21) | collective-permute-done | bytes 163872 | tf_op jit(solution)/shard_map/ppermute | solution.py:392
  71.9 2.6 %backward_two.1 = (f32[33,128,128]{2,1,0:T(8,128)S(1)}, f32[128,128]{1,0:T(8,128)S(1)}) custom-call(s32[8,640]{1,0:T(8,128)S(1)} %get-tuple-element.38.codes_ref, bf16[512,128,128]{2,1,0:T(8,128)(2,1)S(1)} %get-tuple-element.39.adj_ref, f32[33,128,128]{2,1,0:T(8,128)S(1)} %backward_zero.1.before, bf16[2176,128]{1,0:T(8,128)(2,1)S(1)} %merge_z.1.column, ...), custom_call_target="tpu_custom_call" | custom-call | flops 2147483648 | bytes 5242880 | tf_op jit(solution)/shard_map/backward_two/pallas_call | solution.py:144
  74.4 0.3 collective-permute-done.24.second
  74.8 3.3 %backward_other.1 = (f32[2176,128]{1,0:T(8,128)S(1)}, f32[128,128]{1,0:T(8,128)S(1)}) custom-call(s32[8,640]{1,0:T(8,128)S(1)} %get-tuple-element.38.codes_ref, bf16[512,128,128]{2,1,0:T(8,128)(2,1)S(1)} %get-tuple-element.39.adj_ref, f32[33,128,128]{2,1,0:T(8,128)S(1)} %get-tuple-element.58.before, f32[128,128]{1,0:T(8,128)S(1)} %get-tuple-element.59.wpart, ...), custom_call_target="tpu_custom_call" | custom-call | flops 2147483648 | bytes 5242880 | tf_op jit(solution)/shard_map/backward_other/pallas_call | solution.py:144
  78.1 1.9 %collective-permute-start.25 = (f32[2176,128]{1,0:T(8,128)S(1)}, f32[2176,128]{1,0:T(8,128)S(1)}, u32[]{:S(2)}, u32[]{:S(2)}) collective-permute-start(f32[2176,128]{1,0:T(8,128)S(1)} %get-tuple-element.61), channel_id=1, source_target_pairs={{0,16},{16,0},{32,48},{48,32},{64,80},{80,64},{96,112},{112,96},{1... | collective-permute-start | bytes 3342344 | tf_op jit(solution)/shard_map/ppermute | solution.py:400
  80.0 3.3 %backward_own.1.keep = f32[2048,128]{1,0:T(8,128)S(1)} custom-call(s32[8,640]{1,0:T(8,128)S(1)} %get-tuple-element.38.codes_ref, bf16[512,128,128]{2,1,0:T(8,128)(2,1)S(1)} %get-tuple-element.39.adj_ref, f32[33,128,128]{2,1,0:T(8,128)S(1)} %get-tuple-element.58.before, bf16[2176,128]{1,0:T(8,128)(2,1)S(1)} %collective-permute-done.23.first, ...), custom_call_target="tpu_custom_call" | custom-call | flops 2147483648 | bytes 5242880 | tf_op jit(solution)/shard_map/backward_own/pallas_call | solution.py:144
  83.4 0.1 add_core.1
  83.5 1.8 %collective-permute-start.26 = (bf16[640,128]{1,0:T(8,128)(2,1)S(1)}, bf16[640,128]{1,0:T(8,128)(2,1)S(1)}, u32[]{:S(2)}, u32[]{:S(2)}) collective-permute-start(bf16[640,128]{1,0:T(8,128)(2,1)S(1)} %get-tuple-element.64), channel_id=1, source_target_pairs={{0,32},{16,48},{32,64},{48,80},{64,96},{80,112},{96,0},{112,16},{1... | collective-permute-start | bytes 491528 | tf_op jit(solution)/shard_map/ppermute | solution.py:396
  85.3 2.5 %collective-permute-start.28 = (bf16[640,128]{1,0:T(8,128)(2,1)S(1)}, bf16[640,128]{1,0:T(8,128)(2,1)S(1)}, u32[]{:S(2)}, u32[]{:S(2)}) collective-permute-start(bf16[640,128]{1,0:T(8,128)(2,1)S(1)} %get-tuple-element.66), channel_id=1, source_target_pairs={{0,96},{16,112},{32,0},{48,16},{64,32},{80,48},{96,64},{112,80},{1... | collective-permute-start | bytes 491528 | tf_op jit(solution)/shard_map/ppermute | solution.py:396
  87.8 6.4 %collective-permute-done.26.refs_0_ = bf16[640,128]{1,0:T(8,128)(2,1)S(1)} collective-permute-done((bf16[640,128]{1,0:T(8,128)(2,1)S(1)}, bf16[640,128]{1,0:T(8,128)(2,1)S(1)}, u32[]{:S(2)}, u32[]{:S(2)}) %collective-permute-start.26) | collective-permute-done | bytes 163872 | tf_op jit(solution)/shard_map/ppermute | solution.py:396
  94.2 0.8 collective-permute-done.28.refs_2_
  95.0 0.9 finish.1
  (18 shorter events, 0.0 us)
Async XLA Ops:
  0.6 15.3 %collective-permute-start = (bf16[512,128]{1,0:T(8,128)(2,1)}, bf16[512,128]{1,0:T(8,128)(2,1)S(1)}, u32[]{:S(2)}, u32[]{:S(2)}) collective-permute-start(bf16[512,128]{1,0:T(8,128)(2,1)} %refs_0_.1), channel_id=1, source_target_pairs={{0,32},{16,48},{32,64},{48,80},{64,96},{80,112},{96,0},{112,16},{1... | collective-permute-start | bytes 393224 | tf_op jit(solution)/shard_map/ppermute | solution.py:396
  2.8 13.1 %collective-permute-start.1 = (bf16[512,128]{1,0:T(8,128)(2,1)}, bf16[512,128]{1,0:T(8,128)(2,1)S(1)}, u32[]{:S(2)}, u32[]{:S(2)}) collective-permute-start(bf16[512,128]{1,0:T(8,128)(2,1)} %refs_0_.1), channel_id=1, source_target_pairs={{0,64},{16,80},{32,96},{48,112},{64,0},{80,16},{96,32},{112,48},{1... | collective-permute-start | bytes 393224 | tf_op jit(solution)/shard_map/ppermute | solution.py:396
  5.4 10.5 %collective-permute-start.2 = (bf16[512,128]{1,0:T(8,128)(2,1)}, bf16[512,128]{1,0:T(8,128)(2,1)S(1)}, u32[]{:S(2)}, u32[]{:S(2)}) collective-permute-start(bf16[512,128]{1,0:T(8,128)(2,1)} %refs_0_.1), channel_id=1, source_target_pairs={{0,96},{16,112},{32,0},{48,16},{64,32},{80,48},{96,64},{112,80},{1... | collective-permute-start | bytes 393224 | tf_op jit(solution)/shard_map/ppermute | solution.py:396
  6.5 10.1 %collective-permute-start.3 = (bf16[512,128]{1,0:T(8,128)(2,1)}, bf16[512,128]{1,0:T(8,128)(2,1)S(1)}, u32[]{:S(2)}, u32[]{:S(2)}) collective-permute-start(bf16[512,128]{1,0:T(8,128)(2,1)} %refs_0_.1), channel_id=1, source_target_pairs={{0,16},{16,0},{32,48},{48,32},{64,80},{80,64},{96,112},{112,96},{1... | collective-permute-start | bytes 393224 | tf_op jit(solution)/shard_map/ppermute | solution.py:400
  8.7 0.7 copy-start.3
  9.4 0.7 copy-start.4
  10.0 7.8 %copy-start = (bf16[512,128]{1,0:T(8,128)(2,1)S(1)}, bf16[512,128]{1,0:T(8,128)(2,1)}, u32[]{:S(2)}) copy-start(bf16[512,128]{1,0:T(8,128)(2,1)} %refs_0_.1) | copy-start | bytes 393220
  15.9 1.4 %collective-permute-start.4 = (bf16[512,128]{1,0:T(8,128)(2,1)S(1)}, bf16[512,128]{1,0:T(8,128)(2,1)S(1)}, u32[]{:S(2)}, u32[]{:S(2)}) collective-permute-start(bf16[512,128]{1,0:T(8,128)(2,1)S(1)} %collective-permute-done.refs_1_), channel_id=1, source_target_pairs={{0,16},{16,0},{32,48},{48,32},{64,80},{80,64},{96,112},{112,96},{1... | collective-permute-start | bytes 393224 | tf_op jit(solution)/shard_map/ppermute | solution.py:400
  16.0 1.5 %collective-permute-start.5 = (bf16[512,128]{1,0:T(8,128)(2,1)S(1)}, bf16[512,128]{1,0:T(8,128)(2,1)S(1)}, u32[]{:S(2)}, u32[]{:S(2)}) collective-permute-start(bf16[512,128]{1,0:T(8,128)(2,1)S(1)} %collective-permute-done.1.refs_2_), channel_id=1, source_target_pairs={{0,16},{16,0},{32,48},{48,32},{64,80},{80,64},{96,112},{112,96},{1... | collective-permute-start | bytes 393224 | tf_op jit(solution)/shard_map/ppermute | solution.py:400
  16.5 1.3 %collective-permute-start.6 = (bf16[512,128]{1,0:T(8,128)(2,1)S(1)}, bf16[512,128]{1,0:T(8,128)(2,1)S(1)}, u32[]{:S(2)}, u32[]{:S(2)}) collective-permute-start(bf16[512,128]{1,0:T(8,128)(2,1)S(1)} %collective-permute-done.2.refs_3_), channel_id=1, source_target_pairs={{0,16},{16,0},{32,48},{48,32},{64,80},{80,64},{96,112},{112,96},{1... | collective-permute-start | bytes 393224 | tf_op jit(solution)/shard_map/ppermute | solution.py:400
  22.5 15.0 %collective-permute-start.7 = (bf16[2048,128]{1,0:T(8,128)(2,1)S(1)}, bf16[2048,128]{1,0:T(8,128)(2,1)S(1)}, u32[]{:S(2)}, u32[]{:S(2)}) collective-permute-start(bf16[2048,128]{1,0:T(8,128)(2,1)S(1)} %get-tuple-element.45), channel_id=1, source_target_pairs={{0,4},{1,5},{2,6},{3,7},{4,8},{5,9},{6,10},{7,11},{8,12},{9,13},{1... | collective-permute-start | bytes 1572872 | tf_op jit(solution)/shard_map/ppermute | solution.py:388
  22.6 15.0 %collective-permute-start.8 = (bf16[2048,128]{1,0:T(8,128)(2,1)S(1)}, bf16[2048,128]{1,0:T(8,128)(2,1)S(1)}, u32[]{:S(2)}, u32[]{:S(2)}) collective-permute-start(bf16[2048,128]{1,0:T(8,128)(2,1)S(1)} %get-tuple-element.46), channel_id=1, source_target_pairs={{0,12},{1,13},{2,14},{3,15},{4,0},{5,1},{6,2},{7,3},{8,4},{9,5},{1... | collective-permute-start | bytes 1572872 | tf_op jit(solution)/shard_map/ppermute | solution.py:388
  27.7 15.1 %collective-permute-start.12 = (bf16[512,128]{1,0:T(8,128)(2,1)S(1)}, bf16[512,128]{1,0:T(8,128)(2,1)S(1)}, u32[]{:S(2)}, u32[]{:S(2)}) collective-permute-start(bf16[512,128]{1,0:T(8,128)(2,1)S(1)} %get-tuple-element.53), channel_id=1, source_target_pairs={{0,1},{1,2},{2,3},{3,0},{4,5},{5,6},{6,7},{7,4},{8,9},{9,10},{10,1... | collective-permute-start | bytes 393224 | tf_op jit(solution)/shard_map/ppermute | solution.py:392
  30.4 13.0 %collective-permute-start.13 = (bf16[512,128]{1,0:T(8,128)(2,1)S(1)}, bf16[512,128]{1,0:T(8,128)(2,1)S(1)}, u32[]{:S(2)}, u32[]{:S(2)}) collective-permute-start(bf16[512,128]{1,0:T(8,128)(2,1)S(1)} %get-tuple-element.54), channel_id=1, source_target_pairs={{0,2},{1,3},{2,0},{3,1},{4,6},{5,7},{6,4},{7,5},{8,10},{9,11},{10,... | collective-permute-start | bytes 393224 | tf_op jit(solution)/shard_map/ppermute | solution.py:392
  31.9 11.6 %collective-permute-start.14 = (bf16[512,128]{1,0:T(8,128)(2,1)S(1)}, bf16[512,128]{1,0:T(8,128)(2,1)S(1)}, u32[]{:S(2)}, u32[]{:S(2)}) collective-permute-start(bf16[512,128]{1,0:T(8,128)(2,1)S(1)} %get-tuple-element.55), channel_id=1, source_target_pairs={{0,3},{1,0},{2,1},{3,2},{4,7},{5,4},{6,5},{7,6},{8,11},{9,8},{10,9... | collective-permute-start | bytes 393224 | tf_op jit(solution)/shard_map/ppermute | solution.py:392
  36.5 12.8 %copy-start.1 = (bf16[512,128]{1,0:T(8,128)(2,1)S(1)}, bf16[512,128]{1,0:T(8,128)(2,1)}, u32[]{:S(2)}) copy-start(bf16[512,128]{1,0:T(8,128)(2,1)} %grad_ref.1) | copy-start | bytes 393220
  36.5 12.8 %copy-start.2 = (bf16[128,128]{1,0:T(8,128)(2,1)S(1)}, bf16[128,128]{1,0:T(8,128)(2,1)}, u32[]{:S(2)}) copy-start(bf16[128,128]{1,0:T(8,128)(2,1)} %weight_ref.3) | copy-start | bytes 98308
  37.7 7.4 %collective-permute-start.9 = (bf16[512,128]{1,0:T(8,128)(2,1)S(1)}, bf16[512,128]{1,0:T(8,128)(2,1)S(1)}, u32[]{:S(2)}, u32[]{:S(2)}) collective-permute-start(bf16[512,128]{1,0:T(8,128)(2,1)S(1)} %get-tuple-element.49), channel_id=1, source_target_pairs={{0,1},{1,2},{2,3},{3,0},{4,5},{5,6},{6,7},{7,4},{8,9},{9,10},{10,1... | collective-permute-start | bytes 393224 | tf_op jit(solution)/shard_map/ppermute | solution.py:392
  39.2 9.6 %collective-permute-start.10 = (bf16[512,128]{1,0:T(8,128)(2,1)S(1)}, bf16[512,128]{1,0:T(8,128)(2,1)S(1)}, u32[]{:S(2)}, u32[]{:S(2)}) collective-permute-start(bf16[512,128]{1,0:T(8,128)(2,1)S(1)} %get-tuple-element.50), channel_id=1, source_target_pairs={{0,2},{1,3},{2,0},{3,1},{4,6},{5,7},{6,4},{7,5},{8,10},{9,11},{10,... | collective-permute-start | bytes 393224 | tf_op jit(solution)/shard_map/ppermute | solution.py:392
  42.9 6.0 %collective-permute-start.11 = (bf16[512,128]{1,0:T(8,128)(2,1)S(1)}, bf16[512,128]{1,0:T(8,128)(2,1)S(1)}, u32[]{:S(2)}, u32[]{:S(2)}) collective-permute-start(bf16[512,128]{1,0:T(8,128)(2,1)S(1)} %get-tuple-element.51), channel_id=1, source_target_pairs={{0,3},{1,0},{2,1},{3,2},{4,7},{5,4},{6,5},{7,6},{8,11},{9,8},{10,9... | collective-permute-start | bytes 393224 | tf_op jit(solution)/shard_map/ppermute | solution.py:392
  43.5 5.7 %collective-permute-start.15 = (bf16[512,128]{1,0:T(8,128)(2,1)S(1)}, bf16[512,128]{1,0:T(8,128)(2,1)S(1)}, u32[]{:S(2)}, u32[]{:S(2)}) collective-permute-start(bf16[512,128]{1,0:T(8,128)(2,1)S(1)} %add_z.1), channel_id=1, source_target_pairs={{0,8},{1,9},{2,10},{3,11},{4,12},{5,13},{6,14},{7,15},{8,0},{9,1},... | collective-permute-start | bytes 393224 | tf_op jit(solution)/shard_map/ppermute | solution.py:388
  50.3 5.4 %collective-permute-start.16 = (bf16[640,128]{1,0:T(8,128)(2,1)S(1)}, bf16[640,128]{1,0:T(8,128)(2,1)S(1)}, u32[]{:S(2)}, u32[]{:S(2)}) collective-permute-start(bf16[640,128]{1,0:T(8,128)(2,1)S(1)} %get-tuple-element.57.refs_0_), channel_id=1, source_target_pairs={{0,1},{1,2},{2,3},{3,0},{4,5},{5,6},{6,7},{7,4},{8,9},{9,10},{10,1... | collective-permute-start | bytes 491528 | tf_op jit(solution)/shard_map/ppermute | solution.py:392
  51.5 8.6 %collective-permute-start.17 = (bf16[640,128]{1,0:T(8,128)(2,1)S(1)}, bf16[640,128]{1,0:T(8,128)(2,1)S(1)}, u32[]{:S(2)}, u32[]{:S(2)}) collective-permute-start(bf16[640,128]{1,0:T(8,128)(2,1)S(1)} %get-tuple-element.57.refs_0_), channel_id=1, source_target_pairs={{0,2},{1,3},{2,0},{3,1},{4,6},{5,7},{6,4},{7,5},{8,10},{9,11},{10,... | collective-permute-start | bytes 491528 | tf_op jit(solution)/shard_map/ppermute | solution.py:392
  53.3 6.8 %collective-permute-start.18 = (bf16[640,128]{1,0:T(8,128)(2,1)S(1)}, bf16[640,128]{1,0:T(8,128)(2,1)S(1)}, u32[]{:S(2)}, u32[]{:S(2)}) collective-permute-start(bf16[640,128]{1,0:T(8,128)(2,1)S(1)} %get-tuple-element.57.refs_0_), channel_id=1, source_target_pairs={{0,3},{1,0},{2,1},{3,2},{4,7},{5,4},{6,5},{7,6},{8,11},{9,8},{10,9... | collective-permute-start | bytes 491528 | tf_op jit(solution)/shard_map/ppermute | solution.py:392
  53.9 9.1 %collective-permute-start.19 = (bf16[640,128]{1,0:T(8,128)(2,1)S(1)}, bf16[640,128]{1,0:T(8,128)(2,1)S(1)}, u32[]{:S(2)}, u32[]{:S(2)}) collective-permute-start(bf16[640,128]{1,0:T(8,128)(2,1)S(1)} %get-tuple-element.57.refs_0_), channel_id=1, source_target_pairs={{0,8},{1,9},{2,10},{3,11},{4,12},{5,13},{6,14},{7,15},{8,0},{9,1},... | collective-permute-start | bytes 491528 | tf_op jit(solution)/shard_map/ppermute | solution.py:388
  60.2 14.2 %collective-permute-start.23 = (bf16[2176,128]{1,0:T(8,128)(2,1)S(1)}, bf16[2176,128]{1,0:T(8,128)(2,1)S(1)}, u32[]{:S(2)}, u32[]{:S(2)}) collective-permute-start(bf16[2176,128]{1,0:T(8,128)(2,1)S(1)} %merge_z.1.column), channel_id=1, source_target_pairs={{0,4},{1,5},{2,6},{3,7},{4,8},{5,9},{6,10},{7,11},{8,12},{9,13},{1... | collective-permute-start | bytes 1671176 | tf_op jit(solution)/shard_map/ppermute | solution.py:388
  62.3 12.5 %collective-permute-start.24 = (bf16[2176,128]{1,0:T(8,128)(2,1)S(1)}, bf16[2176,128]{1,0:T(8,128)(2,1)S(1)}, u32[]{:S(2)}, u32[]{:S(2)}) collective-permute-start(bf16[2176,128]{1,0:T(8,128)(2,1)S(1)} %merge_z.1.column), channel_id=1, source_target_pairs={{0,12},{1,13},{2,14},{3,15},{4,0},{5,1},{6,2},{7,3},{8,4},{9,5},{1... | collective-permute-start | bytes 1671176 | tf_op jit(solution)/shard_map/ppermute | solution.py:388
  62.9 6.9 %collective-permute-start.20 = (bf16[640,128]{1,0:T(8,128)(2,1)S(1)}, bf16[640,128]{1,0:T(8,128)(2,1)S(1)}, u32[]{:S(2)}, u32[]{:S(2)}) collective-permute-start(bf16[640,128]{1,0:T(8,128)(2,1)S(1)} %collective-permute-done.19.refs_0_), channel_id=1, source_target_pairs={{0,1},{1,2},{2,3},{3,0},{4,5},{5,6},{6,7},{7,4},{8,9},{9,10},{10,1... | collective-permute-start | bytes 491528 | tf_op jit(solution)/shard_map/ppermute | solution.py:392
  64.0 7.8 %collective-permute-start.21 = (bf16[640,128]{1,0:T(8,128)(2,1)S(1)}, bf16[640,128]{1,0:T(8,128)(2,1)S(1)}, u32[]{:S(2)}, u32[]{:S(2)}) collective-permute-start(bf16[640,128]{1,0:T(8,128)(2,1)S(1)} %collective-permute-done.19.refs_0_), channel_id=1, source_target_pairs={{0,2},{1,3},{2,0},{3,1},{4,6},{5,7},{6,4},{7,5},{8,10},{9,11},{10,... | collective-permute-start | bytes 491528 | tf_op jit(solution)/shard_map/ppermute | solution.py:392
  66.8 5.1 %collective-permute-start.22 = (bf16[640,128]{1,0:T(8,128)(2,1)S(1)}, bf16[640,128]{1,0:T(8,128)(2,1)S(1)}, u32[]{:S(2)}, u32[]{:S(2)}) collective-permute-start(bf16[640,128]{1,0:T(8,128)(2,1)S(1)} %collective-permute-done.19.refs_0_), channel_id=1, source_target_pairs={{0,3},{1,0},{2,1},{3,2},{4,7},{5,4},{6,5},{7,6},{8,11},{9,8},{10,9... | collective-permute-start | bytes 491528 | tf_op jit(solution)/shard_map/ppermute | solution.py:392
  78.1 5.2 %collective-permute-start.25 = (f32[2176,128]{1,0:T(8,128)S(1)}, f32[2176,128]{1,0:T(8,128)S(1)}, u32[]{:S(2)}, u32[]{:S(2)}) collective-permute-start(f32[2176,128]{1,0:T(8,128)S(1)} %get-tuple-element.61), channel_id=1, source_target_pairs={{0,16},{16,0},{32,48},{48,32},{64,80},{80,64},{96,112},{112,96},{1... | collective-permute-start | bytes 3342344 | tf_op jit(solution)/shard_map/ppermute | solution.py:400
  83.5 10.7 %collective-permute-start.26 = (bf16[640,128]{1,0:T(8,128)(2,1)S(1)}, bf16[640,128]{1,0:T(8,128)(2,1)S(1)}, u32[]{:S(2)}, u32[]{:S(2)}) collective-permute-start(bf16[640,128]{1,0:T(8,128)(2,1)S(1)} %get-tuple-element.64), channel_id=1, source_target_pairs={{0,32},{16,48},{32,64},{48,80},{64,96},{80,112},{96,0},{112,16},{1... | collective-permute-start | bytes 491528 | tf_op jit(solution)/shard_map/ppermute | solution.py:396
  85.3 8.9 %collective-permute-start.27 = (bf16[640,128]{1,0:T(8,128)(2,1)S(1)}, bf16[640,128]{1,0:T(8,128)(2,1)S(1)}, u32[]{:S(2)}, u32[]{:S(2)}) collective-permute-start(bf16[640,128]{1,0:T(8,128)(2,1)S(1)} %get-tuple-element.65), channel_id=1, source_target_pairs={{0,64},{16,80},{32,96},{48,112},{64,0},{80,16},{96,32},{112,48},{1... | collective-permute-start | bytes 491528 | tf_op jit(solution)/shard_map/ppermute | solution.py:396
  85.3 9.7 %collective-permute-start.28 = (bf16[640,128]{1,0:T(8,128)(2,1)S(1)}, bf16[640,128]{1,0:T(8,128)(2,1)S(1)}, u32[]{:S(2)}, u32[]{:S(2)}) collective-permute-start(bf16[640,128]{1,0:T(8,128)(2,1)S(1)} %get-tuple-element.66), channel_id=1, source_target_pairs={{0,96},{16,112},{32,0},{48,16},{64,32},{80,48},{96,64},{112,80},{1... | collective-permute-start | bytes 491528 | tf_op jit(solution)/shard_map/ppermute | solution.py:396
